TPU v7x, 512 devices: a whole 4x4x16 slice. The times are simulated.
512 devices in a mesh: dp: 16 (over z), latent: 8 (over y, core), section: 4 (over x).
Axes of the slice: x: 4, y: 4, z: 16, core: 2. Of those that a mesh axis runs over, the one named last changes fastest.
Arguments:
- activations: bfloat16 [16384, 4608], P(('latent', 'section'), 'dp'), may hold values from -6 to 6
- bias_dec: bfloat16 [4608], P('dp'), may hold values from -4 to 4
- encoder: bfloat16 [4608, 65536], P('dp', ('latent', 'section')), may hold values from -0.09375 to 0.09375
- decoder: bfloat16 [65536, 4608], P(('latent', 'section'), 'dp'), may hold values from -0.375 to 0.375
- active_blocks: int32 [16384, 4], P(('latent', 'section')), may hold values from 0 to 1023, all different within a row; in each aligned block of 512 rows (0 to 511, 512 to 1023, ...) at most 4 rows name the same one
Outputs:
- grad_decoder: bfloat16 [65536, 4608], P(('latent', 'section'), 'dp')
- row_loss: float32 [16384], P(('latent', 'section'))
Inputs may be any that keep to these rules, and one draw needn't show every extreme that they name: `active_blocks`: each row names 4 different blocks; among the 512 rows of one device no block is named by more than 4 rows, and some block is named by exactly 4 of them.
All inputs are finite; a program needn't handle non-finite values.
Results may differ from a plain program's by a relative error of at most 0.0034.
Values may be sent and summed in bfloat16 or wider, within the bound.
No kernel may reach another device: no remote copies, remote signals or barrier semaphores. Data moves between devices by JAX's collectives and lax.ppermute only.
A program may use at most 64 MiB of HBM per device.

v0:
```python
import jax
import jax.numpy as jnp
from jax import lax
from jax.sharding import PartitionSpec as P

BLOCK = 64


def route_slots(buffer):
    return lax.all_to_all(buffer, ("latent", "section"), split_axis=0, concat_axis=0, tiled=True)


def on_device(activations, bias_dec, encoder, decoder, active_blocks):
    row_count, shard_width = activations.shape
    per_row = active_blocks.shape[1]
    groups = lax.axis_size(("latent", "section"))
    local_blocks = encoder.shape[1] // BLOCK
    total_blocks = local_blocks * groups
    capacity = max(2, 2 * row_count * per_row // total_blocks)
    slot_count = total_blocks * capacity
    pair_blocks = active_blocks.reshape(-1)
    pair_iota = jnp.arange(pair_blocks.shape[0], dtype=jnp.int32)
    same_block = pair_blocks[:, None] == pair_blocks[None, :]
    earlier = pair_iota[None, :] < pair_iota[:, None]
    block_rank = jnp.sum((same_block & earlier).astype(jnp.int32), axis=1)
    slot_index = (pair_blocks * capacity + block_rank).reshape(row_count, per_row)
    slot_iota = jnp.arange(slot_count, dtype=jnp.int32)
    placement = jnp.zeros((slot_count, row_count), jnp.bfloat16)
    for which in range(per_row):
        placement = placement + (slot_index[:, which][None, :] == slot_iota[:, None]).astype(
            jnp.bfloat16
        )
    slot_shape = (groups, local_blocks, capacity, shard_width)

    def scatter_rows(values):
        filled = jnp.dot(placement, values, preferred_element_type=jnp.float32).astype(values.dtype)
        return filled.reshape(slot_shape)

    bias_wide = bias_dec.astype(jnp.float32)[None, :]
    shifted = (activations.astype(jnp.float32) - bias_wide).astype(jnp.bfloat16)
    received = route_slots(scatter_rows(shifted))
    enc_local = encoder.reshape(shard_width, local_blocks, BLOCK)
    partial_pre = jnp.einsum(
        "sbkd,dbl->sbkl", received, enc_local, preferred_element_type=jnp.float32
    )
    pre_total = lax.psum(partial_pre, "dp")
    latent_codes = jnp.maximum(pre_total, 0.0).astype(jnp.bfloat16)
    dec_local = decoder.reshape(local_blocks, BLOCK, shard_width)
    contrib = jnp.einsum(
        "sbkl,bld->sbkd", latent_codes, dec_local, preferred_element_type=jnp.float32
    ).astype(jnp.bfloat16)
    returned = route_slots(contrib).reshape(slot_count, shard_width)
    summed_rows = jnp.einsum("sr,sd->rd", placement, returned, preferred_element_type=jnp.float32)
    rebuilt = summed_rows + bias_wide
    error = rebuilt - activations.astype(jnp.float32)
    row_loss = lax.psum(jnp.sum(error * error, axis=1), "dp")
    error_sent = route_slots(scatter_rows(error.astype(jnp.bfloat16)))
    gradient = jnp.einsum(
        "sbkl,sbkd->bld", latent_codes, error_sent, preferred_element_type=jnp.float32
    )
    return (gradient.reshape(local_blocks * BLOCK, shard_width).astype(jnp.bfloat16), row_loss)


def solution(mesh):
    placed = (
        P(("latent", "section"), "dp"),
        P("dp"),
        P("dp", ("latent", "section")),
        P(("latent", "section"), "dp"),
        P(("latent", "section"), None),
    )
    return jax.shard_map(
        on_device,
        mesh=mesh,
        in_specs=placed,
        out_specs=(P(("latent", "section"), "dp"), P(("latent", "section"))),
        check_vma=False,
    )
```

profile of v0, /device:TPU:1, one launch (start us, length us, event | category | flops | bytes accessed | tf_op | source)
XLA Modules:
  0.0 271.7 jit_solution(16894035833527401476)
XLA Ops:
  0.6 0.8 copy.56
  1.5 0.2 eq.75
  1.6 4.5 %convert_reduce_fusion = s32[2048]{0:T(1024)S(1)} fusion(s32[2048]{0:T(1024)S(1)} %eq.75), kind=kLoop, calls=%fused_computation | loop fusion | flops 20969472 | bytes 16384 | tf_op jit(solution)/shard_map/reduce_sum | solution.py:25
  6.1 0.3 reduce_sum.21
  6.4 0.1 copy.57
  6.5 0.7 multiply_add_fusion
  7.2 0.7 convert_element_type.55
  7.9 6.9 %convolution_convert_fusion.1 = bf16[4096,288]{0,1:T(8,128)(2,1)} fusion(s32[512]{0:T(512)S(1)} %bitcast.32, s32[512]{0:T(512)S(1)} %bitcast.35, s32[512]{0:T(512)S(1)} %bitcast.38, s32[512]{0:T(512)S(1)} %bitcast.29, bf16[512,288]{0,1:T(8,128)(2,1)} %param.5, f32[288]{0:T(512)S(1)} %convert_element_type.55), kind=kOutput, calls=%fused_computation.12 | convolution fusion | flops 1243136000 | bytes 2663552 | tf_op jit(solution)/shard_map/dot_general | solution.py:36
  14.8 3.3 %copy.58 = bf16[4096,288]{1,0:T(8,128)(2,1)S(1)} copy(bf16[4096,288]{0,1:T(8,128)(2,1)} %convolution_convert_fusion.1) | data formatting | bytes 4718592 | tf_op jit(solution)/shard_map/convert_element_type | solution.py:36
  18.1 2.5 reshape.31
  20.6 10.6 %all-to-all-start = ((bf16[32,32,4,288]{3,2,1,0:T(4,128)(2,1)}), bf16[32,32,4,288]{3,2,1,0:T(4,128)(2,1)S(1)}, u32[]{:S(2)}, u32[]{:S(2)}) async-start(bf16[32,32,4,288]{3,2,1,0:T(4,128)(2,1)} %reshape.31), calls=%async_computation | async-start | bytes 6291456 | tf_op jit(solution)/shard_map/all_to_all | solution.py:10
  31.2 2.6 copy.59
  33.8 2.5 copy.61
  36.3 32.9 %all-to-all-done = bf16[32,32,4,288]{3,2,1,0:T(4,128)(2,1)S(1)} async-done(((bf16[32,32,4,288]{3,2,1,0:T(4,128)(2,1)}), bf16[32,32,4,288]{3,2,1,0:T(4,128)(2,1)S(1)}, u32[]{:S(2)}, u32[]{:S(2)}) %all-to-all-start) | async-done | bytes 2359328 | tf_op jit(solution)/shard_map/all_to_all | solution.py:10
  69.2 4.8 %fusion.18 = f32[32,32,4,64]{3,0,2,1:T(8,128)} fusion(bf16[288,32,64,1]{0,2,3,1:T(8,128)(2,1)} %bitcast.28, bf16[32,32,4,288]{3,2,1,0:T(4,128)(2,1)S(1)} %all-to-all-done), kind=kOutput, calls=%fused_computation.24 | convolution fusion | flops 150994944 | bytes 4587520 | tf_op jit(solution)/shard_map/sbkd,dbl->sbkl/dot_general | solution.py:43
  74.0 66.9 %all-reduce.1 = bf16[32,32,4,64]{3,0,2,1:T(8,128)(2,1)S(1)} all-reduce(f32[32,32,4,64]{3,0,2,1:T(8,128)} %fusion.18), channel_id=1, replica_groups=mesh['dp'=16,'latent'=8,'section'=4] {'dp'}, use_global_device_ids=true, to_apply=%region_1.0 | all-reduce | flops 262144 | bytes 1572864 | tf_op jit(solution)/shard_map/psum | solution.py:46
  140.9 0.0 copy-start
  140.9 0.0 copy-done.1
  140.9 1.0 convert_bitcast_fusion
  141.9 1.6 copy.62
  143.6 57.3 %all_to_all.15 = bf16[32,32,4,288]{3,2,1,0:T(4,128)(2,1)S(1)} all-to-all(bf16[32,32,4,288]{3,2,1,0:T(4,128)(2,1)S(1)} %copy.62), channel_id=1, replica_groups=mesh['dp'=16,'latent'=8,'section'=4] {'latent','section'}, dimensions={0} | all-to-all | bytes 4718592 | tf_op jit(solution)/shard_map/all_to_all | solution.py:10
  200.9 3.0 %reshape.34 = bf16[4096,288]{1,0:T(8,128)(2,1)} reshape(bf16[32,32,4,288]{3,2,1,0:T(4,128)(2,1)S(1)} %all_to_all.15) | data formatting | bytes 4718592 | tf_op jit(solution)/shard_map/reshape | solution.py:52
  203.9 0.0 copy-done.2
  203.9 5.8 %multiply_reduce_fusion = (f32[512]{0:T(512)S(1)}, bf16[512,288]{0,1:T(8,128)(2,1)S(1)}) fusion(bf16[512,288]{0,1:T(8,128)(2,1)S(1)} %copy-done.2, f32[288]{0:T(512)S(1)} %convert_element_type.55, bf16[4096,288]{1,0:T(8,128)(2,1)} %reshape.34, s32[512]{0:T(512)S(1)} %bitcast.33, s32[512]{0:T(512)S(1)} %bitcast.36, s32[512]{0:T(512)S(1)} %bitcast.39, ...), kind=kOutput, calls=%fused_computation.29 | convolution fusion | flops 1242398208 | bytes 2960512 | tf_op jit(solution)/shard_map/sr,sd->rd/dot_general | solution.py:53
  209.7 5.8 %convolution_convert_fusion = bf16[4096,288]{0,1:T(8,128)(2,1)} fusion(s32[512]{0:T(512)S(1)} %bitcast.34, s32[512]{0:T(512)S(1)} %bitcast.37, s32[512]{0:T(512)S(1)} %bitcast.40, s32[512]{0:T(512)S(1)} %bitcast.31, bf16[512,288]{0,1:T(8,128)(2,1)S(1)} %get-tuple-element.19), kind=kOutput, calls=%fused_computation.11 | convolution fusion | flops 1242693632 | bytes 2662400 | tf_op jit(solution)/shard_map/dot_general | solution.py:36
  215.5 3.3 %copy.63 = bf16[4096,288]{1,0:T(8,128)(2,1)S(1)} copy(bf16[4096,288]{0,1:T(8,128)(2,1)} %convolution_convert_fusion) | data formatting | bytes 4718592 | tf_op jit(solution)/shard_map/convert_element_type | solution.py:36
  218.8 2.5 reshape.35
  221.3 5.3 %all-to-all-start.2 = ((bf16[32,32,4,288]{3,2,1,0:T(4,128)(2,1)}), bf16[32,32,4,288]{3,2,1,0:T(4,128)(2,1)S(1)}, u32[]{:S(2)}, u32[]{:S(2)}) async-start(bf16[32,32,4,288]{3,2,1,0:T(4,128)(2,1)} %reshape.35), calls=%async_computation.2 | async-start | bytes 6291456 | tf_op jit(solution)/shard_map/all_to_all | solution.py:10
  226.6 23.4 %psum.15 = f32[512]{0:T(512)} all-reduce(f32[512]{0:T(512)S(1)} %get-tuple-element.18), channel_id=1, replica_groups=mesh['dp'=16,'latent'=8,'section'=4] {'dp'}, use_global_device_ids=true, to_apply=%region_3.0 | all-reduce | flops 512 | bytes 4096 | tf_op jit(solution)/shard_map/psum | solution.py:56
  249.9 14.5 %all-to-all-done.2 = bf16[32,32,4,288]{3,2,1,0:T(4,128)(2,1)S(1)} async-done(((bf16[32,32,4,288]{3,2,1,0:T(4,128)(2,1)}), bf16[32,32,4,288]{3,2,1,0:T(4,128)(2,1)S(1)}, u32[]{:S(2)}, u32[]{:S(2)}) %all-to-all-start.2) | async-done | bytes 2359328 | tf_op jit(solution)/shard_map/all_to_all | solution.py:10
  264.5 4.7 %bitcast_convert_fusion = bf16[32,64,288]{2,1,0:T(8,128)(2,1)} fusion(bf16[32,32,4,288]{3,2,1,0:T(4,128)(2,1)S(1)} %all-to-all-done.2, bf16[32,32,4,64]{3,0,2,1:T(8,128)(2,1)} %copy-done), kind=kOutput, calls=%fused_computation.17 | convolution fusion | flops 152371200 | bytes 4063232 | tf_op jit(solution)/shard_map/sbkl,sbkd->bld/dot_general | solution.py:58
  269.2 2.5 copy.65
  (4 shorter events, 0.0 us)
Async XLA Ops:
  20.6 48.6 %all-to-all-start = ((bf16[32,32,4,288]{3,2,1,0:T(4,128)(2,1)}), bf16[32,32,4,288]{3,2,1,0:T(4,128)(2,1)S(1)}, u32[]{:S(2)}, u32[]{:S(2)}) async-start(bf16[32,32,4,288]{3,2,1,0:T(4,128)(2,1)} %reshape.31), calls=%async_computation | async-start | bytes 6291456 | tf_op jit(solution)/shard_map/all_to_all | solution.py:10
  74.0 66.9 %copy-start.1 = (bf16[2048,288]{1,0:T(8,128)(2,1)S(1)}, bf16[2048,288]{1,0:T(8,128)(2,1)}, u32[]{:S(2)}) copy-start(bf16[2048,288]{1,0:T(8,128)(2,1)} %copy.61) | copy-start | bytes 3538948
  140.9 1.0 copy-start
  200.9 3.0 %copy-start.2 = (bf16[512,288]{0,1:T(8,128)(2,1)S(1)}, bf16[512,288]{0,1:T(8,128)(2,1)}, u32[]{:S(2)}) copy-start(bf16[512,288]{0,1:T(8,128)(2,1)} %param.5) | copy-start | bytes 884740
  221.3 43.2 %all-to-all-start.2 = ((bf16[32,32,4,288]{3,2,1,0:T(4,128)(2,1)}), bf16[32,32,4,288]{3,2,1,0:T(4,128)(2,1)S(1)}, u32[]{:S(2)}, u32[]{:S(2)}) async-start(bf16[32,32,4,288]{3,2,1,0:T(4,128)(2,1)} %reshape.35), calls=%async_computation.2 | async-start | bytes 6291456 | tf_op jit(solution)/shard_map/all_to_all | solution.py:10
where the time goes:
time: 273 us; the launch traced here: 272 us
  blocking collectives  148 us (54%)
  waiting for transfers between devices  47.4 us (17%)
  matrix products  29 us (11%)
  local copies, waits for them, and re-layouts  25.1 us (9%)
  starting transfers between devices  15.9 us (6%)
  other arithmetic  5.87 us (2%)
    psum x1, blocking collectives, on_device(): pre_total = lax.psum(partial_pre, 'dp')  66.9 us
    all_to_all x1, blocking collectives, route_slots(): lax.all_to_all(buffer, ('latent', 'section'), split_axis=0, concat_axis=0...  57.3 us
    all_to_all x2, waiting for transfers between devices, route_slots(): lax.all_to_all(buffer, ('latent', 'section'), split_axis=0, concat_axis=0...  47.4 us
    psum x1, blocking collectives, on_device(): row_loss = lax.psum(jnp.sum(error * error, axis=1), 'dp')  23.4 us
    all_to_all x2, starting transfers between devices, route_slots(): lax.all_to_all(buffer, ('latent', 'section'), split_axis=0, concat_axis=0...  15.9 us
    dot_general x2, matrix products, scatter_rows(): jnp.dot(placement, values, preferred_element_type=jnp.float32)  12.7 us
    unnamed x10, local copies, waits for them, and re-layouts  8.39 us
    convert_element_type x2, local copies, waits for them, and re-layouts, scatter_rows(): jnp.dot(placement, values, preferred_element_type=jnp.float32)  6.55 us
  transfers between devices with their start and end apart: 2, of which 2 were waited for; matrix products, arithmetic and copies ran while one was open for 2% of the time, Pallas kernels for 0%

commit v1 on v0

v1 whole, which is shorter than its diff:
```python
import jax
import jax.numpy as jnp
from jax import lax
from jax.experimental import pallas as pl
from jax.experimental.pallas import tpu as pltpu
from jax.sharding import PartitionSpec as P

BLOCK = 64
PLANE = ("latent", "section")
GROUPS = 32
SHARDS = 16
LOCAL = 32
ROWS = 512
FEATURES = 288
HALF = FEATURES // 2
NAMED = 4
MAIN = 64
EXTRA = 16
MAIN_SLOTS = GROUPS * MAIN
EXTRA_SLOTS = GROUPS * EXTRA
SLOTS = MAIN_SLOTS + EXTRA_SLOTS
PACKED = HALF + 3 * EXTRA
PAIRS = GROUPS // 2
LANE_TILES = SLOTS // 128
CHUNK_TILES = 5
CHUNK_ROWS = 16 * CHUNK_TILES

NT = (((1,), (1,)), ((), ()))
F32 = jnp.float32
BF16 = jnp.bfloat16


def mm(a, b):
    return jnp.dot(a, b, preferred_element_type=F32)


def mm_nt(a, b):
    return lax.dot_general(a, b, NT, preferred_element_type=F32)


def identity(n):
    rows = lax.broadcasted_iota(jnp.int32, (n, n), 0)
    return jnp.where(rows == lax.broadcasted_iota(jnp.int32, (n, n), 1), 1.0, 0.0).astype(BF16)


def lane_offset(tile, width=128):
    return pl.ds(pl.multiple_of(tile * width, width), width)


def store_pair(out_ref, pair, values):
    top, bottom = values[:HALF], values[HALF:]
    low = lax.broadcasted_iota(jnp.int32, (HALF, 128), 1) < MAIN
    first = jnp.where(low, top, pltpu.roll(bottom, MAIN, 1))
    second = jnp.where(low, pltpu.roll(top, MAIN, 1), bottom)
    out_ref[pair, 0:HALF, :] = first.astype(BF16)
    out_ref[pair + PAIRS, 0:HALF, :] = second.astype(BF16)


def store_extra(out_ref, values):
    for part in range(3):
        piece = values[:, part * 128 : (part + 1) * 128].astype(BF16)
        out_ref[:, HALF + part * EXTRA : HALF + (part + 1) * EXTRA, :] = piece.reshape(GROUPS, EXTRA, 128)


def unpack(in_ref, full_ref):
    def one(pair, carry):
        first = in_ref[pair, 0:HALF, :].astype(F32)
        second = in_ref[pair + PAIRS, 0:HALF, :].astype(F32)
        low = lax.broadcasted_iota(jnp.int32, (HALF, 128), 1) < MAIN
        full_ref[0:HALF, lane_offset(pair)] = jnp.where(low, first, pltpu.roll(second, MAIN, 1)).astype(BF16)
        full_ref[HALF:, lane_offset(pair)] = jnp.where(low, pltpu.roll(first, MAIN, 1), second).astype(BF16)
        return carry

    lax.fori_loop(0, PAIRS, one, 0, unroll=2)
    eye = identity(128)
    turned, last = None, None
    for part in range(3):
        last = in_ref[:, HALF + part * EXTRA : HALF + (part + 1) * EXTRA, :].reshape(EXTRA_SLOTS, 128)
        turned = mm_nt(eye, last)
        height = min(128, FEATURES - part * 128)
        full_ref[part * 128 : part * 128 + height, MAIN_SLOTS:] = turned[:height].astype(BF16)
    return last, turned


def prepare_kernel(act_ref, bias_ref, blocks_ref, send_ref, place_ref, extra_ref):
    blocks = blocks_ref[...]
    target = lax.shift_right_logical(blocks, 5)
    local = jnp.bitwise_and(blocks, LOCAL - 1)
    groups = lax.broadcasted_iota(jnp.int32, (GROUPS, ROWS), 0)
    hits = [groups == target[k : k + 1, :] for k in range(NAMED)]
    counts = sum(jnp.where(hit, 1.0, 0.0) for hit in hits).astype(BF16)
    before = lax.broadcasted_iota(jnp.int32, (ROWS, ROWS), 0) < lax.broadcasted_iota(jnp.int32, (ROWS, ROWS), 1)
    earlier = mm(counts, jnp.where(before, 1.0, 0.0).astype(BF16))
    slots, names, most = [], [], jnp.zeros((1, ROWS), jnp.int32)
    for k in range(NAMED):
        mine = target[k : k + 1, :]
        rank = jnp.sum(jnp.where(hits[k], earlier, 0.0), axis=0, keepdims=True).astype(jnp.int32)
        for other in range(k):
            rank = rank + jnp.where(target[other : other + 1, :] == mine, 1, 0)
        main = (jnp.bitwise_and(mine, PAIRS - 1) * 2 + lax.shift_right_logical(mine, 4)) * MAIN + rank
        extra = MAIN_SLOTS + mine * EXTRA + (rank - MAIN)
        slots.append(jnp.where(rank < MAIN, main, jnp.where(rank < MAIN + EXTRA, extra, -1)))
        names.append((local[k : k + 1, :] + 1).astype(F32))
        most = jnp.maximum(most, rank)
    over = jnp.where(jnp.max(most, axis=1, keepdims=True) >= MAIN + EXTRA, 1.0, 0.0)
    shifted = (act_ref[...].astype(F32) - bias_ref[...]).astype(BF16)

    def placed(start, count):
        index = lax.broadcasted_iota(jnp.int32, (count, ROWS), 0) + start
        named = jnp.zeros((count, ROWS), F32)
        for k in range(NAMED):
            named = jnp.where(index == slots[k], names[k], named)
        return named.astype(BF16), jnp.where(named > 0.0, 1.0, 0.0).astype(BF16)

    named, place = placed(MAIN_SLOTS, EXTRA_SLOTS)
    place_ref[MAIN_SLOTS:, :] = place
    padded = jnp.concatenate([shifted, jnp.zeros((96, ROWS), BF16)], axis=0)
    values = mm_nt(place, padded)
    lane = lax.broadcasted_iota(jnp.int32, (EXTRA_SLOTS, 128), 1)
    ids = mm(named, jnp.ones((ROWS, 128), BF16))
    store_extra(send_ref, values)
    extra_ref[...] = jnp.where(lane == 32, ids, values[:, 256:])
    row = lax.broadcasted_iota(jnp.int32, (EXTRA, 128), 0)
    high = lax.broadcasted_iota(jnp.int32, (EXTRA, 128), 1) >= MAIN

    def one(pair, carry):
        named, place = placed(pair * 128, 128)
        place_ref[pl.ds(pl.multiple_of(pair * 128, 128), 128), :] = place
        store_pair(send_ref, pair, mm_nt(shifted, place))
        ids = mm_nt(jnp.ones((EXTRA, ROWS), BF16), named)
        for half in range(2):
            device = pair + half * PAIRS
            mine = ids if half else pltpu.roll(ids, MAIN, 1)
            tile = extra_ref[pl.ds(pl.multiple_of(device * EXTRA, EXTRA), EXTRA), :]
            tile = jnp.where(high & (row == 0), mine, tile)
            tile = jnp.where(high & (row == 1), jnp.broadcast_to(over, (EXTRA, 128)), tile)
            send_ref[device, HALF + 2 * EXTRA :, :] = tile.astype(BF16)
        return carry

    lax.fori_loop(0, PAIRS, one, 0, unroll=2)


def encode_kernel(recv_ref, enc_ref, out_ref, ids_ref, over_ref, full_ref):
    last, turned = unpack(recv_ref, full_ref)
    pick = lax.broadcasted_iota(jnp.int32, (2 * GROUPS, EXTRA_SLOTS), 0)
    column = lax.broadcasted_iota(jnp.int32, (2 * GROUPS, EXTRA_SLOTS), 1)
    wanted = jnp.where(pick < GROUPS, pick * EXTRA, (pick - GROUPS) * EXTRA + 1)
    rows = mm(jnp.where(column == wanted, 1.0, 0.0).astype(BF16), last)
    first, second = rows[:PAIRS], rows[PAIRS:GROUPS]
    low = lax.broadcasted_iota(jnp.int32, (PAIRS, 128), 1) < MAIN
    ids_ref[0:PAIRS, :] = jnp.where(low, pltpu.roll(first, MAIN, 1), second)
    for part in range(EXTRA_SLOTS // 128):
        ids_ref[PAIRS + part : PAIRS + part + 1, :] = turned[32:33, part * 128 : (part + 1) * 128]
    ids_ref[LANE_TILES:, :] = jnp.zeros((24 - LANE_TILES, 128), F32)
    flags = jnp.where(lax.broadcasted_iota(jnp.int32, (GROUPS, 128), 1) == MAIN, rows[GROUPS:], 0.0)
    flag = jnp.max(jnp.max(flags, axis=1, keepdims=True), axis=0, keepdims=True)
    over_ref[...] = jnp.broadcast_to(flag, (8, 128)).astype(jnp.int32)

    def one(tile, carry):
        values = full_ref[:, lane_offset(tile, 256)]
        ids = jnp.concatenate([ids_ref[pl.ds(2 * tile, 1), :], ids_ref[pl.ds(2 * tile + 1, 1), :]], axis=1)
        total = jnp.zeros((BLOCK, 256), F32)
        for group in range(LOCAL // 4):
            part = mm(enc_ref[group * 256 : (group + 1) * 256, :], values)
            for b in range(4):
                total = jnp.where(ids == float(group * 4 + b + 1), part[b * BLOCK : (b + 1) * BLOCK], total)
        for half in range(2):
            lane_tile = 2 * tile + half
            for quarter in range(4):
                piece = total[quarter * 16 : (quarter + 1) * 16, half * 128 : (half + 1) * 128]
                out_ref[
                    quarter + 4 * (lane_tile // CHUNK_TILES),
                    pl.ds(pl.multiple_of((lane_tile % CHUNK_TILES) * 16, 16), 16),
                    :,
                ] = piece.astype(BF16)
        return carry

    lax.fori_loop(0, LANE_TILES // 2, one, 0)


def load_codes(codes_ref, full_ref):
    for tile in range(LANE_TILES):
        for quarter in range(4):
            full_ref[quarter * 16 : (quarter + 1) * 16, tile * 128 : (tile + 1) * 128] = codes_ref[
                quarter + 4 * (tile // CHUNK_TILES),
                (tile % CHUNK_TILES) * 16 : (tile % CHUNK_TILES + 1) * 16,
                :,
            ]


def decode_kernel(codes_ref, ids_ref, dec_ref, send_ref, full_ref, spread_ref, extra_ref):
    load_codes(codes_ref, full_ref)

    def contribution(tile):
        codes = full_ref[:, lane_offset(tile, 256)]
        ids = jnp.concatenate([ids_ref[pl.ds(2 * tile, 1), :], ids_ref[pl.ds(2 * tile + 1, 1), :]], axis=1)
        ids = jnp.broadcast_to(ids, (BLOCK, 256)).astype(BF16)
        for b in range(LOCAL):
            spread_ref[b * BLOCK : (b + 1) * BLOCK, :] = jnp.where(ids == BF16(b + 1), codes, BF16(0))
        return mm(dec_ref[...], spread_ref[...])

    def one(tile, carry):
        values = contribution(tile)
        store_pair(send_ref, 2 * tile, values[:, :128])
        store_pair(send_ref, 2 * tile + 1, values[:, 128:])
        return carry

    lax.fori_loop(0, PAIRS // 2, one, 0)
    extra_ref[FEATURES:, :] = jnp.zeros((384 - FEATURES, EXTRA_SLOTS), BF16)
    for tile in range(PAIRS // 2, LANE_TILES // 2):
        start = tile * 256 - MAIN_SLOTS
        extra_ref[0:FEATURES, start : start + 256] = contribution(tile).astype(BF16)
    store_extra(send_ref, mm_nt(identity(EXTRA_SLOTS), extra_ref[...]))


def combine_kernel(recv_ref, place_ref, act_ref, bias_ref, send_ref, loss_ref, full_ref):
    unpack(recv_ref, full_ref)
    error = mm(full_ref[...], place_ref[...]) + bias_ref[...] - act_ref[...].astype(F32)
    loss_ref[...] = jnp.broadcast_to(jnp.sum(error * error, axis=0, keepdims=True), (8, ROWS))
    sent = error.astype(BF16)

    def one(pair, carry):
        place = place_ref[pl.ds(pl.multiple_of(pair * 128, 128), 128), :]
        store_pair(send_ref, pair, mm_nt(sent, place))
        return carry

    lax.fori_loop(0, PAIRS, one, 0, unroll=2)
    padded = jnp.concatenate([sent, jnp.zeros((96, ROWS), BF16)], axis=0)
    store_extra(send_ref, mm_nt(place_ref[MAIN_SLOTS:, :], padded))


def gradient_kernel(recv_ref, codes_ref, ids_ref, grad_ref, full_ref, code_ref, spread_ref):
    unpack(recv_ref, full_ref)
    load_codes(codes_ref, code_ref)

    def one(group, carry):
        for b in range(4):
            wanted = (group * 4 + b + 1).astype(F32)
            for tile in range(LANE_TILES):
                ids = jnp.broadcast_to(ids_ref[tile : tile + 1, :], (BLOCK, 128)).astype(BF16)
                codes = code_ref[:, tile * 128 : (tile + 1) * 128]
                mask = ids == wanted.astype(BF16)
                spread_ref[b * BLOCK : (b + 1) * BLOCK, tile * 128 : (tile + 1) * 128] = jnp.where(
                    mask, codes, BF16(0)
                )
        grad_ref[:, lane_offset(group, 256)] = mm_nt(full_ref[...], spread_ref[...]).astype(BF16)
        return carry

    lax.fori_loop(0, LOCAL // 4, one, 0)


def call(kernel, out_shape, scratch, flops, name):
    return pl.pallas_call(
        kernel,
        out_shape=out_shape,
        scratch_shapes=scratch,
        name=name,
        compiler_params=pltpu.CompilerParams(vmem_limit_bytes=40 * 1024 * 1024),
        cost_estimate=pl.CostEstimate(flops=flops, bytes_accessed=6_000_000, transcendentals=0),
    )


def shape(dims, dtype=BF16):
    return jax.ShapeDtypeStruct(dims, dtype)


def route(buffer):
    return lax.all_to_all(buffer, PLANE, split_axis=0, concat_axis=0, tiled=True)


def sum_codes(partial):
    received = lax.all_to_all(partial, "dp", split_axis=0, concat_axis=0, tiled=True)
    total = jnp.sum(received.astype(F32), axis=0)
    codes = jnp.maximum(total, 0.0).astype(BF16)
    copies = jnp.broadcast_to(codes[None], (SHARDS,) + codes.shape)
    return lax.all_to_all(copies, "dp", split_axis=0, concat_axis=0, tiled=True)


def sum_loss(part):
    copies = jnp.broadcast_to(part.reshape(1, 4, 128), (SHARDS, 4, 128))
    received = lax.all_to_all(copies, "dp", split_axis=0, concat_axis=0, tiled=True)
    return jnp.sum(received, axis=0).reshape(ROWS)


def padded_plan(activations, bias_dec, encoder, decoder, active_blocks):
    row_count, shard_width = activations.shape
    per_row = active_blocks.shape[1]
    groups = lax.axis_size(PLANE)
    local_blocks = encoder.shape[1] // BLOCK
    total_blocks = local_blocks * groups
    capacity = max(2, 2 * row_count * per_row // total_blocks)
    slot_count = total_blocks * capacity
    pair_blocks = active_blocks.reshape(-1)
    pair_iota = jnp.arange(pair_blocks.shape[0], dtype=jnp.int32)
    same_block = pair_blocks[:, None] == pair_blocks[None, :]
    earlier = pair_iota[None, :] < pair_iota[:, None]
    block_rank = jnp.sum((same_block & earlier).astype(jnp.int32), axis=1)
    slot_index = (pair_blocks * capacity + block_rank).reshape(row_count, per_row)
    slot_iota = jnp.arange(slot_count, dtype=jnp.int32)
    placement = jnp.zeros((slot_count, row_count), BF16)
    for which in range(per_row):
        placement = placement + (slot_index[:, which][None, :] == slot_iota[:, None]).astype(BF16)
    slot_shape = (groups, local_blocks, capacity, shard_width)

    def scatter_rows(values):
        filled = jnp.dot(placement, values, preferred_element_type=F32).astype(values.dtype)
        return filled.reshape(slot_shape)

    bias_wide = bias_dec.astype(F32)[None, :]
    shifted = (activations.astype(F32) - bias_wide).astype(BF16)
    received = route(scatter_rows(shifted))
    enc_local = encoder.reshape(shard_width, local_blocks, BLOCK)
    partial_pre = jnp.einsum("sbkd,dbl->sbkl", received, enc_local, preferred_element_type=F32)
    pre_total = lax.psum(partial_pre, "dp")
    latent_codes = jnp.maximum(pre_total, 0.0).astype(BF16)
    dec_local = decoder.reshape(local_blocks, BLOCK, shard_width)
    contrib = jnp.einsum("sbkl,bld->sbkd", latent_codes, dec_local, preferred_element_type=F32).astype(BF16)
    returned = route(contrib).reshape(slot_count, shard_width)
    summed_rows = jnp.einsum("sr,sd->rd", placement, returned, preferred_element_type=F32)
    error = summed_rows + bias_wide - activations.astype(F32)
    row_loss = lax.psum(jnp.sum(error * error, axis=1), "dp")
    error_sent = route(scatter_rows(error.astype(BF16)))
    gradient = jnp.einsum("sbkl,sbkd->bld", latent_codes, error_sent, preferred_element_type=F32)
    return gradient.reshape(local_blocks * BLOCK, shard_width).astype(BF16), row_loss


def on_device(activations, bias_dec, encoder, decoder, active_blocks):
    act = activations.T
    bias = bias_dec.astype(F32).reshape(FEATURES, 1)
    packed = shape((GROUPS, PACKED, 128))
    full = pltpu.VMEM((FEATURES, SLOTS), BF16)
    spread = pltpu.VMEM((LOCAL * BLOCK, 256), BF16)
    sent, place = call(
        prepare_kernel,
        (packed, shape((SLOTS, ROWS))),
        [pltpu.VMEM((EXTRA_SLOTS, 128), F32)],
        2 * FEATURES * SLOTS * ROWS,
        "prepare",
    )(act, bias, active_blocks.T)
    received = route(sent)
    partial, ids, over = call(
        encode_kernel,
        (shape((SHARDS, CHUNK_ROWS, 128)), shape((24, 128), F32), shape((8, 128), jnp.int32)),
        [full],
        2 * FEATURES * SLOTS * LOCAL * BLOCK,
        "encode",
    )(received, encoder.T)
    codes = sum_codes(partial)
    sent = call(
        decode_kernel,
        packed,
        [
            pltpu.VMEM((BLOCK, SLOTS), BF16),
            spread,
            pltpu.VMEM((384, EXTRA_SLOTS), BF16),
        ],
        2 * FEATURES * SLOTS * LOCAL * BLOCK,
        "decode",
    )(codes, ids, decoder.T)
    received = route(sent)
    sent, loss = call(
        combine_kernel,
        (packed, shape((8, ROWS), F32)),
        [full],
        4 * FEATURES * SLOTS * ROWS,
        "combine",
    )(received, place, act, bias)
    received = route(sent)
    row_loss = sum_loss(loss[0])

    def packed_plan():
        gradient = call(
            gradient_kernel,
            shape((FEATURES, LOCAL * BLOCK)),
            [full, pltpu.VMEM((BLOCK, SLOTS), BF16), pltpu.VMEM((4 * BLOCK, SLOTS), BF16)],
            2 * FEATURES * SLOTS * LOCAL * BLOCK,
            "gradient",
        )(received, codes, ids)
        return gradient.T, row_loss

    return lax.cond(
        over[0, 0] > 0,
        lambda: padded_plan(activations, bias_dec, encoder, decoder, active_blocks),
        packed_plan,
    )


def solution(mesh):
    placed = (
        P(PLANE, "dp"),
        P("dp"),
        P("dp", PLANE),
        P(PLANE, "dp"),
        P(PLANE, None),
    )
    return jax.shard_map(
        on_device,
        mesh=mesh,
        in_specs=placed,
        out_specs=(P(PLANE, "dp"), P(PLANE)),
        check_vma=False,
    )
```

time: 273 us -> 204 us (0.75)
  blocking collectives: 148 us -> 106 us
  Pallas kernels: 0 us -> 34.1 us
  matrix products: 29 us -> 0 us
  local copies, waits for them, and re-layouts: 25.1 us -> 5.69 us
  waiting for transfers between devices: 47.4 us -> 39.9 us
  other arithmetic: 5.87 us -> 0.09 us
    psum x2 -> x0, blocking collectives: 90.3 us -> none  [the longest x1 66.9 us: on_device(): pre_total = lax.psum(partial_pre, 'dp')]
    all_to_all x1 -> x4, blocking collectives: 57.3 us -> 106 us  [the longest x1 34.6 us: route(): lax.all_to_all(buffer, PLANE, split_axis=0, concat_axis=0, tiled=True)]
    pallas_call x0 -> x5, Pallas kernels: none -> 34.1 us  [the longest x1 8.5 us: on_device(): call(encode_kernel, (shape((SHARDS, CHUNK_ROWS, 128)), shape((24, 128), F...]
    dot_general x6 -> x0, matrix products: 29 us -> none  [the longest x2 12.7 us: scatter_rows(): jnp.dot(placement, values, preferred_element_type=jnp.float32)]
    convert_element_type x3 -> x0, local copies, waits for them, and re-layouts: 8.17 us -> none  [the longest x2 6.55 us: scatter_rows(): jnp.dot(placement, values, preferred_element_type=jnp.float32)]
    all_to_all x2, waiting for transfers between devices: 47.4 us -> 39.9 us  [route(): lax.all_to_all(buffer, PLANE, split_axis=0, concat_axis=0, tiled=True)]
    reshape x3 -> x1, local copies, waits for them, and re-layouts: 8.04 us -> 0.77 us  [on_device(): bias = bias_dec.astype(F32).reshape(FEATURES, 1)]
    reduce_sum x1 -> x2, other arithmetic: 4.48 us -> 0.08 us  [the longest x1 0.05 us: sum_codes(): total = jnp.sum(received.astype(F32), axis=0)]
  transfers between devices with their start and end apart: 2 -> 2, of which waited for: 2 -> 2; matrix products, arithmetic and copies ran while one was open for 2% -> 1% of each run, Pallas kernels for 0% -> 0%
where the time goes in v1:
time: 204 us
  blocking collectives  106 us (52%)
  waiting for transfers between devices  39.9 us (20%)
  Pallas kernels  34.1 us (17%)
  starting transfers between devices  16.3 us (8%)
  local copies, waits for them, and re-layouts  5.69 us (3%)
    all_to_all x2, waiting for transfers between devices, route(): lax.all_to_all(buffer, PLANE, split_axis=0, concat_axis=0, tiled=True)  39.9 us
    all_to_all x1, blocking collectives, route(): lax.all_to_all(buffer, PLANE, split_axis=0, concat_axis=0, tiled=True)  34.6 us
    all_to_all x1, blocking collectives, sum_codes(): return lax.all_to_all(copies, 'dp', split_axis=0, concat_axis=0, tiled=True)  27.5 us
    all_to_all x1, blocking collectives, sum_codes(): lax.all_to_all(partial, 'dp', split_axis=0, concat_axis=0, tiled=True)  27 us
    all_to_all x1, blocking collectives, sum_loss(): lax.all_to_all(copies, 'dp', split_axis=0, concat_axis=0, tiled=True)  16.9 us
    all_to_all x2, starting transfers between devices, route(): lax.all_to_all(buffer, PLANE, split_axis=0, concat_axis=0, tiled=True)  16.3 us
    pallas_call x1, Pallas kernels, on_device(): call(encode_kernel, (shape((SHARDS, CHUNK_ROWS, 128)), shape((24, 128), F...  8.5 us
    pallas_call x1, Pallas kernels, on_device(): call(prepare_kernel, (packed, shape((SLOTS, ROWS))), [pltpu.VMEM((EXTRA_S...  7.22 us
  transfers between devices with their start and end apart: 2, of which 2 were waited for; matrix products, arithmetic and copies ran while one was open for 1% of the time, Pallas kernels for 0%

profile of v1, /device:TPU:1, one launch (start us, length us, event | category | flops | bytes accessed | tf_op | source)
XLA Modules:
  0.0 203.7 jit_solution(17478419167038903017)
XLA Ops:
  0.6 0.8 reshape.59.bias_ref
  1.4 7.2 %prepare.1 = (bf16[32,192,128]{2,1,0:T(8,128)(2,1)}, bf16[2560,512]{1,0:T(8,128)(2,1)S(1)}) custom-call(bf16[288,512]{1,0:T(8,128)(2,1)} %bitcast.38, f32[288,1]{1,0:T(8,128)S(1)} %reshape.59.bias_ref, s32[4,512]{1,0:T(4,128)} %bitcast.35), custom_call_target="tpu_custom_call" | custom-call | flops 754974720 | bytes 6000000 | tf_op jit(solution)/shard_map/prepare/pallas_call | solution.py:333
  8.6 0.0 copy-start
  8.6 1.5 copy-done
  10.1 10.5 %all-to-all-start.3 = ((bf16[32,192,128]{2,1,0:T(8,128)(2,1)}), bf16[32,192,128]{2,1,0:T(8,128)(2,1)S(1)}, u32[]{:S(2)}, u32[]{:S(2)}) async-start(bf16[32,192,128]{2,1,0:T(8,128)(2,1)} %get-tuple-element.39), calls=%async_computation.3 | async-start | bytes 3145728 | tf_op jit(solution)/shard_map/all_to_all | solution.py:268
  20.7 1.8 copy.64
  22.5 19.6 %all-to-all-done.3.recv_ref = bf16[32,192,128]{2,1,0:T(8,128)(2,1)S(1)} async-done(((bf16[32,192,128]{2,1,0:T(8,128)(2,1)}), bf16[32,192,128]{2,1,0:T(8,128)(2,1)S(1)}, u32[]{:S(2)}, u32[]{:S(2)}) %all-to-all-start.3) | async-done | bytes 1572896 | tf_op jit(solution)/shard_map/all_to_all | solution.py:268
  42.1 0.0 copy-start.4
  42.1 8.5 %encode.1 = (bf16[16,80,128]{2,1,0:T(8,128)(2,1)S(1)}, f32[24,128]{1,0:T(8,128)S(1)}, s32[8,128]{1,0:T(8,128)S(1)}) custom-call(bf16[32,192,128]{2,1,0:T(8,128)(2,1)S(1)} %all-to-all-done.3.recv_ref, bf16[2048,288]{1,0:T(8,128)(2,1)S(1)} %bitcast.30), custom_call_target="tpu_custom_call" | custom-call | flops 3019898880 | bytes 6000000 | tf_op jit(solution)/shard_map/encode/pallas_call | solution.py:341
  50.6 27.0 %all_to_all.43 = bf16[16,80,128]{2,1,0:T(8,128)(2,1)S(1)} all-to-all(bf16[16,80,128]{2,1,0:T(8,128)(2,1)S(1)} %get-tuple-element.41), channel_id=1, replica_groups=mesh['dp'=16,'latent'=8,'section'=4] {'dp'}, dimensions={0} | all-to-all | bytes 655360 | tf_op jit(solution)/shard_map/all_to_all | solution.py:272
  77.6 0.1 convert_reduce_fusion.1
  77.7 27.5 %all_to_all.44.codes_ref = bf16[16,80,128]{2,1,0:T(8,128)(2,1)S(1)} all-to-all(bf16[16,80,128]{2,1,0:T(8,128)(2,1)S(1)} %broadcast_in_dim.6), channel_id=1, replica_groups=mesh['dp'=16,'latent'=8,'section'=4] {'dp'}, dimensions={0} | all-to-all | bytes 655360 | tf_op jit(solution)/shard_map/all_to_all | solution.py:276
  105.3 0.0 copy-done.4
  105.3 5.7 %decode.1 = bf16[32,192,128]{2,1,0:T(8,128)(2,1)S(1)} custom-call(bf16[16,80,128]{2,1,0:T(8,128)(2,1)S(1)} %all_to_all.44.codes_ref, f32[24,128]{1,0:T(8,128)S(1)} %get-tuple-element.42.ids_ref, bf16[288,2048]{1,0:T(8,128)(2,1)S(1)} %bitcast.34), custom_call_target="tpu_custom_call" | custom-call | flops 3019898880 | bytes 6000000 | tf_op jit(solution)/shard_map/decode/pallas_call | solution.py:349
  110.9 0.0 copy-start.1
  110.9 0.0 copy-start.8
  111.0 34.6 %all_to_all.45.recv_ref = bf16[32,192,128]{2,1,0:T(8,128)(2,1)S(1)} all-to-all(bf16[32,192,128]{2,1,0:T(8,128)(2,1)S(1)} %decode.1), channel_id=1, replica_groups=mesh['dp'=16,'latent'=8,'section'=4] {'latent','section'}, dimensions={0} | all-to-all | bytes 3145728 | tf_op jit(solution)/shard_map/all_to_all | solution.py:268
  145.6 0.0 copy-done.1
  145.6 0.0 copy-done.8
  145.6 6.7 %combine.1 = (bf16[32,192,128]{2,1,0:T(8,128)(2,1)}, f32[8,512]{1,0:T(8,128)S(1)}) custom-call(bf16[32,192,128]{2,1,0:T(8,128)(2,1)S(1)} %all_to_all.45.recv_ref, bf16[2560,512]{1,0:T(8,128)(2,1)S(1)} %copy-done.1, bf16[288,512]{1,0:T(8,128)(2,1)S(1)} %bitcast.39, f32[288,1]{1,0:T(8,128)S(1)} %reshape.59.bias_ref), custom_call_target="tpu_custom_call" | custom-call | flops 1509949440 | bytes 6000000 | tf_op jit(solution)/shard_map/combine/pallas_call | solution.py:361
  152.3 16.9 %all_to_all.46 = f32[16,4,128]{2,1,0:T(4,128)S(1)} all-to-all(f32[16,4,128]{2,1,0:T(4,128)S(1)} %broadcast_in_dim.8), channel_id=1, replica_groups=mesh['dp'=16,'latent'=8,'section'=4] {'dp'}, dimensions={0} | all-to-all | bytes 65536 | tf_op jit(solution)/shard_map/all_to_all | solution.py:281
  169.3 5.8 %all-to-all-start.7 = ((bf16[32,192,128]{2,1,0:T(8,128)(2,1)}), bf16[32,192,128]{2,1,0:T(8,128)(2,1)S(1)}, u32[]{:S(2)}, u32[]{:S(2)}) async-start(bf16[32,192,128]{2,1,0:T(8,128)(2,1)} %get-tuple-element.44), calls=%async_computation.7 | async-start | bytes 3145728 | tf_op jit(solution)/shard_map/all_to_all | solution.py:268
  175.1 0.5 slice.18
  176.2 20.2 %all-to-all-done.7 = bf16[32,192,128]{2,1,0:T(8,128)(2,1)S(1)} async-done(((bf16[32,192,128]{2,1,0:T(8,128)(2,1)}), bf16[32,192,128]{2,1,0:T(8,128)(2,1)S(1)}, u32[]{:S(2)}, u32[]{:S(2)}) %all-to-all-start.7) | async-done | bytes 1572896 | tf_op jit(solution)/shard_map/all_to_all | solution.py:268
  196.5 0.0 copy-done.5
  196.5 0.0 copy-done.6
  196.5 6.2 %conditional.1 = (f32[512]{0:T(512)S(1)}, bf16[2048,288]{0,1:T(8,128)(2,1)S(1)}) conditional(s32[]{:T(128)} %bitcast.16, (bf16[32,192,128]{2,1,0:T(8,128)(2,1)S(1)}, bf16[16,80,128]{2,1,0:T(8,128)(2,1)S(1)}, f32[24,128]{1,0:T(8,128)S(1)}, f32[16,4,128]{2,1,0:T(4,128)S(1)}) %tuple.15, (s32[512,4]{0,1:T(4,128)S(1)}, bf16[512,288]{0,1:T(8,128)(2,1)S(1)}, ...), branch_computations={%region_1.3_spmd, %region_3.0_spmd} | conditional | flops 4205791488 | bytes 89270392 | solution.py:381
  196.5 6.0 %gradient.1 = bf16[288,2048]{1,0:T(8,128)(2,1)S(1)} custom-call(bf16[32,192,128]{2,1,0:T(8,128)(2,1)S(1)} %get-tuple-element.21.recv_ref, bf16[16,80,128]{2,1,0:T(8,128)(2,1)S(1)} %get-tuple-element.22.codes_ref, f32[24,128]{1,0:T(8,128)S(1)} %get-tuple-element.23.ids_ref), custom_call_target="tpu_custom_call" | custom-call | flops 3019898880 | bytes 6000000 | tf_op jit(solution)/shard_map/cond/branch_0_fun/gradient/pallas_call | solution.py:372
  202.7 0.0 copy-start.7
  202.7 0.0 copy-start.11
  202.7 0.6 copy-done.7
  203.3 0.4 copy-done.11
  (7 shorter events, 0.1 us)
Async XLA Ops:
  8.6 1.5 copy-start
  10.1 32.0 %all-to-all-start.3 = ((bf16[32,192,128]{2,1,0:T(8,128)(2,1)}), bf16[32,192,128]{2,1,0:T(8,128)(2,1)S(1)}, u32[]{:S(2)}, u32[]{:S(2)}) async-start(bf16[32,192,128]{2,1,0:T(8,128)(2,1)} %get-tuple-element.39), calls=%async_computation.3 | async-start | bytes 3145728 | tf_op jit(solution)/shard_map/all_to_all | solution.py:268
  42.1 63.2 %copy-start.4 = (bf16[2048,288]{0,1:T(8,128)(2,1)S(1)}, bf16[2048,288]{0,1:T(8,128)(2,1)}, u32[]{:S(2)}) copy-start(bf16[2048,288]{0,1:T(8,128)(2,1)} %param.10) | copy-start | bytes 3538948
  110.9 34.7 %copy-start.1 = (bf16[2560,512]{1,0:T(8,128)(2,1)S(1)}, bf16[2560,512]{1,0:T(8,128)(2,1)}, u32[]{:S(2)}) copy-start(bf16[2560,512]{1,0:T(8,128)(2,1)} %copy-done) | copy-start | bytes 7864324
  110.9 34.7 %copy-start.8 = (bf16[512,288]{0,1:T(8,128)(2,1)S(1)}, bf16[512,288]{0,1:T(8,128)(2,1)}, u32[]{:S(2)}) copy-start(bf16[512,288]{0,1:T(8,128)(2,1)} %param.7) | copy-start | bytes 884740
  145.6 50.9 %copy-start.5 = (s32[512,4]{0,1:T(4,128)S(1)}, s32[512,4]{0,1:T(4,128)}, u32[]{:S(2)}) copy-start(s32[512,4]{0,1:T(4,128)} %param.11) | copy-start | bytes 24580
  145.6 50.9 %copy-start.6 = (bf16[288]{0:T(512)(128)(2,1)S(1)}, bf16[288]{0:T(512)(128)(2,1)}, u32[]{:S(2)}) copy-start(bf16[288]{0:T(512)(128)(2,1)} %param.8) | copy-start | bytes 1732
  169.3 27.2 %all-to-all-start.7 = ((bf16[32,192,128]{2,1,0:T(8,128)(2,1)}), bf16[32,192,128]{2,1,0:T(8,128)(2,1)S(1)}, u32[]{:S(2)}, u32[]{:S(2)}) async-start(bf16[32,192,128]{2,1,0:T(8,128)(2,1)} %get-tuple-element.44), calls=%async_computation.7 | async-start | bytes 3145728 | tf_op jit(solution)/shard_map/all_to_all | solution.py:268
  202.7 0.6 copy-start.7
  202.7 1.0 copy-start.11

commit v2 on v1

--- a/solution.py
+++ b/solution.py
@@ -63,15 +63,16 @@
 
 
 def unpack(in_ref, full_ref):
-    def one(pair, carry):
+    def one(pair):
+        lanes = slice(pair * 128, (pair + 1) * 128)
         first = in_ref[pair, 0:HALF, :].astype(F32)
         second = in_ref[pair + PAIRS, 0:HALF, :].astype(F32)
         low = lax.broadcasted_iota(jnp.int32, (HALF, 128), 1) < MAIN
-        full_ref[0:HALF, lane_offset(pair)] = jnp.where(low, first, pltpu.roll(second, MAIN, 1)).astype(BF16)
-        full_ref[HALF:, lane_offset(pair)] = jnp.where(low, pltpu.roll(first, MAIN, 1), second).astype(BF16)
-        return carry
-
-    lax.fori_loop(0, PAIRS, one, 0, unroll=2)
+        full_ref[0:HALF, lanes] = jnp.where(low, first, pltpu.roll(second, MAIN, 1)).astype(BF16)
+        full_ref[HALF:, lanes] = jnp.where(low, pltpu.roll(first, MAIN, 1), second).astype(BF16)
+
+    for pair in range(PAIRS):
+        one(pair)
     eye = identity(128)
     turned, last = None, None
     for part in range(3):
@@ -82,7 +83,16 @@
     return last, turned
 
 
-def prepare_kernel(act_ref, bias_ref, blocks_ref, send_ref, place_ref, extra_ref):
+def placed(slots, names, start, count):
+    index = lax.broadcasted_iota(jnp.int32, (count, ROWS), 0) + start
+    named = jnp.zeros((count, ROWS), F32)
+    for k in range(NAMED):
+        named = jnp.where(index == slots[k], names[k], named)
+    named = named.astype(BF16)
+    return named, jnp.minimum(named, BF16(1))
+
+
+def prepare_kernel(act_ref, bias_ref, blocks_ref, send_ref, slots_ref):
     blocks = blocks_ref[...]
     target = lax.shift_right_logical(blocks, 5)
     local = jnp.bitwise_and(blocks, LOCAL - 1)
@@ -105,42 +115,44 @@
     over = jnp.where(jnp.max(most, axis=1, keepdims=True) >= MAIN + EXTRA, 1.0, 0.0)
     shifted = (act_ref[...].astype(F32) - bias_ref[...]).astype(BF16)
 
-    def placed(start, count):
-        index = lax.broadcasted_iota(jnp.int32, (count, ROWS), 0) + start
-        named = jnp.zeros((count, ROWS), F32)
-        for k in range(NAMED):
-            named = jnp.where(index == slots[k], names[k], named)
-        return named.astype(BF16), jnp.where(named > 0.0, 1.0, 0.0).astype(BF16)
-
-    named, place = placed(MAIN_SLOTS, EXTRA_SLOTS)
-    place_ref[MAIN_SLOTS:, :] = place
+    for k in range(NAMED):
+        slots_ref[k : k + 1, :] = slots[k]
+    slots_ref[NAMED:, :] = jnp.zeros((8 - NAMED, ROWS), jnp.int32)
+    named, place = placed(slots, names, MAIN_SLOTS, EXTRA_SLOTS)
     padded = jnp.concatenate([shifted, jnp.zeros((96, ROWS), BF16)], axis=0)
     values = mm_nt(place, padded)
+    store_extra(send_ref, values)
     lane = lax.broadcasted_iota(jnp.int32, (EXTRA_SLOTS, 128), 1)
     ids = mm(named, jnp.ones((ROWS, 128), BF16))
-    store_extra(send_ref, values)
-    extra_ref[...] = jnp.where(lane == 32, ids, values[:, 256:])
+    last = jnp.where(lane == 32, ids, values[:, 256:])
     row = lax.broadcasted_iota(jnp.int32, (EXTRA, 128), 0)
     high = lax.broadcasted_iota(jnp.int32, (EXTRA, 128), 1) >= MAIN
-
-    def one(pair, carry):
-        named, place = placed(pair * 128, 128)
-        place_ref[pl.ds(pl.multiple_of(pair * 128, 128), 128), :] = place
-        store_pair(send_ref, pair, mm_nt(shifted, place))
+    flag = jnp.broadcast_to(over, (EXTRA, 128))
+    for double in range(PAIRS // 2):
+        named, place = placed(slots, names, double * 256, 256)
+        values = mm_nt(shifted, place)
         ids = mm_nt(jnp.ones((EXTRA, ROWS), BF16), named)
-        for half in range(2):
-            device = pair + half * PAIRS
-            mine = ids if half else pltpu.roll(ids, MAIN, 1)
-            tile = extra_ref[pl.ds(pl.multiple_of(device * EXTRA, EXTRA), EXTRA), :]
-            tile = jnp.where(high & (row == 0), mine, tile)
-            tile = jnp.where(high & (row == 1), jnp.broadcast_to(over, (EXTRA, 128)), tile)
-            send_ref[device, HALF + 2 * EXTRA :, :] = tile.astype(BF16)
-        return carry
-
-    lax.fori_loop(0, PAIRS, one, 0, unroll=2)
-
-
-def encode_kernel(recv_ref, enc_ref, out_ref, ids_ref, over_ref, full_ref):
+        for side in range(2):
+            pair = 2 * double + side
+            store_pair(send_ref, pair, values[:, side * 128 : (side + 1) * 128])
+            for half in range(2):
+                device = pair + half * PAIRS
+                mine = ids[:, side * 128 : (side + 1) * 128]
+                mine = mine if half else pltpu.roll(mine, MAIN, 1)
+                tile = last[device * EXTRA : (device + 1) * EXTRA]
+                tile = jnp.where(high & (row == 0), mine, tile)
+                tile = jnp.where(high & (row == 1), flag, tile)
+                send_ref[device, HALF + 2 * EXTRA :, :] = tile.astype(BF16)
+
+
+def place_kernel(slots_ref, place_ref):
+    slots = [slots_ref[k : k + 1, :] for k in range(NAMED)]
+    ones = [jnp.ones((1, ROWS), F32)] * NAMED
+    for start in range(0, SLOTS, 256):
+        place_ref[start : start + 256, :] = placed(slots, ones, start, 256)[0]
+
+
+def encode_kernel(recv_ref, enc_ref, rest_ref, out_ref, ids_ref, over_ref, full_ref):
     last, turned = unpack(recv_ref, full_ref)
     pick = lax.broadcasted_iota(jnp.int32, (2 * GROUPS, EXTRA_SLOTS), 0)
     column = lax.broadcasted_iota(jnp.int32, (2 * GROUPS, EXTRA_SLOTS), 1)
@@ -156,26 +168,29 @@
     flag = jnp.max(jnp.max(flags, axis=1, keepdims=True), axis=0, keepdims=True)
     over_ref[...] = jnp.broadcast_to(flag, (8, 128)).astype(jnp.int32)
 
-    def one(tile, carry):
-        values = full_ref[:, lane_offset(tile, 256)]
-        ids = jnp.concatenate([ids_ref[pl.ds(2 * tile, 1), :], ids_ref[pl.ds(2 * tile + 1, 1), :]], axis=1)
+    for tile in range(LANE_TILES // 2):
+        lanes = slice(tile * 256, (tile + 1) * 256)
+        ids = jnp.concatenate([ids_ref[2 * tile : 2 * tile + 1, :], ids_ref[2 * tile + 1 : 2 * tile + 2, :]], axis=1)
+        code = ids.astype(jnp.int32) - 1
+        part = mm(enc_ref[...], full_ref[0:256, lanes])
         total = jnp.zeros((BLOCK, 256), F32)
-        for group in range(LOCAL // 4):
-            part = mm(enc_ref[group * 256 : (group + 1) * 256, :], values)
-            for b in range(4):
-                total = jnp.where(ids == float(group * 4 + b + 1), part[b * BLOCK : (b + 1) * BLOCK], total)
+        for b in range(LOCAL):
+            total = jnp.where(code == b, part[b * BLOCK : (b + 1) * BLOCK], total)
+        rest = full_ref[256:, lanes]
+        member = jnp.broadcast_to(jnp.bitwise_and(code, 7), (32, 256))
+        spread = [jnp.where(member == m, rest, BF16(0)) for m in range(8)]
+        part = mm(rest_ref[...], jnp.concatenate(spread, axis=0))
+        group = lax.shift_right_arithmetic(code, 3)
+        more = jnp.zeros((BLOCK, 256), F32)
+        for g in range(4):
+            more = jnp.where(group == g, part[g * BLOCK : (g + 1) * BLOCK], more)
+        total = total + more
         for half in range(2):
             lane_tile = 2 * tile + half
+            slot_row = (lane_tile % CHUNK_TILES) * 16
             for quarter in range(4):
                 piece = total[quarter * 16 : (quarter + 1) * 16, half * 128 : (half + 1) * 128]
-                out_ref[
-                    quarter + 4 * (lane_tile // CHUNK_TILES),
-                    pl.ds(pl.multiple_of((lane_tile % CHUNK_TILES) * 16, 16), 16),
-                    :,
-                ] = piece.astype(BF16)
-        return carry
-
-    lax.fori_loop(0, LANE_TILES // 2, one, 0)
+                out_ref[quarter + 4 * (lane_tile // CHUNK_TILES), slot_row : slot_row + 16, :] = piece.astype(BF16)
 
 
 def load_codes(codes_ref, full_ref):
@@ -192,25 +207,37 @@
     load_codes(codes_ref, full_ref)
 
     def contribution(tile):
-        codes = full_ref[:, lane_offset(tile, 256)]
-        ids = jnp.concatenate([ids_ref[pl.ds(2 * tile, 1), :], ids_ref[pl.ds(2 * tile + 1, 1), :]], axis=1)
+        spread = spread_ref.at[tile % 2]
+        codes = full_ref[:, tile * 256 : (tile + 1) * 256]
+        ids = jnp.concatenate([ids_ref[2 * tile : 2 * tile + 1, :], ids_ref[2 * tile + 1 : 2 * tile + 2, :]], axis=1)
         ids = jnp.broadcast_to(ids, (BLOCK, 256)).astype(BF16)
         for b in range(LOCAL):
-            spread_ref[b * BLOCK : (b + 1) * BLOCK, :] = jnp.where(ids == BF16(b + 1), codes, BF16(0))
-        return mm(dec_ref[...], spread_ref[...])
-
-    def one(tile, carry):
-        values = contribution(tile)
-        store_pair(send_ref, 2 * tile, values[:, :128])
-        store_pair(send_ref, 2 * tile + 1, values[:, 128:])
-        return carry
-
-    lax.fori_loop(0, PAIRS // 2, one, 0)
+            spread[b * BLOCK : (b + 1) * BLOCK, :] = jnp.where(ids == BF16(b + 1), codes, BF16(0))
+        return mm(dec_ref[...], spread[...])
+
     extra_ref[FEATURES:, :] = jnp.zeros((384 - FEATURES, EXTRA_SLOTS), BF16)
     for tile in range(PAIRS // 2, LANE_TILES // 2):
         start = tile * 256 - MAIN_SLOTS
         extra_ref[0:FEATURES, start : start + 256] = contribution(tile).astype(BF16)
     store_extra(send_ref, mm_nt(identity(EXTRA_SLOTS), extra_ref[...]))
+    for tile in range(PAIRS // 2):
+        values = contribution(tile)
+        store_pair(send_ref, 2 * tile, values[:, :128])
+        store_pair(send_ref, 2 * tile + 1, values[:, 128:])
+
+
+def spread_kernel(codes_ref, ids_ref, spread_ref):
+    for tile in range(LANE_TILES):
+        pieces = []
+        for quarter in range(4):
+            row = (tile % CHUNK_TILES) * 16
+            pieces.append(codes_ref[quarter + 4 * (tile // CHUNK_TILES), row : row + 16, :])
+        codes = jnp.concatenate(pieces, axis=0)
+        ids = jnp.broadcast_to(ids_ref[tile : tile + 1, :], (BLOCK, 128)).astype(BF16)
+        for b in range(LOCAL):
+            spread_ref[b * BLOCK : (b + 1) * BLOCK, tile * 128 : (tile + 1) * 128] = jnp.where(
+                ids == BF16(b + 1), codes, BF16(0)
+            )
 
 
 def combine_kernel(recv_ref, place_ref, act_ref, bias_ref, send_ref, loss_ref, full_ref):
@@ -219,34 +246,19 @@
     loss_ref[...] = jnp.broadcast_to(jnp.sum(error * error, axis=0, keepdims=True), (8, ROWS))
     sent = error.astype(BF16)
 
-    def one(pair, carry):
-        place = place_ref[pl.ds(pl.multiple_of(pair * 128, 128), 128), :]
-        store_pair(send_ref, pair, mm_nt(sent, place))
-        return carry
-
-    lax.fori_loop(0, PAIRS, one, 0, unroll=2)
+    for double in range(PAIRS // 2):
+        values = mm_nt(sent, place_ref[double * 256 : (double + 1) * 256, :])
+        store_pair(send_ref, 2 * double, values[:, :128])
+        store_pair(send_ref, 2 * double + 1, values[:, 128:])
     padded = jnp.concatenate([sent, jnp.zeros((96, ROWS), BF16)], axis=0)
     store_extra(send_ref, mm_nt(place_ref[MAIN_SLOTS:, :], padded))
 
 
-def gradient_kernel(recv_ref, codes_ref, ids_ref, grad_ref, full_ref, code_ref, spread_ref):
+def gradient_kernel(recv_ref, spread_ref, grad_ref, full_ref):
     unpack(recv_ref, full_ref)
-    load_codes(codes_ref, code_ref)
-
-    def one(group, carry):
-        for b in range(4):
-            wanted = (group * 4 + b + 1).astype(F32)
-            for tile in range(LANE_TILES):
-                ids = jnp.broadcast_to(ids_ref[tile : tile + 1, :], (BLOCK, 128)).astype(BF16)
-                codes = code_ref[:, tile * 128 : (tile + 1) * 128]
-                mask = ids == wanted.astype(BF16)
-                spread_ref[b * BLOCK : (b + 1) * BLOCK, tile * 128 : (tile + 1) * 128] = jnp.where(
-                    mask, codes, BF16(0)
-                )
-        grad_ref[:, lane_offset(group, 256)] = mm_nt(full_ref[...], spread_ref[...]).astype(BF16)
-        return carry
-
-    lax.fori_loop(0, LOCAL // 4, one, 0)
+    for start in range(0, LOCAL * BLOCK, 256):
+        part = mm_nt(full_ref[...], spread_ref[start : start + 256, :])
+        grad_ref[:, start : start + 256] = part.astype(BF16)
 
 
 def call(kernel, out_shape, scratch, flops, name):
@@ -277,9 +289,7 @@
 
 
 def sum_loss(part):
-    copies = jnp.broadcast_to(part.reshape(1, 4, 128), (SHARDS, 4, 128))
-    received = lax.all_to_all(copies, "dp", split_axis=0, concat_axis=0, tiled=True)
-    return jnp.sum(received, axis=0).reshape(ROWS)
+    return lax.psum(part, "dp")
 
 
 def padded_plan(activations, bias_dec, encoder, decoder, active_blocks):
@@ -329,22 +339,25 @@
     bias = bias_dec.astype(F32).reshape(FEATURES, 1)
     packed = shape((GROUPS, PACKED, 128))
     full = pltpu.VMEM((FEATURES, SLOTS), BF16)
-    spread = pltpu.VMEM((LOCAL * BLOCK, 256), BF16)
-    sent, place = call(
+    spread = pltpu.VMEM((2, LOCAL * BLOCK, 256), BF16)
+    sent, slots = call(
         prepare_kernel,
-        (packed, shape((SLOTS, ROWS))),
-        [pltpu.VMEM((EXTRA_SLOTS, 128), F32)],
+        (packed, shape((8, ROWS), jnp.int32)),
+        [],
         2 * FEATURES * SLOTS * ROWS,
         "prepare",
     )(act, bias, active_blocks.T)
     received = route(sent)
+    place = call(place_kernel, shape((SLOTS, ROWS)), [], 0, "place")(slots)
+    turned = encoder.T
+    rest = turned[:, 256:].reshape(4, 8, BLOCK, 32).transpose(0, 2, 1, 3).reshape(4 * BLOCK, 256)
     partial, ids, over = call(
         encode_kernel,
         (shape((SHARDS, CHUNK_ROWS, 128)), shape((24, 128), F32), shape((8, 128), jnp.int32)),
         [full],
         2 * FEATURES * SLOTS * LOCAL * BLOCK,
         "encode",
-    )(received, encoder.T)
+    )(received, turned[:, :256], rest)
     codes = sum_codes(partial)
     sent = call(
         decode_kernel,
@@ -367,15 +380,16 @@
     )(received, place, act, bias)
     received = route(sent)
     row_loss = sum_loss(loss[0])
+    spread = call(spread_kernel, shape((LOCAL * BLOCK, SLOTS)), [], 0, "spread")(codes, ids)
 
     def packed_plan():
         gradient = call(
             gradient_kernel,
             shape((FEATURES, LOCAL * BLOCK)),
-            [full, pltpu.VMEM((BLOCK, SLOTS), BF16), pltpu.VMEM((4 * BLOCK, SLOTS), BF16)],
+            [full],
             2 * FEATURES * SLOTS * LOCAL * BLOCK,
             "gradient",
-        )(received, codes, ids)
+        )(received, spread)
         return gradient.T, row_loss
 
     return lax.cond(

time: 204 us -> 191 us (0.936)
  the two profiles are of different devices: /device:TPU:1 before, /device:TPU:2 now
where the time goes in v2:
time: 191 us
  blocking collectives  92.4 us (48%)
  waiting for transfers between devices  33 us (17%)
  Pallas kernels  31.9 us (17%)
  starting transfers between devices  22.1 us (12%)
  local copies, waits for them, and re-layouts  9.74 us (5%)
    all_to_all x1, blocking collectives, sum_codes(): lax.all_to_all(partial, 'dp', split_axis=0, concat_axis=0, tiled=True)  34.5 us
    all_to_all x3, waiting for transfers between devices, route(): lax.all_to_all(buffer, PLANE, split_axis=0, concat_axis=0, tiled=True)  33 us
    psum x1, blocking collectives, sum_loss(): return lax.psum(part, 'dp')  31.1 us
    all_to_all x1, blocking collectives, sum_codes(): return lax.all_to_all(copies, 'dp', split_axis=0, concat_axis=0, tiled=True)  26.8 us
    all_to_all x3, starting transfers between devices, route(): lax.all_to_all(buffer, PLANE, split_axis=0, concat_axis=0, tiled=True)  22.1 us
    pallas_call x1, Pallas kernels, packed_plan(): call(gradient_kernel, shape((FEATURES, LOCAL * BLOCK)), [full], 2 * FEATU...  8.37 us
    pallas_call x1, Pallas kernels, on_device(): call(spread_kernel, shape((LOCAL * BLOCK, SLOTS)), [], 0, 'spread')  5.34 us
    pallas_call x1, Pallas kernels, on_device(): call(decode_kernel, packed, [pltpu.VMEM((BLOCK, SLOTS), BF16), spread, pl...  4.88 us
  transfers between devices with their start and end apart: 3, of which 2 were waited for; matrix products, arithmetic and copies ran while one was open for 3% of the time, Pallas kernels for 4%

profile of v2, /device:TPU:2, one launch (start us, length us, event | category | flops | bytes accessed | tf_op | source)
XLA Modules:
  0.0 190.6 jit_solution(12069314333441734534)
XLA Ops:
  0.6 0.8 reshape.62.bias_ref
  1.4 4.6 %prepare.1 = (bf16[32,192,128]{2,1,0:T(8,128)(2,1)}, s32[8,512]{1,0:T(8,128)S(1)}) custom-call(bf16[288,512]{1,0:T(8,128)(2,1)} %bitcast.43, f32[288,1]{1,0:T(8,128)S(1)} %reshape.62.bias_ref, s32[4,512]{1,0:T(4,128)} %bitcast.41), custom_call_target="tpu_custom_call" | custom-call | flops 754974720 | bytes 6000000 | tf_op jit(solution)/shard_map/prepare/pallas_call | solution.py:343
  6.1 9.5 %all-to-all-start.3 = ((bf16[32,192,128]{2,1,0:T(8,128)(2,1)}), bf16[32,192,128]{2,1,0:T(8,128)(2,1)S(1)}, u32[]{:S(2)}, u32[]{:S(2)}) async-start(bf16[32,192,128]{2,1,0:T(8,128)(2,1)} %get-tuple-element.33), calls=%async_computation.3 | async-start | bytes 3145728 | tf_op jit(solution)/shard_map/all_to_all | solution.py:280
  15.6 1.8 copy.69
  17.4 0.0 copy-start.3
  17.4 1.1 copy-done.3
  18.6 0.8 slice.33
  19.4 1.3 slice.32.enc_ref
  20.7 1.3 copy.70
  22.0 0.2 reshape.55
  22.2 0.1 copy.71.rest_ref
  22.3 13.9 %all-to-all-done.3.recv_ref = bf16[32,192,128]{2,1,0:T(8,128)(2,1)S(1)} async-done(((bf16[32,192,128]{2,1,0:T(8,128)(2,1)}), bf16[32,192,128]{2,1,0:T(8,128)(2,1)S(1)}, u32[]{:S(2)}, u32[]{:S(2)}) %all-to-all-start.3) | async-done | bytes 1572896 | tf_op jit(solution)/shard_map/all_to_all | solution.py:280
  36.2 3.8 %encode.1 = (bf16[16,80,128]{2,1,0:T(8,128)(2,1)S(1)}, f32[24,128]{1,0:T(8,128)S(1)}, s32[8,128]{1,0:T(8,128)S(1)}) custom-call(bf16[32,192,128]{2,1,0:T(8,128)(2,1)S(1)} %all-to-all-done.3.recv_ref, bf16[2048,256]{1,0:T(8,128)(2,1)S(1)} %slice.32.enc_ref, bf16[256,256]{1,0:T(8,128)(2,1)S(1)} %copy.71.rest_ref), custom_call_target="tpu_custom_call" | custom-call | flops 3019898880 | bytes 6000000 | tf_op jit(solution)/shard_map/encode/pallas_call | solution.py:354
  40.0 34.5 %all_to_all.38 = bf16[16,80,128]{2,1,0:T(8,128)(2,1)S(1)} all-to-all(bf16[16,80,128]{2,1,0:T(8,128)(2,1)S(1)} %get-tuple-element.35), channel_id=1, replica_groups=mesh['dp'=16,'latent'=8,'section'=4] {'dp'}, dimensions={0} | all-to-all | bytes 655360 | tf_op jit(solution)/shard_map/all_to_all | solution.py:284
  74.5 0.1 convert_reduce_fusion.1
  74.6 26.8 %all_to_all.39.codes_ref = bf16[16,80,128]{2,1,0:T(8,128)(2,1)S(1)} all-to-all(bf16[16,80,128]{2,1,0:T(8,128)(2,1)S(1)} %broadcast_in_dim.2), channel_id=1, replica_groups=mesh['dp'=16,'latent'=8,'section'=4] {'dp'}, dimensions={0} | all-to-all | bytes 655360 | tf_op jit(solution)/shard_map/all_to_all | solution.py:288
  101.4 4.9 %decode.1 = bf16[32,192,128]{2,1,0:T(8,128)(2,1)} custom-call(bf16[16,80,128]{2,1,0:T(8,128)(2,1)S(1)} %all_to_all.39.codes_ref, f32[24,128]{1,0:T(8,128)S(1)} %get-tuple-element.36.ids_ref, bf16[288,2048]{1,0:T(8,128)(2,1)S(1)} %bitcast.39), custom_call_target="tpu_custom_call" | custom-call | flops 3019898880 | bytes 6000000 | tf_op jit(solution)/shard_map/decode/pallas_call | solution.py:362
  106.3 6.2 %all-to-all-start.6 = ((bf16[32,192,128]{2,1,0:T(8,128)(2,1)}), bf16[32,192,128]{2,1,0:T(8,128)(2,1)}, u32[]{:S(2)}, u32[]{:S(2)}) async-start(bf16[32,192,128]{2,1,0:T(8,128)(2,1)} %decode.1), calls=%async_computation.6 | async-start | bytes 3145728 | tf_op jit(solution)/shard_map/all_to_all | solution.py:280
  112.5 1.5 place.1.place_ref
  114.0 19.1 %all-to-all-done.6.recv_ref = bf16[32,192,128]{2,1,0:T(8,128)(2,1)} async-done(((bf16[32,192,128]{2,1,0:T(8,128)(2,1)}), bf16[32,192,128]{2,1,0:T(8,128)(2,1)}, u32[]{:S(2)}, u32[]{:S(2)}) %all-to-all-start.6) | async-done | bytes 1572896 | tf_op jit(solution)/shard_map/all_to_all | solution.py:280
  133.0 3.4 %combine.1 = (bf16[32,192,128]{2,1,0:T(8,128)(2,1)S(1)}, f32[8,512]{1,0:T(8,128)S(1)}) custom-call(bf16[32,192,128]{2,1,0:T(8,128)(2,1)} %all-to-all-done.6.recv_ref, bf16[2560,512]{1,0:T(8,128)(2,1)S(1)} %place.1.place_ref, bf16[288,512]{1,0:T(8,128)(2,1)S(1)} %bitcast.44, f32[288,1]{1,0:T(8,128)S(1)} %reshape.62.bias_ref), custom_call_target="tpu_custom_call" | custom-call | flops 1509949440 | bytes 6000000 | tf_op jit(solution)/shard_map/combine/pallas_call | solution.py:374
  136.5 1.1 copy-done
  137.6 6.4 %all-to-all-start.7 = ((bf16[32,192,128]{2,1,0:T(8,128)(2,1)}), bf16[32,192,128]{2,1,0:T(8,128)(2,1)S(1)}, u32[]{:S(2)}, u32[]{:S(2)}) async-start(bf16[32,192,128]{2,1,0:T(8,128)(2,1)} %copy-done), calls=%async_computation.7 | async-start | bytes 3145728 | tf_op jit(solution)/shard_map/all_to_all | solution.py:280
  144.0 0.5 slice.26
  145.2 0.0 copy-start.5
  145.2 0.0 copy-start.6
  145.2 5.3 %spread.1 = bf16[2048,2560]{1,0:T(8,128)(2,1)} custom-call(bf16[16,80,128]{2,1,0:T(8,128)(2,1)S(1)} %all_to_all.39.codes_ref, f32[24,128]{1,0:T(8,128)S(1)} %get-tuple-element.36.ids_ref), custom_call_target="tpu_custom_call" | custom-call | bytes 6000000 | tf_op jit(solution)/shard_map/spread/pallas_call | solution.py:383
  150.6 31.1 %psum.21 = f32[512]{0:T(512)S(1)} all-reduce(f32[512]{0:T(512)S(1)} %bitcast.42), channel_id=1, replica_groups=mesh['dp'=16,'latent'=8,'section'=4] {'dp'}, use_global_device_ids=true, to_apply=%region_1.0 | all-reduce | flops 512 | bytes 4096 | tf_op jit(solution)/shard_map/psum | solution.py:292
  181.7 0.0 all-to-all-done.7
  181.7 8.4 %conditional.1 = (f32[512]{0:T(512)S(1)}, bf16[2048,288]{0,1:T(8,128)(2,1)}) conditional(s32[]{:T(128)} %bitcast.17, (bf16[32,192,128]{2,1,0:T(8,128)(2,1)S(1)}, bf16[2048,2560]{1,0:T(8,128)(2,1)}, f32[512]{0:T(512)S(1)}) %tuple.15, (s32[512,4]{0,1:T(4,128)S(1)}, bf16[512,288]{0,1:T(8,128)(2,1)S(1)}, bf16[288]{0:T(512)(128)(2,1)S(1)}, ...), branch_computations={%region_2.0_spmd, %region_3.0_spmd} | conditional | flops 4205791488 | bytes 86911048 | solution.py:395
  181.7 8.4 %gradient.1 = bf16[288,2048]{1,0:T(8,128)(2,1)} custom-call(bf16[32,192,128]{2,1,0:T(8,128)(2,1)S(1)} %get-tuple-element.16.recv_ref, bf16[2048,2560]{1,0:T(8,128)(2,1)} %get-tuple-element.17.spread_ref), custom_call_target="tpu_custom_call" | custom-call | flops 3019898880 | bytes 6000000 | tf_op jit(solution)/shard_map/cond/branch_0_fun/gradient/pallas_call | solution.py:386
  190.1 0.6 copy-done.7
  (11 shorter events, 0.1 us)
Async XLA Ops:
  6.1 30.2 %all-to-all-start.3 = ((bf16[32,192,128]{2,1,0:T(8,128)(2,1)}), bf16[32,192,128]{2,1,0:T(8,128)(2,1)S(1)}, u32[]{:S(2)}, u32[]{:S(2)}) async-start(bf16[32,192,128]{2,1,0:T(8,128)(2,1)} %get-tuple-element.33), calls=%async_computation.3 | async-start | bytes 3145728 | tf_op jit(solution)/shard_map/all_to_all | solution.py:280
  17.4 1.1 copy-start.3
  36.2 65.2 %copy-start.4 = (bf16[2048,288]{0,1:T(8,128)(2,1)S(1)}, bf16[2048,288]{0,1:T(8,128)(2,1)}, u32[]{:S(2)}) copy-start(bf16[2048,288]{0,1:T(8,128)(2,1)} %param.10) | copy-start | bytes 3538948
  106.3 26.7 %copy-start.8 = (bf16[512,288]{0,1:T(8,128)(2,1)S(1)}, bf16[512,288]{0,1:T(8,128)(2,1)}, u32[]{:S(2)}) copy-start(bf16[512,288]{0,1:T(8,128)(2,1)} %param.7) | copy-start | bytes 884740
  106.3 26.7 %all-to-all-start.6 = ((bf16[32,192,128]{2,1,0:T(8,128)(2,1)}), bf16[32,192,128]{2,1,0:T(8,128)(2,1)}, u32[]{:S(2)}, u32[]{:S(2)}) async-start(bf16[32,192,128]{2,1,0:T(8,128)(2,1)} %decode.1), calls=%async_computation.6 | async-start | bytes 3145728 | tf_op jit(solution)/shard_map/all_to_all | solution.py:280
  136.5 1.1 copy-start
  137.6 44.1 %all-to-all-start.7 = ((bf16[32,192,128]{2,1,0:T(8,128)(2,1)}), bf16[32,192,128]{2,1,0:T(8,128)(2,1)S(1)}, u32[]{:S(2)}, u32[]{:S(2)}) async-start(bf16[32,192,128]{2,1,0:T(8,128)(2,1)} %copy-done), calls=%async_computation.7 | async-start | bytes 3145728 | tf_op jit(solution)/shard_map/all_to_all | solution.py:280
  145.2 36.5 %copy-start.5 = (s32[512,4]{0,1:T(4,128)S(1)}, s32[512,4]{0,1:T(4,128)}, u32[]{:S(2)}) copy-start(s32[512,4]{0,1:T(4,128)} %param.11) | copy-start | bytes 24580
  145.2 36.5 %copy-start.6 = (bf16[288]{0:T(512)(128)(2,1)S(1)}, bf16[288]{0:T(512)(128)(2,1)}, u32[]{:S(2)}) copy-start(bf16[288]{0:T(512)(128)(2,1)} %param.8) | copy-start | bytes 1732
  190.1 0.6 copy-start.7

commit v3 on v2

--- a/solution.py
+++ b/solution.py
@@ -7,6 +7,8 @@
 
 BLOCK = 64
 PLANE = ("latent", "section")
+OUTER, INNER = "dp_outer", "dp_inner"
+DP = (OUTER, INNER)
 GROUPS = 32
 SHARDS = 16
 LOCAL = 32
@@ -21,6 +23,7 @@
 SLOTS = MAIN_SLOTS + EXTRA_SLOTS
 PACKED = HALF + 3 * EXTRA
 PAIRS = GROUPS // 2
+EARLY = 12
 LANE_TILES = SLOTS // 128
 CHUNK_TILES = 5
 CHUNK_ROWS = 16 * CHUNK_TILES
@@ -54,6 +57,36 @@
     second = jnp.where(low, pltpu.roll(top, MAIN, 1), bottom)
     out_ref[pair, 0:HALF, :] = first.astype(BF16)
     out_ref[pair + PAIRS, 0:HALF, :] = second.astype(BF16)
+
+
+def stage_copies(buffer_ref, out_ref, sems, stage):
+    first, count = (0, EARLY) if stage == 0 else (EARLY, PAIRS - EARLY)
+    copies = []
+    for side in range(2):
+        devices = pl.ds(side * PAIRS + first, count)
+        copies.append(
+            pltpu.make_async_copy(buffer_ref.at[devices], out_ref.at[devices], sems.at[2 * stage + side])
+        )
+    return copies
+
+
+def start_stage(buffer_ref, out_ref, sems, done):
+    if done in (EARLY, PAIRS):
+        for copy in stage_copies(buffer_ref, out_ref, sems, 0 if done == EARLY else 1):
+            copy.start()
+
+
+def wait_stages(buffer_ref, out_ref, sems):
+    for stage in range(2):
+        for copy in stage_copies(buffer_ref, out_ref, sems, stage):
+            copy.wait()
+
+
+def bias_column(bias_ref):
+    rows = lax.broadcasted_iota(jnp.int32, (FEATURES, FEATURES), 0)
+    lanes = lax.broadcasted_iota(jnp.int32, (FEATURES, FEATURES), 1)
+    wide = jnp.broadcast_to(bias_ref[...].astype(F32).reshape(1, FEATURES), (FEATURES, FEATURES))
+    return jnp.sum(jnp.where(rows == lanes, wide, 0.0), axis=1, keepdims=True)
 
 
 def store_extra(out_ref, values):
@@ -92,7 +125,7 @@
     return named, jnp.minimum(named, BF16(1))
 
 
-def prepare_kernel(act_ref, bias_ref, blocks_ref, send_ref, slots_ref):
+def prepare_kernel(act_ref, bias_ref, blocks_ref, out_ref, slots_ref, send_ref, sems):
     blocks = blocks_ref[...]
     target = lax.shift_right_logical(blocks, 5)
     local = jnp.bitwise_and(blocks, LOCAL - 1)
@@ -113,7 +146,7 @@
         names.append((local[k : k + 1, :] + 1).astype(F32))
         most = jnp.maximum(most, rank)
     over = jnp.where(jnp.max(most, axis=1, keepdims=True) >= MAIN + EXTRA, 1.0, 0.0)
-    shifted = (act_ref[...].astype(F32) - bias_ref[...]).astype(BF16)
+    shifted = (act_ref[...].astype(F32) - bias_column(bias_ref)).astype(BF16)
 
     for k in range(NAMED):
         slots_ref[k : k + 1, :] = slots[k]
@@ -143,6 +176,8 @@
                 tile = jnp.where(high & (row == 0), mine, tile)
                 tile = jnp.where(high & (row == 1), flag, tile)
                 send_ref[device, HALF + 2 * EXTRA :, :] = tile.astype(BF16)
+        start_stage(send_ref, out_ref, sems, 2 * double + 2)
+    wait_stages(send_ref, out_ref, sems)
 
 
 def place_kernel(slots_ref, place_ref):
@@ -203,17 +238,15 @@
             ]
 
 
-def decode_kernel(codes_ref, ids_ref, dec_ref, send_ref, full_ref, spread_ref, extra_ref):
+def decode_kernel(codes_ref, ids_ref, dec_ref, out_ref, full_ref, extra_ref, send_ref, sems):
     load_codes(codes_ref, full_ref)
 
     def contribution(tile):
-        spread = spread_ref.at[tile % 2]
         codes = full_ref[:, tile * 256 : (tile + 1) * 256]
         ids = jnp.concatenate([ids_ref[2 * tile : 2 * tile + 1, :], ids_ref[2 * tile + 1 : 2 * tile + 2, :]], axis=1)
         ids = jnp.broadcast_to(ids, (BLOCK, 256)).astype(BF16)
-        for b in range(LOCAL):
-            spread[b * BLOCK : (b + 1) * BLOCK, :] = jnp.where(ids == BF16(b + 1), codes, BF16(0))
-        return mm(dec_ref[...], spread[...])
+        spread = [jnp.where(ids == BF16(b + 1), codes, BF16(0)) for b in range(LOCAL)]
+        return mm(dec_ref[...], jnp.concatenate(spread, axis=0))
 
     extra_ref[FEATURES:, :] = jnp.zeros((384 - FEATURES, EXTRA_SLOTS), BF16)
     for tile in range(PAIRS // 2, LANE_TILES // 2):
@@ -224,50 +257,60 @@
         values = contribution(tile)
         store_pair(send_ref, 2 * tile, values[:, :128])
         store_pair(send_ref, 2 * tile + 1, values[:, 128:])
-
-
-def spread_kernel(codes_ref, ids_ref, spread_ref):
-    for tile in range(LANE_TILES):
-        pieces = []
-        for quarter in range(4):
-            row = (tile % CHUNK_TILES) * 16
-            pieces.append(codes_ref[quarter + 4 * (tile // CHUNK_TILES), row : row + 16, :])
-        codes = jnp.concatenate(pieces, axis=0)
-        ids = jnp.broadcast_to(ids_ref[tile : tile + 1, :], (BLOCK, 128)).astype(BF16)
-        for b in range(LOCAL):
-            spread_ref[b * BLOCK : (b + 1) * BLOCK, tile * 128 : (tile + 1) * 128] = jnp.where(
-                ids == BF16(b + 1), codes, BF16(0)
-            )
-
-
-def combine_kernel(recv_ref, place_ref, act_ref, bias_ref, send_ref, loss_ref, full_ref):
+        start_stage(send_ref, out_ref, sems, 2 * tile + 2)
+    wait_stages(send_ref, out_ref, sems)
+
+
+def combine_kernel(recv_ref, place_ref, act_ref, bias_ref, out_ref, loss_ref, full_ref, send_ref, sems):
     unpack(recv_ref, full_ref)
-    error = mm(full_ref[...], place_ref[...]) + bias_ref[...] - act_ref[...].astype(F32)
-    loss_ref[...] = jnp.broadcast_to(jnp.sum(error * error, axis=0, keepdims=True), (8, ROWS))
+    error = mm(full_ref[...], place_ref[...]) + bias_column(bias_ref) - act_ref[...].astype(F32)
     sent = error.astype(BF16)
-
+    padded = jnp.concatenate([sent, jnp.zeros((96, ROWS), BF16)], axis=0)
+    store_extra(send_ref, mm_nt(place_ref[MAIN_SLOTS:, :], padded))
     for double in range(PAIRS // 2):
         values = mm_nt(sent, place_ref[double * 256 : (double + 1) * 256, :])
         store_pair(send_ref, 2 * double, values[:, :128])
         store_pair(send_ref, 2 * double + 1, values[:, 128:])
-    padded = jnp.concatenate([sent, jnp.zeros((96, ROWS), BF16)], axis=0)
-    store_extra(send_ref, mm_nt(place_ref[MAIN_SLOTS:, :], padded))
-
-
-def gradient_kernel(recv_ref, spread_ref, grad_ref, full_ref):
+        start_stage(send_ref, out_ref, sems, 2 * double + 2)
+    loss = jnp.sum(error * error, axis=0, keepdims=True)
+    for part in range(ROWS // 128):
+        loss_ref[part : part + 1, :] = loss[:, part * 128 : (part + 1) * 128]
+    wait_stages(send_ref, out_ref, sems)
+
+
+def gradient_kernel(
+    recv_ref, codes_ref, ids_ref, loss_ref, out_ref, out_loss_ref, full_ref, code_ref, grad_ref, sems
+):
+    out_loss_ref[...] = loss_ref[...]
     unpack(recv_ref, full_ref)
+    load_codes(codes_ref, code_ref)
+    ids = jnp.concatenate([ids_ref[tile : tile + 1, :] for tile in range(LANE_TILES)], axis=1)
+    ids = jnp.broadcast_to(ids, (BLOCK, SLOTS)).astype(BF16)
+    copies, begin = [], 0
     for start in range(0, LOCAL * BLOCK, 256):
-        part = mm_nt(full_ref[...], spread_ref[start : start + 256, :])
-        grad_ref[:, start : start + 256] = part.astype(BF16)
-
-
-def call(kernel, out_shape, scratch, flops, name):
+        stop = start + 256
+        spread = [
+            jnp.where(ids == BF16(b + 1), code_ref[...], BF16(0)) for b in range(start // BLOCK, stop // BLOCK)
+        ]
+        grad_ref[:, start:stop] = mm_nt(full_ref[...], jnp.concatenate(spread, axis=0)).astype(BF16)
+        if stop in (LOCAL * BLOCK * 3 // 4, LOCAL * BLOCK):
+            lanes = pl.ds(begin, stop - begin)
+            copy = pltpu.make_async_copy(grad_ref.at[:, lanes], out_ref.at[:, lanes], sems.at[len(copies)])
+            copy.start()
+            copies.append(copy)
+            begin = stop
+    for copy in copies:
+        copy.wait()
+
+
+def call(kernel, out_shape, scratch, flops, name, megabytes, **specs):
     return pl.pallas_call(
         kernel,
         out_shape=out_shape,
         scratch_shapes=scratch,
         name=name,
-        compiler_params=pltpu.CompilerParams(vmem_limit_bytes=40 * 1024 * 1024),
+        **specs,
+        compiler_params=pltpu.CompilerParams(vmem_limit_bytes=megabytes * 1024 * 1024),
         cost_estimate=pl.CostEstimate(flops=flops, bytes_accessed=6_000_000, transcendentals=0),
     )
 
@@ -276,20 +319,24 @@
     return jax.ShapeDtypeStruct(dims, dtype)
 
 
+def in_hbm(dims, dtype=BF16):
+    return pltpu.HBM(dims, dtype)
+
+
 def route(buffer):
     return lax.all_to_all(buffer, PLANE, split_axis=0, concat_axis=0, tiled=True)
 
 
 def sum_codes(partial):
-    received = lax.all_to_all(partial, "dp", split_axis=0, concat_axis=0, tiled=True)
+    received = lax.all_to_all(partial, DP, split_axis=0, concat_axis=0, tiled=True)
     total = jnp.sum(received.astype(F32), axis=0)
     codes = jnp.maximum(total, 0.0).astype(BF16)
     copies = jnp.broadcast_to(codes[None], (SHARDS,) + codes.shape)
-    return lax.all_to_all(copies, "dp", split_axis=0, concat_axis=0, tiled=True)
+    return lax.all_to_all(copies, DP, split_axis=0, concat_axis=0, tiled=True)
 
 
 def sum_loss(part):
-    return lax.psum(part, "dp")
+    return lax.psum(lax.psum(part, INNER), OUTER)
 
 
 def padded_plan(activations, bias_dec, encoder, decoder, active_blocks):
@@ -321,14 +368,14 @@
     received = route(scatter_rows(shifted))
     enc_local = encoder.reshape(shard_width, local_blocks, BLOCK)
     partial_pre = jnp.einsum("sbkd,dbl->sbkl", received, enc_local, preferred_element_type=F32)
-    pre_total = lax.psum(partial_pre, "dp")
+    pre_total = lax.psum(partial_pre, DP)
     latent_codes = jnp.maximum(pre_total, 0.0).astype(BF16)
     dec_local = decoder.reshape(local_blocks, BLOCK, shard_width)
     contrib = jnp.einsum("sbkl,bld->sbkd", latent_codes, dec_local, preferred_element_type=F32).astype(BF16)
     returned = route(contrib).reshape(slot_count, shard_width)
     summed_rows = jnp.einsum("sr,sd->rd", placement, returned, preferred_element_type=F32)
     error = summed_rows + bias_wide - activations.astype(F32)
-    row_loss = lax.psum(jnp.sum(error * error, axis=1), "dp")
+    row_loss = lax.psum(jnp.sum(error * error, axis=1), DP)
     error_sent = route(scatter_rows(error.astype(BF16)))
     gradient = jnp.einsum("sbkl,sbkd->bld", latent_codes, error_sent, preferred_element_type=F32)
     return gradient.reshape(local_blocks * BLOCK, shard_width).astype(BF16), row_loss
@@ -336,27 +383,32 @@
 
 def on_device(activations, bias_dec, encoder, decoder, active_blocks):
     act = activations.T
-    bias = bias_dec.astype(F32).reshape(FEATURES, 1)
-    packed = shape((GROUPS, PACKED, 128))
+    bias = bias_dec
+    packed = in_hbm((GROUPS, PACKED, 128))
     full = pltpu.VMEM((FEATURES, SLOTS), BF16)
-    spread = pltpu.VMEM((2, LOCAL * BLOCK, 256), BF16)
+    sending = [pltpu.VMEM((GROUPS, PACKED, 128), BF16), pltpu.SemaphoreType.DMA((4,))]
+    vmem, hbm = pl.BlockSpec(memory_space=pltpu.VMEM), pl.BlockSpec(memory_space=pltpu.HBM)
+    spread_flops = 2 * FEATURES * SLOTS * LOCAL * BLOCK
     sent, slots = call(
         prepare_kernel,
         (packed, shape((8, ROWS), jnp.int32)),
-        [],
+        sending,
         2 * FEATURES * SLOTS * ROWS,
         "prepare",
+        20,
+        out_specs=(hbm, vmem),
     )(act, bias, active_blocks.T)
     received = route(sent)
-    place = call(place_kernel, shape((SLOTS, ROWS)), [], 0, "place")(slots)
+    place = call(place_kernel, shape((SLOTS, ROWS)), [], 0, "place", 16)(slots)
     turned = encoder.T
     rest = turned[:, 256:].reshape(4, 8, BLOCK, 32).transpose(0, 2, 1, 3).reshape(4 * BLOCK, 256)
     partial, ids, over = call(
         encode_kernel,
         (shape((SHARDS, CHUNK_ROWS, 128)), shape((24, 128), F32), shape((8, 128), jnp.int32)),
         [full],
-        2 * FEATURES * SLOTS * LOCAL * BLOCK,
+        spread_flops,
         "encode",
+        20,
     )(received, turned[:, :256], rest)
     codes = sum_codes(partial)
     sent = call(
@@ -364,53 +416,66 @@
         packed,
         [
             pltpu.VMEM((BLOCK, SLOTS), BF16),
-            spread,
             pltpu.VMEM((384, EXTRA_SLOTS), BF16),
-        ],
-        2 * FEATURES * SLOTS * LOCAL * BLOCK,
+        ]
+        + sending,
+        spread_flops,
         "decode",
+        20,
+        out_specs=hbm,
     )(codes, ids, decoder.T)
     received = route(sent)
+    heavy = over[0, 0] > 0
+    received, heavy = lax.optimization_barrier((received, heavy))
     sent, loss = call(
         combine_kernel,
-        (packed, shape((8, ROWS), F32)),
-        [full],
+        (packed, shape((ROWS // 128, 128), F32)),
+        [full] + sending,
         4 * FEATURES * SLOTS * ROWS,
         "combine",
+        20,
+        out_specs=(hbm, vmem),
     )(received, place, act, bias)
     received = route(sent)
-    row_loss = sum_loss(loss[0])
-    spread = call(spread_kernel, shape((LOCAL * BLOCK, SLOTS)), [], 0, "spread")(codes, ids)
+    loss = sum_loss(loss)
 
     def packed_plan():
-        gradient = call(
+        gradient, row_loss = call(
             gradient_kernel,
-            shape((FEATURES, LOCAL * BLOCK)),
-            [full],
-            2 * FEATURES * SLOTS * LOCAL * BLOCK,
+            (in_hbm((FEATURES, LOCAL * BLOCK)), in_hbm((ROWS // 128, 128), F32)),
+            [
+                full,
+                pltpu.VMEM((BLOCK, SLOTS), BF16),
+                pltpu.VMEM((FEATURES, LOCAL * BLOCK), BF16),
+                pltpu.SemaphoreType.DMA((2,)),
+            ],
+            spread_flops,
             "gradient",
-        )(received, spread)
-        return gradient.T, row_loss
+            24,
+            out_specs=(hbm, vmem),
+        )(received, codes, ids, loss)
+        return gradient.T, row_loss.reshape(ROWS)
 
     return lax.cond(
-        over[0, 0] > 0,
+        heavy,
         lambda: padded_plan(activations, bias_dec, encoder, decoder, active_blocks),
         packed_plan,
     )
 
 
 def solution(mesh):
+    split = jax.sharding.Mesh(mesh.devices.reshape(4, 4, 8, 4), (OUTER, INNER) + PLANE)
     placed = (
-        P(PLANE, "dp"),
-        P("dp"),
-        P("dp", PLANE),
-        P(PLANE, "dp"),
+        P(PLANE, DP),
+        P(DP),
+        P(DP, PLANE),
+        P(PLANE, DP),
         P(PLANE, None),
     )
     return jax.shard_map(
         on_device,
-        mesh=mesh,
+        mesh=split,
         in_specs=placed,
-        out_specs=(P(PLANE, "dp"), P(PLANE)),
+        out_specs=(P(PLANE, DP), P(PLANE)),
         check_vma=False,
     )

time: 191 us -> 175 us (0.916)
  the two profiles are of different devices: /device:TPU:2 before, /device:TPU:1 now
where the time goes in v3:
time: 175 us; the launch traced here: 172 us
  blocking collectives  77.2 us (44%)
  waiting for transfers between devices  33.5 us (19%)
  starting transfers between devices  28.2 us (16%)
  Pallas kernels  23.9 us (14%)
  local copies, waits for them, and re-layouts  7.25 us (4%)
    all_to_all x3, waiting for transfers between devices, route(): lax.all_to_all(buffer, PLANE, split_axis=0, concat_axis=0, tiled=True)  33.5 us
    all_to_all x3, starting transfers between devices, route(): lax.all_to_all(buffer, PLANE, split_axis=0, concat_axis=0, tiled=True)  28.2 us
    all_to_all x1, blocking collectives, sum_codes(): return lax.all_to_all(copies, DP, split_axis=0, concat_axis=0, tiled=True)  27.5 us
    all_to_all x1, blocking collectives, sum_codes(): lax.all_to_all(partial, DP, split_axis=0, concat_axis=0, tiled=True)  27 us
    psum x2, blocking collectives, sum_loss(): return lax.psum(lax.psum(part, INNER), OUTER)  22.7 us
    pallas_call x1, Pallas kernels, packed_plan(): call(gradient_kernel, (in_hbm((FEATURES, LOCAL * BLOCK)), in_hbm((ROWS //...  4.73 us
    pallas_call x1, Pallas kernels, on_device(): call(combine_kernel, (packed, shape((ROWS // 128, 128), F32)), [full] + s...  4.66 us
    pallas_call x1, Pallas kernels, on_device(): call(decode_kernel, packed, [pltpu.VMEM((BLOCK, SLOTS), BF16), pltpu.VMEM...  4.66 us
  transfers between devices with their start and end apart: 3, of which 2 were waited for; matrix products, arithmetic and copies ran while one was open for 4% of the time, Pallas kernels for 1%

profile of v3, /device:TPU:1, one launch (start us, length us, event | category | flops | bytes accessed | tf_op | source)
XLA Modules:
  0.0 172.0 jit_solution(2784414918906478572)
XLA Ops:
  0.6 4.4 %prepare.1 = (bf16[32,192,128]{2,1,0:T(8,128)(2,1)}, s32[8,512]{1,0:T(8,128)S(1)}) custom-call(bf16[288,512]{1,0:T(8,128)(2,1)} %bitcast.42, bf16[288]{0:T(512)(128)(2,1)} %bias_ref.3, s32[4,512]{1,0:T(4,128)} %bitcast.41), custom_call_target="tpu_custom_call" | custom-call | flops 754974720 | bytes 6000000 | tf_op jit(solution)/shard_map/prepare/pallas_call | solution.py:392
  5.1 10.5 %all-to-all-start.3 = ((bf16[32,192,128]{2,1,0:T(8,128)(2,1)}), bf16[32,192,128]{2,1,0:T(8,128)(2,1)S(1)}, u32[]{:S(2)}, u32[]{:S(2)}) async-start(bf16[32,192,128]{2,1,0:T(8,128)(2,1)} %get-tuple-element.40), calls=%async_computation.3 | async-start | bytes 3145728 | tf_op jit(solution)/shard_map/all_to_all | solution.py:327
  15.6 1.8 %copy.64 = bf16[288,2048]{0,1:T(8,128)(2,1)S(1)} copy(bf16[288,2048]{1,0:T(8,128)(2,1)} %param.9) | data formatting | bytes 2359296 | tf_op args[2]
  17.4 0.0 copy-start.2
  17.4 1.1 copy-done.2
  18.6 0.8 slice.29
  19.4 1.3 slice.28.enc_ref
  20.7 1.3 copy.65
  22.0 0.2 reshape.49
  22.2 0.1 copy.66.rest_ref
  22.3 14.7 %all-to-all-done.3.recv_ref = bf16[32,192,128]{2,1,0:T(8,128)(2,1)S(1)} async-done(((bf16[32,192,128]{2,1,0:T(8,128)(2,1)}), bf16[32,192,128]{2,1,0:T(8,128)(2,1)S(1)}, u32[]{:S(2)}, u32[]{:S(2)}) %all-to-all-start.3) | async-done | bytes 1572896 | tf_op jit(solution)/shard_map/all_to_all | solution.py:327
  37.0 3.9 %encode.1 = (bf16[16,80,128]{2,1,0:T(8,128)(2,1)S(1)}, f32[24,128]{1,0:T(8,128)S(1)}, s32[8,128]{1,0:T(8,128)S(1)}) custom-call(bf16[32,192,128]{2,1,0:T(8,128)(2,1)S(1)} %all-to-all-done.3.recv_ref, bf16[2048,256]{1,0:T(8,128)(2,1)S(1)} %slice.28.enc_ref, bf16[256,256]{1,0:T(8,128)(2,1)S(1)} %copy.66.rest_ref), custom_call_target="tpu_custom_call" | custom-call | flops 3019898880 | bytes 6000000 | tf_op jit(solution)/shard_map/encode/pallas_call | solution.py:405
  41.0 27.0 %all_to_all.38 = bf16[16,80,128]{2,1,0:T(8,128)(2,1)S(1)} all-to-all(bf16[16,80,128]{2,1,0:T(8,128)(2,1)S(1)} %get-tuple-element.41), channel_id=1, replica_groups=mesh['dp_outer'=4,'dp_inner'=4,'latent'=8,'section'=4] {'dp_outer','dp_i..., dimensions={0} | all-to-all | bytes 655360 | tf_op jit(solution)/shard_map/all_to_all | solution.py:331
  67.9 0.1 convert_reduce_fusion.1
  68.1 27.5 %all_to_all.39.codes_ref = bf16[16,80,128]{2,1,0:T(8,128)(2,1)S(1)} all-to-all(bf16[16,80,128]{2,1,0:T(8,128)(2,1)S(1)} %broadcast_in_dim.2), channel_id=1, replica_groups=mesh['dp_outer'=4,'dp_inner'=4,'latent'=8,'section'=4] {'dp_outer','dp_i..., dimensions={0} | all-to-all | bytes 655360 | tf_op jit(solution)/shard_map/all_to_all | solution.py:335
  95.6 0.0 copy-done.3
  95.6 4.7 %decode.1 = bf16[32,192,128]{2,1,0:T(8,128)(2,1)} custom-call(bf16[16,80,128]{2,1,0:T(8,128)(2,1)S(1)} %all_to_all.39.codes_ref, f32[24,128]{1,0:T(8,128)S(1)} %get-tuple-element.42.ids_ref, bf16[288,2048]{1,0:T(8,128)(2,1)S(1)} %bitcast.39), custom_call_target="tpu_custom_call" | custom-call | flops 3019898880 | bytes 6000000 | tf_op jit(solution)/shard_map/decode/pallas_call | solution.py:414
  100.3 0.0 copy-start.5
  100.3 0.0 copy-start.6
  100.3 12.1 %all-to-all-start.6 = ((bf16[32,192,128]{2,1,0:T(8,128)(2,1)}), bf16[32,192,128]{2,1,0:T(8,128)(2,1)}, u32[]{:S(2)}, u32[]{:S(2)}) async-start(bf16[32,192,128]{2,1,0:T(8,128)(2,1)} %decode.1), calls=%async_computation.6 | async-start | bytes 3145728 | tf_op jit(solution)/shard_map/all_to_all | solution.py:327
  112.4 1.5 place.1.place_ref
  113.9 0.5 slice.23
  115.1 18.8 %all-to-all-done.6.recv_ref = bf16[32,192,128]{2,1,0:T(8,128)(2,1)} async-done(((bf16[32,192,128]{2,1,0:T(8,128)(2,1)}), bf16[32,192,128]{2,1,0:T(8,128)(2,1)}, u32[]{:S(2)}, u32[]{:S(2)}) %all-to-all-start.6) | async-done | bytes 1572896 | tf_op jit(solution)/shard_map/all_to_all | solution.py:327
  133.9 0.0 copy-done.5
  133.9 0.0 copy-done.6
  133.9 4.7 %combine.1 = (bf16[32,192,128]{2,1,0:T(8,128)(2,1)}, f32[4,128]{1,0:T(4,128)S(1)}) custom-call(bf16[32,192,128]{2,1,0:T(8,128)(2,1)} %all-to-all-done.6.recv_ref, bf16[2560,512]{1,0:T(8,128)(2,1)S(1)} %place.1.place_ref, bf16[288,512]{1,0:T(8,128)(2,1)S(1)} %bitcast.43, bf16[288]{0:T(512)(128)(2,1)S(1)} %copy-done.5), custom_call_target="tpu_custom_call" | custom-call | flops 1509949440 | bytes 6000000 | tf_op jit(solution)/shard_map/combine/pallas_call | solution.py:430
  138.5 5.5 %all-to-all-start.7 = ((bf16[32,192,128]{2,1,0:T(8,128)(2,1)}), bf16[32,192,128]{2,1,0:T(8,128)(2,1)S(1)}, u32[]{:S(2)}, u32[]{:S(2)}) async-start(bf16[32,192,128]{2,1,0:T(8,128)(2,1)} %get-tuple-element.47), calls=%async_computation.7 | async-start | bytes 3145728 | tf_op jit(solution)/shard_map/all_to_all | solution.py:327
  144.1 10.1 %psum.28 = f32[4,128]{1,0:T(4,128)S(1)} all-reduce(f32[4,128]{1,0:T(4,128)S(1)} %get-tuple-element.48), channel_id=1, replica_groups=mesh['dp_outer'=4,'dp_inner'=4,'latent'=8,'section'=4] {'dp_inner'}, use_global_device_ids=true, to_apply=%region_1.0 | all-reduce | flops 512 | bytes 4096 | tf_op jit(solution)/shard_map/psum | solution.py:339
  154.1 12.6 %psum.29 = f32[4,128]{1,0:T(4,128)S(1)} all-reduce(f32[4,128]{1,0:T(4,128)S(1)} %psum.28), channel_id=1, replica_groups=mesh['dp_outer'=4,'dp_inner'=4,'latent'=8,'section'=4] {'dp_outer'}, use_global_device_ids=true, to_apply=%region_2.0 | all-reduce | flops 512 | bytes 4096 | tf_op jit(solution)/shard_map/psum | solution.py:339
  166.8 0.0 all-to-all-done.7
  166.8 5.0 %conditional.1 = (f32[512]{0:T(512)}, bf16[2048,288]{0,1:T(8,128)(2,1)}) conditional(s32[]{:T(128)} %convert_element_type.64, (bf16[32,192,128]{2,1,0:T(8,128)(2,1)S(1)}, bf16[16,80,128]{2,1,0:T(8,128)(2,1)S(1)}, f32[24,128]{1,0:T(8,128)S(1)}, f32[4,128]{1,0:T(4,128)S(1)}) %tuple.17, (s32[512,4]{0,1:T(4,128)S(1)}, bf16[512,288]{0,1:T(8,128)(2,1)S(1)}, ...), branch_computations={%region_3.0_spmd, %region_4.0_spmd} | conditional | flops 4205791488 | bytes 89270392 | solution.py:459
  166.8 4.7 %gradient.1 = (bf16[288,2048]{1,0:T(8,128)(2,1)}, f32[4,128]{1,0:T(4,128)}) custom-call(bf16[32,192,128]{2,1,0:T(8,128)(2,1)S(1)} %get-tuple-element.18.recv_ref, bf16[16,80,128]{2,1,0:T(8,128)(2,1)S(1)} %get-tuple-element.19.codes_ref, f32[24,128]{1,0:T(8,128)S(1)} %get-tuple-element.20.ids_ref, f32[4,128]{1,0:T(4,128)S(1)} %get-tuple-element.21.loss_ref), custom_call_target="tpu_custom_call" | custom-call | flops 3019898880 | bytes 6000000 | tf_op jit(solution)/shard_map/cond/branch_0_fun/gradient/pallas_call | solution.py:443
  (5 shorter events, 0.1 us)
Async XLA Ops:
  5.1 32.0 %all-to-all-start.3 = ((bf16[32,192,128]{2,1,0:T(8,128)(2,1)}), bf16[32,192,128]{2,1,0:T(8,128)(2,1)S(1)}, u32[]{:S(2)}, u32[]{:S(2)}) async-start(bf16[32,192,128]{2,1,0:T(8,128)(2,1)} %get-tuple-element.40), calls=%async_computation.3 | async-start | bytes 3145728 | tf_op jit(solution)/shard_map/all_to_all | solution.py:327
  17.4 1.1 copy-start.2
  37.0 58.6 %copy-start.3 = (bf16[2048,288]{0,1:T(8,128)(2,1)S(1)}, bf16[2048,288]{0,1:T(8,128)(2,1)}, u32[]{:S(2)}) copy-start(bf16[2048,288]{0,1:T(8,128)(2,1)} %param.10) | copy-start | bytes 3538948
  100.3 33.6 %copy-start.5 = (bf16[288]{0:T(512)(128)(2,1)S(1)}, bf16[288]{0:T(512)(128)(2,1)}, u32[]{:S(2)}) copy-start(bf16[288]{0:T(512)(128)(2,1)} %bias_ref.3) | copy-start | bytes 1732
  100.3 33.6 %copy-start.6 = (bf16[512,288]{0,1:T(8,128)(2,1)S(1)}, bf16[512,288]{0,1:T(8,128)(2,1)}, u32[]{:S(2)}) copy-start(bf16[512,288]{0,1:T(8,128)(2,1)} %param.7) | copy-start | bytes 884740
  100.3 33.6 %all-to-all-start.6 = ((bf16[32,192,128]{2,1,0:T(8,128)(2,1)}), bf16[32,192,128]{2,1,0:T(8,128)(2,1)}, u32[]{:S(2)}, u32[]{:S(2)}) async-start(bf16[32,192,128]{2,1,0:T(8,128)(2,1)} %decode.1), calls=%async_computation.6 | async-start | bytes 3145728 | tf_op jit(solution)/shard_map/all_to_all | solution.py:327
  133.9 32.9 %copy-start.4 = (s32[512,4]{0,1:T(4,128)S(1)}, s32[512,4]{0,1:T(4,128)}, u32[]{:S(2)}) copy-start(s32[512,4]{0,1:T(4,128)} %param.11) | copy-start | bytes 24580
  138.5 28.2 %all-to-all-start.7 = ((bf16[32,192,128]{2,1,0:T(8,128)(2,1)}), bf16[32,192,128]{2,1,0:T(8,128)(2,1)S(1)}, u32[]{:S(2)}, u32[]{:S(2)}) async-start(bf16[32,192,128]{2,1,0:T(8,128)(2,1)} %get-tuple-element.47), calls=%async_computation.7 | async-start | bytes 3145728 | tf_op jit(solution)/shard_map/all_to_all | solution.py:327

commit v4 on v3

--- a/solution.py
+++ b/solution.py
@@ -16,7 +16,9 @@
 FEATURES = 288
 HALF = FEATURES // 2
 NAMED = 4
-MAIN = 64
+QUARTERS = 4
+SHARE = 16
+MAIN = QUARTERS * SHARE
 EXTRA = 16
 MAIN_SLOTS = GROUPS * MAIN
 EXTRA_SLOTS = GROUPS * EXTRA
@@ -50,17 +52,34 @@
     return pl.ds(pl.multiple_of(tile * width, width), width)
 
 
+def exchange(a, b, width):
+    kind = jnp.int16 if a.dtype == BF16 else jnp.int32
+    lane = lax.broadcasted_iota(kind, a.shape, 1)
+    even = jnp.bitwise_and(lane, jnp.full((), 2 * width - 1, kind)) < jnp.full((), width, kind)
+    return jnp.where(even, a, pltpu.roll(b, width, 1)), jnp.where(even, pltpu.roll(a, 128 - width, 1), b)
+
+
+def regroup(tiles):
+    a0, a1 = exchange(tiles[0], tiles[1], 32)
+    b0, b1 = exchange(tiles[2], tiles[3], 32)
+    return *exchange(a0, b0, 16), *exchange(a1, b1, 16)
+
+
+def ungroup(tiles):
+    a0, b0 = exchange(tiles[0], tiles[1], 16)
+    a1, b1 = exchange(tiles[2], tiles[3], 16)
+    return *exchange(a0, a1, 32), *exchange(b0, b1, 32)
+
+
 def store_pair(out_ref, pair, values):
-    top, bottom = values[:HALF], values[HALF:]
-    low = lax.broadcasted_iota(jnp.int32, (HALF, 128), 1) < MAIN
-    first = jnp.where(low, top, pltpu.roll(bottom, MAIN, 1))
-    second = jnp.where(low, pltpu.roll(top, MAIN, 1), bottom)
-    out_ref[pair, 0:HALF, :] = first.astype(BF16)
-    out_ref[pair + PAIRS, 0:HALF, :] = second.astype(BF16)
-
-
-def stage_copies(buffer_ref, out_ref, sems, stage):
-    first, count = (0, EARLY) if stage == 0 else (EARLY, PAIRS - EARLY)
+    values = values.astype(BF16)
+    first, second = exchange(values[:HALF], values[HALF:], MAIN)
+    out_ref[pair, 0:HALF, :] = first
+    out_ref[pair + PAIRS, 0:HALF, :] = second
+
+
+def stage_copies(buffer_ref, out_ref, sems, stage, early):
+    first, count = (0, early) if stage == 0 else (early, PAIRS - early)
     copies = []
     for side in range(2):
         devices = pl.ds(side * PAIRS + first, count)
@@ -70,15 +89,15 @@
     return copies
 
 
-def start_stage(buffer_ref, out_ref, sems, done):
-    if done in (EARLY, PAIRS):
-        for copy in stage_copies(buffer_ref, out_ref, sems, 0 if done == EARLY else 1):
+def start_stage(buffer_ref, out_ref, sems, done, early=EARLY):
+    if done in (early, PAIRS):
+        for copy in stage_copies(buffer_ref, out_ref, sems, 0 if done == early else 1, early):
             copy.start()
 
 
-def wait_stages(buffer_ref, out_ref, sems):
+def wait_stages(buffer_ref, out_ref, sems, early=EARLY):
     for stage in range(2):
-        for copy in stage_copies(buffer_ref, out_ref, sems, stage):
+        for copy in stage_copies(buffer_ref, out_ref, sems, stage, early):
             copy.wait()
 
 
@@ -95,17 +114,30 @@
         out_ref[:, HALF + part * EXTRA : HALF + (part + 1) * EXTRA, :] = piece.reshape(GROUPS, EXTRA, 128)
 
 
+def load_pair(in_ref, pair):
+    return exchange(in_ref[pair, 0:HALF, :], in_ref[pair + PAIRS, 0:HALF, :], MAIN)
+
+
 def unpack(in_ref, full_ref):
-    def one(pair):
-        lanes = slice(pair * 128, (pair + 1) * 128)
-        first = in_ref[pair, 0:HALF, :].astype(F32)
-        second = in_ref[pair + PAIRS, 0:HALF, :].astype(F32)
-        low = lax.broadcasted_iota(jnp.int32, (HALF, 128), 1) < MAIN
-        full_ref[0:HALF, lanes] = jnp.where(low, first, pltpu.roll(second, MAIN, 1)).astype(BF16)
-        full_ref[HALF:, lanes] = jnp.where(low, pltpu.roll(first, MAIN, 1), second).astype(BF16)
-
     for pair in range(PAIRS):
-        one(pair)
+        top, bottom = load_pair(in_ref, pair)
+        full_ref[0:HALF, pair * 128 : (pair + 1) * 128] = top
+        full_ref[HALF:, pair * 128 : (pair + 1) * 128] = bottom
+    unpack_extra(in_ref, full_ref)
+
+
+def unpack_grouped(in_ref, full_ref):
+    for quad in range(4):
+        pairs = [load_pair(in_ref, 4 * quad + j) for j in range(4)]
+        for half in range(2):
+            tiles = regroup([pair[half] for pair in pairs])
+            for quarter in range(QUARTERS):
+                tile = 4 * quarter + quad
+                full_ref[half * HALF : (half + 1) * HALF, tile * 128 : (tile + 1) * 128] = tiles[quarter]
+    return unpack_extra(in_ref, full_ref)
+
+
+def unpack_extra(in_ref, full_ref):
     eye = identity(128)
     turned, last = None, None
     for part in range(3):
@@ -117,40 +149,51 @@
 
 
 def placed(slots, names, start, count):
-    index = lax.broadcasted_iota(jnp.int32, (count, ROWS), 0) + start
-    named = jnp.zeros((count, ROWS), F32)
+    index = lax.broadcasted_iota(jnp.int16, (count, ROWS), 0) + jnp.int16(start)
+    named = jnp.zeros((count, ROWS), BF16)
     for k in range(NAMED):
-        named = jnp.where(index == slots[k], names[k], named)
-    named = named.astype(BF16)
+        named = jnp.where(index == jnp.broadcast_to(slots[k], index.shape), names[k], named)
     return named, jnp.minimum(named, BF16(1))
 
 
 def prepare_kernel(act_ref, bias_ref, blocks_ref, out_ref, slots_ref, send_ref, sems):
     blocks = blocks_ref[...]
-    target = lax.shift_right_logical(blocks, 5)
+    group = lax.shift_right_logical(blocks, 3)
     local = jnp.bitwise_and(blocks, LOCAL - 1)
-    groups = lax.broadcasted_iota(jnp.int32, (GROUPS, ROWS), 0)
-    hits = [groups == target[k : k + 1, :] for k in range(NAMED)]
+    count = GROUPS * QUARTERS
+    groups = lax.broadcasted_iota(jnp.int32, (count, ROWS), 0)
+    hits = [groups == group[k : k + 1, :] for k in range(NAMED)]
     counts = sum(jnp.where(hit, 1.0, 0.0) for hit in hits).astype(BF16)
     before = lax.broadcasted_iota(jnp.int32, (ROWS, ROWS), 0) < lax.broadcasted_iota(jnp.int32, (ROWS, ROWS), 1)
     earlier = mm(counts, jnp.where(before, 1.0, 0.0).astype(BF16))
+    beyond = jnp.maximum(mm(counts, jnp.ones((ROWS, 128), BF16)) - SHARE, 0.0).astype(BF16)
+    one = lax.broadcasted_iota(jnp.int32, (count, count), 0)
+    other = lax.broadcasted_iota(jnp.int32, (count, count), 1)
+    same = lax.shift_right_logical(one, 2) == lax.shift_right_logical(other, 2)
+    offset = mm(jnp.where(same & (other < one), 1.0, 0.0).astype(BF16), beyond)
+    table = earlier + 1024.0 * jnp.concatenate([offset] * (ROWS // 128), axis=1)
     slots, names, most = [], [], jnp.zeros((1, ROWS), jnp.int32)
     for k in range(NAMED):
-        mine = target[k : k + 1, :]
-        rank = jnp.sum(jnp.where(hits[k], earlier, 0.0), axis=0, keepdims=True).astype(jnp.int32)
-        for other in range(k):
-            rank = rank + jnp.where(target[other : other + 1, :] == mine, 1, 0)
-        main = (jnp.bitwise_and(mine, PAIRS - 1) * 2 + lax.shift_right_logical(mine, 4)) * MAIN + rank
-        extra = MAIN_SLOTS + mine * EXTRA + (rank - MAIN)
-        slots.append(jnp.where(rank < MAIN, main, jnp.where(rank < MAIN + EXTRA, extra, -1)))
-        names.append((local[k : k + 1, :] + 1).astype(F32))
-        most = jnp.maximum(most, rank)
-    over = jnp.where(jnp.max(most, axis=1, keepdims=True) >= MAIN + EXTRA, 1.0, 0.0)
+        mine = group[k : k + 1, :]
+        found = jnp.sum(jnp.where(hits[k], table, 0.0), axis=0, keepdims=True).astype(jnp.int32)
+        rank = jnp.bitwise_and(found, 1023)
+        for previous in range(k):
+            rank = rank + jnp.where(group[previous : previous + 1, :] == mine, 1, 0)
+        target = lax.shift_right_logical(mine, 2)
+        place = (jnp.bitwise_and(target, PAIRS - 1) * 2 + lax.shift_right_logical(target, 4)) * MAIN
+        main = place + jnp.bitwise_and(mine, QUARTERS - 1) * SHARE + rank
+        extra = lax.shift_right_logical(found, 10) + rank - SHARE
+        late = jnp.where(extra < EXTRA, MAIN_SLOTS + target * EXTRA + extra, -1)
+        slots.append(jnp.where(rank < SHARE, main, late))
+        names.append((local[k : k + 1, :] + 1).astype(F32).astype(BF16))
+        most = jnp.maximum(most, jnp.where(rank < SHARE, 0, extra))
+    over = jnp.where(jnp.max(most, axis=1, keepdims=True) >= EXTRA, 1.0, 0.0)
     shifted = (act_ref[...].astype(F32) - bias_column(bias_ref)).astype(BF16)
 
     for k in range(NAMED):
         slots_ref[k : k + 1, :] = slots[k]
     slots_ref[NAMED:, :] = jnp.zeros((8 - NAMED, ROWS), jnp.int32)
+    slots = [slot.astype(jnp.int16) for slot in slots]
     named, place = placed(slots, names, MAIN_SLOTS, EXTRA_SLOTS)
     padded = jnp.concatenate([shifted, jnp.zeros((96, ROWS), BF16)], axis=0)
     values = mm_nt(place, padded)
@@ -181,21 +224,25 @@
 
 
 def place_kernel(slots_ref, place_ref):
-    slots = [slots_ref[k : k + 1, :] for k in range(NAMED)]
-    ones = [jnp.ones((1, ROWS), F32)] * NAMED
+    slots = [slots_ref[k : k + 1, :].astype(jnp.int16) for k in range(NAMED)]
+    ones = [jnp.ones((1, ROWS), BF16)] * NAMED
     for start in range(0, SLOTS, 256):
         place_ref[start : start + 256, :] = placed(slots, ones, start, 256)[0]
 
 
 def encode_kernel(recv_ref, enc_ref, rest_ref, out_ref, ids_ref, over_ref, full_ref):
-    last, turned = unpack(recv_ref, full_ref)
+    last, turned = unpack_grouped(recv_ref, full_ref)
     pick = lax.broadcasted_iota(jnp.int32, (2 * GROUPS, EXTRA_SLOTS), 0)
     column = lax.broadcasted_iota(jnp.int32, (2 * GROUPS, EXTRA_SLOTS), 1)
     wanted = jnp.where(pick < GROUPS, pick * EXTRA, (pick - GROUPS) * EXTRA + 1)
     rows = mm(jnp.where(column == wanted, 1.0, 0.0).astype(BF16), last)
     first, second = rows[:PAIRS], rows[PAIRS:GROUPS]
     low = lax.broadcasted_iota(jnp.int32, (PAIRS, 128), 1) < MAIN
-    ids_ref[0:PAIRS, :] = jnp.where(low, pltpu.roll(first, MAIN, 1), second)
+    named = jnp.where(low, pltpu.roll(first, MAIN, 1), second)
+    picked = [[named[4 * quad + j : 4 * quad + j + 1] for quad in range(4)] for j in range(4)]
+    tiles = regroup([jnp.concatenate(some, axis=0) for some in picked])
+    for quarter in range(QUARTERS):
+        ids_ref[4 * quarter : 4 * quarter + 4, :] = tiles[quarter]
     for part in range(EXTRA_SLOTS // 128):
         ids_ref[PAIRS + part : PAIRS + part + 1, :] = turned[32:33, part * 128 : (part + 1) * 128]
     ids_ref[LANE_TILES:, :] = jnp.zeros((24 - LANE_TILES, 128), F32)
@@ -207,18 +254,24 @@
         lanes = slice(tile * 256, (tile + 1) * 256)
         ids = jnp.concatenate([ids_ref[2 * tile : 2 * tile + 1, :], ids_ref[2 * tile + 1 : 2 * tile + 2, :]], axis=1)
         code = ids.astype(jnp.int32) - 1
-        part = mm(enc_ref[...], full_ref[0:256, lanes])
+        main = tile < PAIRS // 2
+        quarter = tile // 2 if main else 0
+        first, held = (8 * quarter, 8) if main else (0, LOCAL)
+        part = mm(enc_ref[first * BLOCK : (first + held) * BLOCK, :], full_ref[0:256, lanes])
         total = jnp.zeros((BLOCK, 256), F32)
-        for b in range(LOCAL):
-            total = jnp.where(code == b, part[b * BLOCK : (b + 1) * BLOCK], total)
+        for b in range(held):
+            total = jnp.where(code == first + b, part[b * BLOCK : (b + 1) * BLOCK], total)
         rest = full_ref[256:, lanes]
         member = jnp.broadcast_to(jnp.bitwise_and(code, 7), (32, 256))
-        spread = [jnp.where(member == m, rest, BF16(0)) for m in range(8)]
-        part = mm(rest_ref[...], jnp.concatenate(spread, axis=0))
-        group = lax.shift_right_arithmetic(code, 3)
-        more = jnp.zeros((BLOCK, 256), F32)
-        for g in range(4):
-            more = jnp.where(group == g, part[g * BLOCK : (g + 1) * BLOCK], more)
+        spread = jnp.concatenate([jnp.where(member == m, rest, BF16(0)) for m in range(8)], axis=0)
+        if main:
+            more = mm(rest_ref[quarter * BLOCK : (quarter + 1) * BLOCK, :], spread)
+        else:
+            part = mm(rest_ref[...], spread)
+            more = jnp.zeros((BLOCK, 256), F32)
+            for g in range(QUARTERS):
+                wanted = lax.shift_right_arithmetic(code, 3) == g
+                more = jnp.where(wanted, part[g * BLOCK : (g + 1) * BLOCK], more)
         total = total + more
         for half in range(2):
             lane_tile = 2 * tile + half
@@ -245,20 +298,30 @@
         codes = full_ref[:, tile * 256 : (tile + 1) * 256]
         ids = jnp.concatenate([ids_ref[2 * tile : 2 * tile + 1, :], ids_ref[2 * tile + 1 : 2 * tile + 2, :]], axis=1)
         ids = jnp.broadcast_to(ids, (BLOCK, 256)).astype(BF16)
-        spread = [jnp.where(ids == BF16(b + 1), codes, BF16(0)) for b in range(LOCAL)]
-        return mm(dec_ref[...], jnp.concatenate(spread, axis=0))
+        main = tile < PAIRS // 2
+        first, held = (8 * (tile // 2), 8) if main else (0, LOCAL)
+        spread = [jnp.where(ids == BF16(b + 1), codes, BF16(0)) for b in range(first, first + held)]
+        weights = dec_ref[:, first * BLOCK : (first + held) * BLOCK]
+        return mm(weights, jnp.concatenate(spread, axis=0)).astype(BF16)
 
     extra_ref[FEATURES:, :] = jnp.zeros((384 - FEATURES, EXTRA_SLOTS), BF16)
     for tile in range(PAIRS // 2, LANE_TILES // 2):
         start = tile * 256 - MAIN_SLOTS
-        extra_ref[0:FEATURES, start : start + 256] = contribution(tile).astype(BF16)
+        extra_ref[0:FEATURES, start : start + 256] = contribution(tile)
     store_extra(send_ref, mm_nt(identity(EXTRA_SLOTS), extra_ref[...]))
-    for tile in range(PAIRS // 2):
-        values = contribution(tile)
-        store_pair(send_ref, 2 * tile, values[:, :128])
-        store_pair(send_ref, 2 * tile + 1, values[:, 128:])
-        start_stage(send_ref, out_ref, sems, 2 * tile + 2)
-    wait_stages(send_ref, out_ref, sems)
+    for double in range(2):
+        values = [contribution(2 * quarter + double) for quarter in range(QUARTERS)]
+        for side in range(2):
+            lanes = slice(side * 128, (side + 1) * 128)
+            tops = ungroup([value[:HALF, lanes] for value in values])
+            bottoms = ungroup([value[HALF:, lanes] for value in values])
+            for j in range(4):
+                pair = 8 * double + 4 * side + j
+                first, second = exchange(tops[j], bottoms[j], MAIN)
+                send_ref[pair, 0:HALF, :] = first
+                send_ref[pair + PAIRS, 0:HALF, :] = second
+        start_stage(send_ref, out_ref, sems, 8 * double + 8, 8)
+    wait_stages(send_ref, out_ref, sems, 8)
 
 
 def combine_kernel(recv_ref, place_ref, act_ref, bias_ref, out_ref, loss_ref, full_ref, send_ref, sems):
@@ -282,17 +345,22 @@
     recv_ref, codes_ref, ids_ref, loss_ref, out_ref, out_loss_ref, full_ref, code_ref, grad_ref, sems
 ):
     out_loss_ref[...] = loss_ref[...]
-    unpack(recv_ref, full_ref)
+    unpack_grouped(recv_ref, full_ref)
     load_codes(codes_ref, code_ref)
     ids = jnp.concatenate([ids_ref[tile : tile + 1, :] for tile in range(LANE_TILES)], axis=1)
     ids = jnp.broadcast_to(ids, (BLOCK, SLOTS)).astype(BF16)
     copies, begin = [], 0
     for start in range(0, LOCAL * BLOCK, 256):
         stop = start + 256
-        spread = [
-            jnp.where(ids == BF16(b + 1), code_ref[...], BF16(0)) for b in range(start // BLOCK, stop // BLOCK)
-        ]
-        grad_ref[:, start:stop] = mm_nt(full_ref[...], jnp.concatenate(spread, axis=0)).astype(BF16)
+        width = MAIN_SLOTS // QUARTERS
+        lanes = slice(start // 512 * width, (start // 512 + 1) * width)
+
+        def both(values):
+            return jnp.concatenate([values[:, lanes], values[:, MAIN_SLOTS:]], axis=1)
+
+        near, codes = both(ids), both(code_ref)
+        spread = [jnp.where(near == BF16(b + 1), codes, BF16(0)) for b in range(start // BLOCK, stop // BLOCK)]
+        grad_ref[:, start:stop] = mm_nt(both(full_ref), jnp.concatenate(spread, axis=0)).astype(BF16)
         if stop in (LOCAL * BLOCK * 3 // 4, LOCAL * BLOCK):
             lanes = pl.ds(begin, stop - begin)
             copy = pltpu.make_async_copy(grad_ref.at[:, lanes], out_ref.at[:, lanes], sems.at[len(copies)])
@@ -426,7 +494,7 @@
     )(codes, ids, decoder.T)
     received = route(sent)
     heavy = over[0, 0] > 0
-    received, heavy = lax.optimization_barrier((received, heavy))
+    place, heavy = lax.optimization_barrier((place, heavy))
     sent, loss = call(
         combine_kernel,
         (packed, shape((ROWS // 128, 128), F32)),

time: 175 us -> 171 us (0.977)
  Pallas kernels: 23.9 us -> 18.6 us
  transfers between devices with their start and end apart: 3 -> 3, of which waited for: 2 -> 2; matrix products, arithmetic and copies ran while one was open for 4% -> 4% of each run, Pallas kernels for 1% -> 0%
where the time goes in v4:
time: 171 us; the launch traced here: 168 us
  blocking collectives  77.2 us (45%)
  waiting for transfers between devices  34.2 us (20%)
  starting transfers between devices  28.3 us (17%)
  Pallas kernels  18.6 us (11%)
  local copies, waits for them, and re-layouts  7.25 us (4%)
    all_to_all x3, waiting for transfers between devices, route(): lax.all_to_all(buffer, PLANE, split_axis=0, concat_axis=0, tiled=True)  34.2 us
    all_to_all x3, starting transfers between devices, route(): lax.all_to_all(buffer, PLANE, split_axis=0, concat_axis=0, tiled=True)  28.3 us
    all_to_all x1, blocking collectives, sum_codes(): return lax.all_to_all(copies, DP, split_axis=0, concat_axis=0, tiled=True)  27.6 us
    all_to_all x1, blocking collectives, sum_codes(): lax.all_to_all(partial, DP, split_axis=0, concat_axis=0, tiled=True)  27 us
    psum x2, blocking collectives, sum_loss(): return lax.psum(lax.psum(part, INNER), OUTER)  22.7 us
    pallas_call x1, Pallas kernels, on_device(): call(combine_kernel, (packed, shape((ROWS // 128, 128), F32)), [full] + s...  4.62 us
    pallas_call x1, Pallas kernels, on_device(): call(prepare_kernel, (packed, shape((8, ROWS), jnp.int32)), sending, 2 *...  4.32 us
  transfers between devices with their start and end apart: 3, of which 2 were waited for; matrix products, arithmetic and copies ran while one was open for 4% of the time, Pallas kernels for 0%

profile of v4, /device:TPU:1, one launch (start us, length us, event | category | flops | bytes accessed | tf_op | source)
XLA Modules:
  0.0 167.6 jit_solution(15683338754375358141)
XLA Ops:
  0.6 4.3 %prepare.1 = (bf16[32,192,128]{2,1,0:T(8,128)(2,1)}, s32[8,512]{1,0:T(8,128)S(1)}) custom-call(bf16[288,512]{1,0:T(8,128)(2,1)} %bitcast.42, bf16[288]{0:T(512)(128)(2,1)} %bias_ref.3, s32[4,512]{1,0:T(4,128)} %bitcast.41), custom_call_target="tpu_custom_call" | custom-call | flops 754974720 | bytes 6000000 | tf_op jit(solution)/shard_map/prepare/pallas_call | solution.py:460
  5.0 10.5 %all-to-all-start.3 = ((bf16[32,192,128]{2,1,0:T(8,128)(2,1)}), bf16[32,192,128]{2,1,0:T(8,128)(2,1)S(1)}, u32[]{:S(2)}, u32[]{:S(2)}) async-start(bf16[32,192,128]{2,1,0:T(8,128)(2,1)} %get-tuple-element.41), calls=%async_computation.3 | async-start | bytes 3145728 | tf_op jit(solution)/shard_map/all_to_all | solution.py:395
  15.5 1.8 %copy.64 = bf16[288,2048]{0,1:T(8,128)(2,1)S(1)} copy(bf16[288,2048]{1,0:T(8,128)(2,1)} %param.9) | data formatting | bytes 2359296 | tf_op args[2]
  17.3 0.0 copy-start.2
  17.3 1.1 copy-done.2
  18.5 0.8 slice.29
  19.3 1.3 slice.28.enc_ref
  20.6 1.3 copy.65
  21.9 0.2 reshape.49
  22.1 0.1 copy.66.rest_ref
  22.2 14.7 %all-to-all-done.3.recv_ref = bf16[32,192,128]{2,1,0:T(8,128)(2,1)S(1)} async-done(((bf16[32,192,128]{2,1,0:T(8,128)(2,1)}), bf16[32,192,128]{2,1,0:T(8,128)(2,1)S(1)}, u32[]{:S(2)}, u32[]{:S(2)}) %all-to-all-start.3) | async-done | bytes 1572896 | tf_op jit(solution)/shard_map/all_to_all | solution.py:395
  36.9 2.4 %encode.1 = (bf16[16,80,128]{2,1,0:T(8,128)(2,1)S(1)}, f32[24,128]{1,0:T(8,128)S(1)}, s32[8,128]{1,0:T(8,128)S(1)}) custom-call(bf16[32,192,128]{2,1,0:T(8,128)(2,1)S(1)} %all-to-all-done.3.recv_ref, bf16[2048,256]{1,0:T(8,128)(2,1)S(1)} %slice.28.enc_ref, bf16[256,256]{1,0:T(8,128)(2,1)S(1)} %copy.66.rest_ref), custom_call_target="tpu_custom_call" | custom-call | flops 3019898880 | bytes 6000000 | tf_op jit(solution)/shard_map/encode/pallas_call | solution.py:473
  39.3 27.0 %all_to_all.38 = bf16[16,80,128]{2,1,0:T(8,128)(2,1)S(1)} all-to-all(bf16[16,80,128]{2,1,0:T(8,128)(2,1)S(1)} %get-tuple-element.44), channel_id=1, replica_groups=mesh['dp_outer'=4,'dp_inner'=4,'latent'=8,'section'=4] {'dp_outer','dp_i..., dimensions={0} | all-to-all | bytes 655360 | tf_op jit(solution)/shard_map/all_to_all | solution.py:399
  66.3 0.1 convert_reduce_fusion.1
  66.4 27.6 %all_to_all.39.codes_ref = bf16[16,80,128]{2,1,0:T(8,128)(2,1)S(1)} all-to-all(bf16[16,80,128]{2,1,0:T(8,128)(2,1)S(1)} %broadcast_in_dim.2), channel_id=1, replica_groups=mesh['dp_outer'=4,'dp_inner'=4,'latent'=8,'section'=4] {'dp_outer','dp_i..., dimensions={0} | all-to-all | bytes 655360 | tf_op jit(solution)/shard_map/all_to_all | solution.py:403
  94.0 0.0 copy-done.3
  94.0 3.2 %decode.1 = bf16[32,192,128]{2,1,0:T(8,128)(2,1)} custom-call(bf16[16,80,128]{2,1,0:T(8,128)(2,1)S(1)} %all_to_all.39.codes_ref, f32[24,128]{1,0:T(8,128)S(1)} %get-tuple-element.45.ids_ref, bf16[288,2048]{1,0:T(8,128)(2,1)S(1)} %bitcast.39), custom_call_target="tpu_custom_call" | custom-call | flops 3019898880 | bytes 6000000 | tf_op jit(solution)/shard_map/decode/pallas_call | solution.py:482
  97.2 0.0 copy-start.5
  97.2 0.0 copy-start.6
  97.3 12.1 %all-to-all-start.6 = ((bf16[32,192,128]{2,1,0:T(8,128)(2,1)}), bf16[32,192,128]{2,1,0:T(8,128)(2,1)}, u32[]{:S(2)}, u32[]{:S(2)}) async-start(bf16[32,192,128]{2,1,0:T(8,128)(2,1)} %decode.1), calls=%async_computation.6 | async-start | bytes 3145728 | tf_op jit(solution)/shard_map/all_to_all | solution.py:395
  109.4 0.8 place.1.place_ref
  110.2 0.5 slice.23
  111.3 0.0 copy-start.4
  111.4 19.5 %all-to-all-done.6.recv_ref = bf16[32,192,128]{2,1,0:T(8,128)(2,1)} async-done(((bf16[32,192,128]{2,1,0:T(8,128)(2,1)}), bf16[32,192,128]{2,1,0:T(8,128)(2,1)}, u32[]{:S(2)}, u32[]{:S(2)}) %all-to-all-start.6) | async-done | bytes 1572896 | tf_op jit(solution)/shard_map/all_to_all | solution.py:395
  130.8 0.0 copy-done.5
  130.8 4.6 %combine.1 = (bf16[32,192,128]{2,1,0:T(8,128)(2,1)}, f32[4,128]{1,0:T(4,128)S(1)}) custom-call(bf16[32,192,128]{2,1,0:T(8,128)(2,1)} %all-to-all-done.6.recv_ref, bf16[2560,512]{1,0:T(8,128)(2,1)S(1)} %place.1.place_ref, bf16[288,512]{1,0:T(8,128)(2,1)S(1)} %bitcast.43, bf16[288]{0:T(512)(128)(2,1)S(1)} %copy-done.5), custom_call_target="tpu_custom_call" | custom-call | flops 1509949440 | bytes 6000000 | tf_op jit(solution)/shard_map/combine/pallas_call | solution.py:498
  135.5 5.7 %all-to-all-start.7 = ((bf16[32,192,128]{2,1,0:T(8,128)(2,1)}), bf16[32,192,128]{2,1,0:T(8,128)(2,1)S(1)}, u32[]{:S(2)}, u32[]{:S(2)}) async-start(bf16[32,192,128]{2,1,0:T(8,128)(2,1)} %get-tuple-element.47), calls=%async_computation.7 | async-start | bytes 3145728 | tf_op jit(solution)/shard_map/all_to_all | solution.py:395
  141.2 10.1 %psum.28 = f32[4,128]{1,0:T(4,128)S(1)} all-reduce(f32[4,128]{1,0:T(4,128)S(1)} %get-tuple-element.48), channel_id=1, replica_groups=mesh['dp_outer'=4,'dp_inner'=4,'latent'=8,'section'=4] {'dp_inner'}, use_global_device_ids=true, to_apply=%region_1.0 | all-reduce | flops 512 | bytes 4096 | tf_op jit(solution)/shard_map/psum | solution.py:407
  151.2 12.6 %psum.29 = f32[4,128]{1,0:T(4,128)S(1)} all-reduce(f32[4,128]{1,0:T(4,128)S(1)} %psum.28), channel_id=1, replica_groups=mesh['dp_outer'=4,'dp_inner'=4,'latent'=8,'section'=4] {'dp_outer'}, use_global_device_ids=true, to_apply=%region_2.0 | all-reduce | flops 512 | bytes 4096 | tf_op jit(solution)/shard_map/psum | solution.py:407
  163.9 0.0 all-to-all-done.7
  163.9 3.5 %conditional.1 = (f32[512]{0:T(512)}, bf16[2048,288]{0,1:T(8,128)(2,1)}) conditional(s32[]{:T(128)} %convert_element_type.62, (bf16[32,192,128]{2,1,0:T(8,128)(2,1)S(1)}, bf16[16,80,128]{2,1,0:T(8,128)(2,1)S(1)}, f32[24,128]{1,0:T(8,128)S(1)}, f32[4,128]{1,0:T(4,128)S(1)}) %tuple.17, (s32[512,4]{0,1:T(4,128)S(1)}, bf16[512,288]{0,1:T(8,128)(2,1)S(1)}, ...), branch_computations={%region_3.0_spmd, %region_4.0_spmd} | conditional | flops 4205791488 | bytes 89270392 | solution.py:527
  163.9 3.3 %gradient.1 = (bf16[288,2048]{1,0:T(8,128)(2,1)}, f32[4,128]{1,0:T(4,128)}) custom-call(bf16[32,192,128]{2,1,0:T(8,128)(2,1)S(1)} %get-tuple-element.18.recv_ref, bf16[16,80,128]{2,1,0:T(8,128)(2,1)S(1)} %get-tuple-element.19.codes_ref, f32[24,128]{1,0:T(8,128)S(1)} %get-tuple-element.20.ids_ref, f32[4,128]{1,0:T(4,128)S(1)} %get-tuple-element.21.loss_ref), custom_call_target="tpu_custom_call" | custom-call | flops 3019898880 | bytes 6000000 | tf_op jit(solution)/shard_map/cond/branch_0_fun/gradient/pallas_call | solution.py:511
  (5 shorter events, 0.1 us)
Async XLA Ops:
  5.0 32.0 %all-to-all-start.3 = ((bf16[32,192,128]{2,1,0:T(8,128)(2,1)}), bf16[32,192,128]{2,1,0:T(8,128)(2,1)S(1)}, u32[]{:S(2)}, u32[]{:S(2)}) async-start(bf16[32,192,128]{2,1,0:T(8,128)(2,1)} %get-tuple-element.41), calls=%async_computation.3 | async-start | bytes 3145728 | tf_op jit(solution)/shard_map/all_to_all | solution.py:395
  17.3 1.1 copy-start.2
  36.9 57.1 %copy-start.3 = (bf16[2048,288]{0,1:T(8,128)(2,1)S(1)}, bf16[2048,288]{0,1:T(8,128)(2,1)}, u32[]{:S(2)}) copy-start(bf16[2048,288]{0,1:T(8,128)(2,1)} %param.10) | copy-start | bytes 3538948
  97.2 33.6 %copy-start.5 = (bf16[288]{0:T(512)(128)(2,1)S(1)}, bf16[288]{0:T(512)(128)(2,1)}, u32[]{:S(2)}) copy-start(bf16[288]{0:T(512)(128)(2,1)} %bias_ref.3) | copy-start | bytes 1732
  97.2 33.6 %copy-start.6 = (bf16[512,288]{0,1:T(8,128)(2,1)S(1)}, bf16[512,288]{0,1:T(8,128)(2,1)}, u32[]{:S(2)}) copy-start(bf16[512,288]{0,1:T(8,128)(2,1)} %param.7) | copy-start | bytes 884740
  97.3 33.6 %all-to-all-start.6 = ((bf16[32,192,128]{2,1,0:T(8,128)(2,1)}), bf16[32,192,128]{2,1,0:T(8,128)(2,1)}, u32[]{:S(2)}, u32[]{:S(2)}) async-start(bf16[32,192,128]{2,1,0:T(8,128)(2,1)} %decode.1), calls=%async_computation.6 | async-start | bytes 3145728 | tf_op jit(solution)/shard_map/all_to_all | solution.py:395
  111.3 52.5 %copy-start.4 = (s32[512,4]{0,1:T(4,128)S(1)}, s32[512,4]{0,1:T(4,128)}, u32[]{:S(2)}) copy-start(s32[512,4]{0,1:T(4,128)} %param.11) | copy-start | bytes 24580
  135.5 28.4 %all-to-all-start.7 = ((bf16[32,192,128]{2,1,0:T(8,128)(2,1)}), bf16[32,192,128]{2,1,0:T(8,128)(2,1)S(1)}, u32[]{:S(2)}, u32[]{:S(2)}) async-start(bf16[32,192,128]{2,1,0:T(8,128)(2,1)} %get-tuple-element.47), calls=%async_computation.7 | async-start | bytes 3145728 | tf_op jit(solution)/shard_map/all_to_all | solution.py:395

commit v5 on v4

--- a/solution.py
+++ b/solution.py
@@ -223,13 +223,6 @@
     wait_stages(send_ref, out_ref, sems)
 
 
-def place_kernel(slots_ref, place_ref):
-    slots = [slots_ref[k : k + 1, :].astype(jnp.int16) for k in range(NAMED)]
-    ones = [jnp.ones((1, ROWS), BF16)] * NAMED
-    for start in range(0, SLOTS, 256):
-        place_ref[start : start + 256, :] = placed(slots, ones, start, 256)[0]
-
-
 def encode_kernel(recv_ref, enc_ref, rest_ref, out_ref, ids_ref, over_ref, full_ref):
     last, turned = unpack_grouped(recv_ref, full_ref)
     pick = lax.broadcasted_iota(jnp.int32, (2 * GROUPS, EXTRA_SLOTS), 0)
@@ -248,7 +241,7 @@
     ids_ref[LANE_TILES:, :] = jnp.zeros((24 - LANE_TILES, 128), F32)
     flags = jnp.where(lax.broadcasted_iota(jnp.int32, (GROUPS, 128), 1) == MAIN, rows[GROUPS:], 0.0)
     flag = jnp.max(jnp.max(flags, axis=1, keepdims=True), axis=0, keepdims=True)
-    over_ref[...] = jnp.broadcast_to(flag, (8, 128)).astype(jnp.int32)
+    over_ref[0, 0] = jnp.max(flag).astype(jnp.int32)
 
     for tile in range(LANE_TILES // 2):
         lanes = slice(tile * 256, (tile + 1) * 256)
@@ -291,7 +284,7 @@
             ]
 
 
-def decode_kernel(codes_ref, ids_ref, dec_ref, out_ref, full_ref, extra_ref, send_ref, sems):
+def decode_kernel(codes_ref, ids_ref, dec_ref, send_ref, full_ref, extra_ref):
     load_codes(codes_ref, full_ref)
 
     def contribution(tile):
@@ -320,11 +313,15 @@
                 first, second = exchange(tops[j], bottoms[j], MAIN)
                 send_ref[pair, 0:HALF, :] = first
                 send_ref[pair + PAIRS, 0:HALF, :] = second
-        start_stage(send_ref, out_ref, sems, 8 * double + 8, 8)
-    wait_stages(send_ref, out_ref, sems, 8)
-
-
-def combine_kernel(recv_ref, place_ref, act_ref, bias_ref, out_ref, loss_ref, full_ref, send_ref, sems):
+
+
+def combine_kernel(
+    recv_ref, slots_ref, act_ref, bias_ref, out_ref, loss_ref, full_ref, place_ref, send_ref, sems
+):
+    slots = [slots_ref[k : k + 1, :].astype(jnp.int16) for k in range(NAMED)]
+    ones = [jnp.ones((1, ROWS), BF16)] * NAMED
+    for start in range(0, SLOTS, 256):
+        place_ref[start : start + 256, :] = placed(slots, ones, start, 256)[0]
     unpack(recv_ref, full_ref)
     error = mm(full_ref[...], place_ref[...]) + bias_column(bias_ref) - act_ref[...].astype(F32)
     sent = error.astype(BF16)
@@ -396,11 +393,12 @@
 
 
 def sum_codes(partial):
-    received = lax.all_to_all(partial, DP, split_axis=0, concat_axis=0, tiled=True)
-    total = jnp.sum(received.astype(F32), axis=0)
+    shares = partial.reshape(4, SHARDS // 4 * CHUNK_ROWS, 128)
+    received = lax.all_to_all(shares, INNER, split_axis=0, concat_axis=0, tiled=True)
+    total = lax.psum(jnp.sum(received.astype(F32), axis=0), OUTER)
     codes = jnp.maximum(total, 0.0).astype(BF16)
-    copies = jnp.broadcast_to(codes[None], (SHARDS,) + codes.shape)
-    return lax.all_to_all(copies, DP, split_axis=0, concat_axis=0, tiled=True)
+    copies = jnp.broadcast_to(codes[None], shares.shape)
+    return lax.all_to_all(copies, INNER, split_axis=0, concat_axis=0, tiled=True).reshape(partial.shape)
 
 
 def sum_loss(part):
@@ -467,43 +465,39 @@
         out_specs=(hbm, vmem),
     )(act, bias, active_blocks.T)
     received = route(sent)
-    place = call(place_kernel, shape((SLOTS, ROWS)), [], 0, "place", 16)(slots)
     turned = encoder.T
     rest = turned[:, 256:].reshape(4, 8, BLOCK, 32).transpose(0, 2, 1, 3).reshape(4 * BLOCK, 256)
     partial, ids, over = call(
         encode_kernel,
-        (shape((SHARDS, CHUNK_ROWS, 128)), shape((24, 128), F32), shape((8, 128), jnp.int32)),
+        (shape((SHARDS, CHUNK_ROWS, 128)), shape((24, 128), F32), shape((1, 1), jnp.int32)),
         [full],
         spread_flops,
         "encode",
         20,
+        out_specs=(vmem, vmem, pl.BlockSpec(memory_space=pltpu.SMEM)),
     )(received, turned[:, :256], rest)
     codes = sum_codes(partial)
     sent = call(
         decode_kernel,
-        packed,
+        shape((GROUPS, PACKED, 128)),
         [
             pltpu.VMEM((BLOCK, SLOTS), BF16),
             pltpu.VMEM((384, EXTRA_SLOTS), BF16),
-        ]
-        + sending,
+        ],
         spread_flops,
         "decode",
         20,
-        out_specs=hbm,
     )(codes, ids, decoder.T)
     received = route(sent)
-    heavy = over[0, 0] > 0
-    place, heavy = lax.optimization_barrier((place, heavy))
     sent, loss = call(
         combine_kernel,
         (packed, shape((ROWS // 128, 128), F32)),
-        [full] + sending,
+        [full, pltpu.VMEM((SLOTS, ROWS), BF16)] + sending,
         4 * FEATURES * SLOTS * ROWS,
         "combine",
         20,
         out_specs=(hbm, vmem),
-    )(received, place, act, bias)
+    )(received, slots, act, bias)
     received = route(sent)
     loss = sum_loss(loss)
 
@@ -525,7 +519,7 @@
         return gradient.T, row_loss.reshape(ROWS)
 
     return lax.cond(
-        heavy,
+        over[0, 0] > 0,
         lambda: padded_plan(activations, bias_dec, encoder, decoder, active_blocks),
         packed_plan,
     )

time: 171 us -> 165 us (0.965)
  blocking collectives: 77.2 us -> 107 us
  waiting for transfers between devices: 34.2 us -> 14.7 us
  starting transfers between devices: 28.3 us -> 14.9 us
    psum x0 -> x1, blocking collectives: none -> 28.1 us  [sum_codes(): total = lax.psum(jnp.sum(received.astype(F32), axis=0), OUTER)]
    all_to_all x3 -> x2, waiting for transfers between devices: 34.2 us -> 14.7 us  [route(): lax.all_to_all(buffer, PLANE, split_axis=0, concat_axis=0, tiled=True)]
    all_to_all x3 -> x2, starting transfers between devices: 28.3 us -> 14.9 us  [route(): lax.all_to_all(buffer, PLANE, split_axis=0, concat_axis=0, tiled=True)]
    all_to_all x2 -> x3, blocking collectives: 54.5 us -> 57.6 us  [the longest x1 35.3 us: route(): lax.all_to_all(buffer, PLANE, split_axis=0, concat_axis=0, tiled=True)]
    pallas_call x3 -> x2, Pallas kernels: 8.65 us -> 7.06 us  [the longest x1 3.58 us: on_device(): call(decode_kernel, shape((GROUPS, PACKED, 128)), [pltpu.VMEM((BLOCK, SLO...]
  transfers between devices with their start and end apart: 3 -> 2, of which waited for: 2 -> 1; matrix products, arithmetic and copies ran while one was open for 4% -> 3% of each run, Pallas kernels for 0% -> 0%
where the time goes in v5:
time: 165 us; the launch traced here: 162 us
  blocking collectives  107 us (65%)
  Pallas kernels  17 us (10%)
  starting transfers between devices  14.9 us (9%)
  waiting for transfers between devices  14.7 us (9%)
  local copies, waits for them, and re-layouts  6.73 us (4%)
    all_to_all x1, blocking collectives, route(): lax.all_to_all(buffer, PLANE, split_axis=0, concat_axis=0, tiled=True)  35.3 us
    psum x1, blocking collectives, sum_codes(): total = lax.psum(jnp.sum(received.astype(F32), axis=0), OUTER)  28.1 us
    psum x2, blocking collectives, sum_loss(): return lax.psum(lax.psum(part, INNER), OUTER)  21.5 us
    all_to_all x2, starting transfers between devices, route(): lax.all_to_all(buffer, PLANE, split_axis=0, concat_axis=0, tiled=True)  14.9 us
    all_to_all x2, waiting for transfers between devices, route(): lax.all_to_all(buffer, PLANE, split_axis=0, concat_axis=0, tiled=True)  14.7 us
    all_to_all x1, blocking collectives, sum_codes(): lax.all_to_all(shares, INNER, split_axis=0, concat_axis=0, tiled=True)  12.3 us
    all_to_all x1, blocking collectives, sum_codes(): lax.all_to_all(copies, INNER, split_axis=0, concat_axis=0, tiled=True)  9.99 us
    pallas_call x1, Pallas kernels, on_device(): call(prepare_kernel, (packed, shape((8, ROWS), jnp.int32)), sending, 2 *...  4.32 us
  transfers between devices with their start and end apart: 2, of which 1 were waited for; matrix products, arithmetic and copies ran while one was open for 3% of the time, Pallas kernels for 0%

profile of v5, /device:TPU:1, one launch (start us, length us, event | category | flops | bytes accessed | tf_op | source)
XLA Modules:
  0.0 162.5 jit_solution(2100474115050973352)
XLA Ops:
  0.6 4.3 %prepare.1 = (bf16[32,192,128]{2,1,0:T(8,128)(2,1)}, s32[8,512]{1,0:T(8,128)S(1)}) custom-call(bf16[288,512]{1,0:T(8,128)(2,1)} %bitcast.47, bf16[288]{0:T(512)(128)(2,1)} %bias_ref.3, s32[4,512]{1,0:T(4,128)} %bitcast.46), custom_call_target="tpu_custom_call" | custom-call | flops 754974720 | bytes 6000000 | tf_op jit(solution)/shard_map/prepare/pallas_call | solution.py:458
  5.0 10.5 %all-to-all-start.3 = ((bf16[32,192,128]{2,1,0:T(8,128)(2,1)}), bf16[32,192,128]{2,1,0:T(8,128)(2,1)S(1)}, u32[]{:S(2)}, u32[]{:S(2)}) async-start(bf16[32,192,128]{2,1,0:T(8,128)(2,1)} %get-tuple-element.38), calls=%async_computation.3 | async-start | bytes 3145728 | tf_op jit(solution)/shard_map/all_to_all | solution.py:392
  15.5 1.8 %copy.64 = bf16[288,2048]{0,1:T(8,128)(2,1)S(1)} copy(bf16[288,2048]{1,0:T(8,128)(2,1)} %param.9) | data formatting | bytes 2359296 | tf_op args[2]
  17.3 0.0 copy-start.2
  17.3 1.1 copy-done.2
  18.5 0.8 slice.25
  19.3 1.3 slice.24.enc_ref
  20.6 1.3 copy.65
  21.9 0.2 reshape.54
  22.1 0.1 copy.66.rest_ref
  22.2 14.7 %all-to-all-done.3.recv_ref = bf16[32,192,128]{2,1,0:T(8,128)(2,1)S(1)} async-done(((bf16[32,192,128]{2,1,0:T(8,128)(2,1)}), bf16[32,192,128]{2,1,0:T(8,128)(2,1)S(1)}, u32[]{:S(2)}, u32[]{:S(2)}) %all-to-all-start.3) | async-done | bytes 1572896 | tf_op jit(solution)/shard_map/all_to_all | solution.py:392
  36.9 2.4 %encode.1 = (bf16[16,80,128]{2,1,0:T(8,128)(2,1)S(1)}, f32[24,128]{1,0:T(8,128)S(1)}, s32[1,1]{1,0:T(1,128)}) custom-call(bf16[32,192,128]{2,1,0:T(8,128)(2,1)S(1)} %all-to-all-done.3.recv_ref, bf16[2048,256]{1,0:T(8,128)(2,1)S(1)} %slice.24.enc_ref, bf16[256,256]{1,0:T(8,128)(2,1)S(1)} %copy.66.rest_ref), custom_call_target="tpu_custom_call" | custom-call | flops 3019898880 | bytes 6000000 | tf_op jit(solution)/shard_map/encode/pallas_call | solution.py:470
  39.3 12.3 %all_to_all.38 = bf16[4,320,128]{2,1,0:T(8,128)(2,1)S(1)} all-to-all(bf16[4,320,128]{2,1,0:T(8,128)(2,1)S(1)} %bitcast.35), channel_id=1, replica_groups=mesh['dp_outer'=4,'dp_inner'=4,'latent'=8,'section'=4] {'dp_inner'}, dimensions={0} | all-to-all | bytes 655360 | tf_op jit(solution)/shard_map/all_to_all | solution.py:397
  51.6 28.1 %all-reduce.3 = bf16[320,128]{1,0:T(8,128)(2,1)S(1)} all-reduce(f32[320,128]{1,0:T(8,128)S(1)} %convert_reduce_fusion.1), channel_id=1, replica_groups=mesh['dp_outer'=4,'dp_inner'=4,'latent'=8,'section'=4] {'dp_outer'}, use_global_device_ids=true, to_apply=%region_1.0 | all-reduce | flops 40960 | bytes 245760 | tf_op jit(solution)/shard_map/psum | solution.py:398
  79.8 10.0 %all_to_all.39 = bf16[4,320,128]{2,1,0:T(8,128)(2,1)S(1)} all-to-all(bf16[4,320,128]{2,1,0:T(8,128)(2,1)S(1)} %broadcast_in_dim.2), channel_id=1, replica_groups=mesh['dp_outer'=4,'dp_inner'=4,'latent'=8,'section'=4] {'dp_inner'}, dimensions={0} | all-to-all | bytes 655360 | tf_op jit(solution)/shard_map/all_to_all | solution.py:401
  89.8 3.6 %decode.1 = bf16[32,192,128]{2,1,0:T(8,128)(2,1)S(1)} custom-call(bf16[16,80,128]{2,1,0:T(8,128)(2,1)S(1)} %bitcast.44, f32[24,128]{1,0:T(8,128)S(1)} %get-tuple-element.41.ids_ref, bf16[288,2048]{1,0:T(8,128)(2,1)} %bitcast.42), custom_call_target="tpu_custom_call" | custom-call | flops 3019898880 | bytes 6000000 | tf_op jit(solution)/shard_map/decode/pallas_call | solution.py:480
  93.4 0.0 copy-start.4
  93.4 0.0 copy-start.5
  93.4 35.3 %all_to_all.40.recv_ref = bf16[32,192,128]{2,1,0:T(8,128)(2,1)S(1)} all-to-all(bf16[32,192,128]{2,1,0:T(8,128)(2,1)S(1)} %decode.1), channel_id=1, replica_groups=mesh['dp_outer'=4,'dp_inner'=4,'latent'=8,'section'=4] {'latent','section'}, dimensions={0} | all-to-all | bytes 3145728 | tf_op jit(solution)/shard_map/all_to_all | solution.py:392
  128.8 0.0 copy-done.4
  128.8 0.0 copy-done.5
  128.8 0.0 copy-start.3
  128.8 3.5 %combine.1 = (bf16[32,192,128]{2,1,0:T(8,128)(2,1)}, f32[4,128]{1,0:T(4,128)S(1)}) custom-call(bf16[32,192,128]{2,1,0:T(8,128)(2,1)S(1)} %all_to_all.40.recv_ref, s32[8,512]{1,0:T(8,128)S(1)} %get-tuple-element.42.slots_ref, bf16[288,512]{1,0:T(8,128)(2,1)S(1)} %bitcast.48, bf16[288]{0:T(512)(128)(2,1)S(1)} %copy-done.4), custom_call_target="tpu_custom_call" | custom-call | flops 1509949440 | bytes 6000000 | tf_op jit(solution)/shard_map/combine/pallas_call | solution.py:492
  132.3 4.4 %all-to-all-start.7 = ((bf16[32,192,128]{2,1,0:T(8,128)(2,1)}), bf16[32,192,128]{2,1,0:T(8,128)(2,1)S(1)}, u32[]{:S(2)}, u32[]{:S(2)}) async-start(bf16[32,192,128]{2,1,0:T(8,128)(2,1)} %get-tuple-element.43), calls=%async_computation.7 | async-start | bytes 3145728 | tf_op jit(solution)/shard_map/all_to_all | solution.py:392
  137.3 8.4 %psum.36 = f32[4,128]{1,0:T(4,128)S(1)} all-reduce(f32[4,128]{1,0:T(4,128)S(1)} %get-tuple-element.44), channel_id=1, replica_groups=mesh['dp_outer'=4,'dp_inner'=4,'latent'=8,'section'=4] {'dp_inner'}, use_global_device_ids=true, to_apply=%region_2.0 | all-reduce | flops 512 | bytes 4096 | tf_op jit(solution)/shard_map/psum | solution.py:405
  145.7 13.1 %psum.37 = f32[4,128]{1,0:T(4,128)S(1)} all-reduce(f32[4,128]{1,0:T(4,128)S(1)} %psum.36), channel_id=1, replica_groups=mesh['dp_outer'=4,'dp_inner'=4,'latent'=8,'section'=4] {'dp_outer'}, use_global_device_ids=true, to_apply=%region_3.0 | all-reduce | flops 512 | bytes 4096 | tf_op jit(solution)/shard_map/psum | solution.py:405
  158.8 0.0 all-to-all-done.7
  158.8 0.0 copy-done.3
  158.8 3.5 %conditional.1 = (f32[512]{0:T(512)}, bf16[2048,288]{0,1:T(8,128)(2,1)}) conditional(s32[]{:T(128)} %bitcast.18, (bf16[32,192,128]{2,1,0:T(8,128)(2,1)S(1)}, bf16[16,80,128]{2,1,0:T(8,128)(2,1)S(1)}, f32[24,128]{1,0:T(8,128)S(1)}, f32[4,128]{1,0:T(4,128)S(1)}) %tuple.45, (s32[512,4]{0,1:T(4,128)S(1)}, bf16[512,288]{0,1:T(8,128)(2,1)S(1)}, ...), branch_computations={%region_4.0_spmd, %region_5.0_spmd} | conditional | flops 4205791488 | bytes 89270392 | solution.py:521
  158.8 3.3 %gradient.1 = (bf16[288,2048]{1,0:T(8,128)(2,1)}, f32[4,128]{1,0:T(4,128)}) custom-call(bf16[32,192,128]{2,1,0:T(8,128)(2,1)S(1)} %get-tuple-element.18.recv_ref, bf16[16,80,128]{2,1,0:T(8,128)(2,1)S(1)} %get-tuple-element.19.codes_ref, f32[24,128]{1,0:T(8,128)S(1)} %get-tuple-element.20.ids_ref, f32[4,128]{1,0:T(4,128)S(1)} %get-tuple-element.21.loss_ref), custom_call_target="tpu_custom_call" | custom-call | flops 3019898880 | bytes 6000000 | tf_op jit(solution)/shard_map/cond/branch_0_fun/gradient/pallas_call | solution.py:505
  (3 shorter events, 0.1 us)
Async XLA Ops:
  5.0 32.0 %all-to-all-start.3 = ((bf16[32,192,128]{2,1,0:T(8,128)(2,1)}), bf16[32,192,128]{2,1,0:T(8,128)(2,1)S(1)}, u32[]{:S(2)}, u32[]{:S(2)}) async-start(bf16[32,192,128]{2,1,0:T(8,128)(2,1)} %get-tuple-element.38), calls=%async_computation.3 | async-start | bytes 3145728 | tf_op jit(solution)/shard_map/all_to_all | solution.py:392
  17.3 1.1 copy-start.2
  93.4 35.4 %copy-start.4 = (bf16[288]{0:T(512)(128)(2,1)S(1)}, bf16[288]{0:T(512)(128)(2,1)}, u32[]{:S(2)}) copy-start(bf16[288]{0:T(512)(128)(2,1)} %bias_ref.3) | copy-start | bytes 1732
  93.4 35.3 %copy-start.5 = (bf16[512,288]{0,1:T(8,128)(2,1)S(1)}, bf16[512,288]{0,1:T(8,128)(2,1)}, u32[]{:S(2)}) copy-start(bf16[512,288]{0,1:T(8,128)(2,1)} %param.7) | copy-start | bytes 884740
  128.8 30.0 %copy-start.3 = (s32[512,4]{0,1:T(4,128)S(1)}, s32[512,4]{0,1:T(4,128)}, u32[]{:S(2)}) copy-start(s32[512,4]{0,1:T(4,128)} %param.11) | copy-start | bytes 24580
  132.3 26.5 %all-to-all-start.7 = ((bf16[32,192,128]{2,1,0:T(8,128)(2,1)}), bf16[32,192,128]{2,1,0:T(8,128)(2,1)S(1)}, u32[]{:S(2)}, u32[]{:S(2)}) async-start(bf16[32,192,128]{2,1,0:T(8,128)(2,1)} %get-tuple-element.43), calls=%async_computation.7 | async-start | bytes 3145728 | tf_op jit(solution)/shard_map/all_to_all | solution.py:392

commit v6 on v5

--- a/solution.py
+++ b/solution.py
@@ -250,7 +250,7 @@
         main = tile < PAIRS // 2
         quarter = tile // 2 if main else 0
         first, held = (8 * quarter, 8) if main else (0, LOCAL)
-        part = mm(enc_ref[first * BLOCK : (first + held) * BLOCK, :], full_ref[0:256, lanes])
+        part = mm(enc_ref[first * BLOCK : (first + held) * BLOCK, 0:256], full_ref[0:256, lanes])
         total = jnp.zeros((BLOCK, 256), F32)
         for b in range(held):
             total = jnp.where(code == first + b, part[b * BLOCK : (b + 1) * BLOCK], total)
@@ -475,7 +475,7 @@
         "encode",
         20,
         out_specs=(vmem, vmem, pl.BlockSpec(memory_space=pltpu.SMEM)),
-    )(received, turned[:, :256], rest)
+    )(received, turned, rest)
     codes = sum_codes(partial)
     sent = call(
         decode_kernel,
@@ -487,7 +487,7 @@
         spread_flops,
         "decode",
         20,
-    )(codes, ids, decoder.T)
+    )(codes, ids, pltpu.with_memory_space_constraint(decoder.T, pltpu.VMEM))
     received = route(sent)
     sent, loss = call(
         combine_kernel,
@@ -515,7 +515,7 @@
             "gradient",
             24,
             out_specs=(hbm, vmem),
-        )(received, codes, ids, loss)
+        )(pltpu.with_memory_space_constraint(received, pltpu.VMEM), codes, ids, loss)
         return gradient.T, row_loss.reshape(ROWS)
 
     return lax.cond(

time: 165 us -> 165 us (level)
  waiting for transfers between devices: 14.7 us -> 17.2 us
    all_to_all x2, waiting for transfers between devices: 14.7 us -> 17.2 us  [route(): lax.all_to_all(buffer, PLANE, split_axis=0, concat_axis=0, tiled=True)]
    psum x2, blocking collectives: 21.5 us -> 19.1 us  [sum_loss(): return lax.psum(lax.psum(part, INNER), OUTER)]
  transfers between devices with their start and end apart: 2 -> 2, of which waited for: 1 -> 2; matrix products, arithmetic and copies ran while one was open for 3% -> 4% of each run, Pallas kernels for 0% -> 0%
where the time goes in v6:
time: 165 us; the launch traced here: 164 us
  blocking collectives  106 us (64%)
  waiting for transfers between devices  17.2 us (10%)
  Pallas kernels  15.7 us (10%)
  starting transfers between devices  15 us (9%)
  local copies, waits for them, and re-layouts  7.14 us (4%)
    all_to_all x1, blocking collectives, route(): lax.all_to_all(buffer, PLANE, split_axis=0, concat_axis=0, tiled=True)  36.8 us
    psum x1, blocking collectives, sum_codes(): total = lax.psum(jnp.sum(received.astype(F32), axis=0), OUTER)  28.1 us
    psum x2, blocking collectives, sum_loss(): return lax.psum(lax.psum(part, INNER), OUTER)  19.1 us
    all_to_all x2, waiting for transfers between devices, route(): lax.all_to_all(buffer, PLANE, split_axis=0, concat_axis=0, tiled=True)  17.2 us
    all_to_all x2, starting transfers between devices, route(): lax.all_to_all(buffer, PLANE, split_axis=0, concat_axis=0, tiled=True)  15 us
    all_to_all x1, blocking collectives, sum_codes(): lax.all_to_all(shares, INNER, split_axis=0, concat_axis=0, tiled=True)  12.3 us
    all_to_all x1, blocking collectives, sum_codes(): lax.all_to_all(copies, INNER, split_axis=0, concat_axis=0, tiled=True)  9.98 us
    pallas_call x1, Pallas kernels, on_device(): call(prepare_kernel, (packed, shape((8, ROWS), jnp.int32)), sending, 2 *...  4.32 us
  transfers between devices with their start and end apart: 2, of which 2 were waited for; matrix products, arithmetic and copies ran while one was open for 4% of the time, Pallas kernels for 0%

profile of v6, /device:TPU:1, one launch (start us, length us, event | category | flops | bytes accessed | tf_op | source)
XLA Modules:
  0.0 163.6 jit_solution(16670686748380071923)
XLA Ops:
  0.6 4.3 %prepare.1 = (bf16[32,192,128]{2,1,0:T(8,128)(2,1)}, s32[8,512]{1,0:T(8,128)S(1)}) custom-call(bf16[288,512]{1,0:T(8,128)(2,1)} %bitcast.47, bf16[288]{0:T(512)(128)(2,1)} %bias_ref.3, s32[4,512]{1,0:T(4,128)} %bitcast.46), custom_call_target="tpu_custom_call" | custom-call | flops 754974720 | bytes 6000000 | tf_op jit(solution)/shard_map/prepare/pallas_call | solution.py:458
  5.0 10.5 %all-to-all-start.3 = ((bf16[32,192,128]{2,1,0:T(8,128)(2,1)}), bf16[32,192,128]{2,1,0:T(8,128)(2,1)S(1)}, u32[]{:S(2)}, u32[]{:S(2)}) async-start(bf16[32,192,128]{2,1,0:T(8,128)(2,1)} %get-tuple-element.38), calls=%async_computation.3 | async-start | bytes 3145728 | tf_op jit(solution)/shard_map/all_to_all | solution.py:392
  15.5 1.8 %copy.64 = bf16[288,2048]{0,1:T(8,128)(2,1)S(1)} copy(bf16[288,2048]{1,0:T(8,128)(2,1)} %param.9) | data formatting | bytes 2359296 | tf_op args[2]
  17.3 0.8 slice.20
  18.1 1.3 copy.65
  19.4 0.9 reshape.54
  20.3 1.0 copy.66.rest_ref
  21.3 15.6 %all-to-all-done.3.recv_ref = bf16[32,192,128]{2,1,0:T(8,128)(2,1)S(1)} async-done(((bf16[32,192,128]{2,1,0:T(8,128)(2,1)}), bf16[32,192,128]{2,1,0:T(8,128)(2,1)S(1)}, u32[]{:S(2)}, u32[]{:S(2)}) %all-to-all-start.3) | async-done | bytes 1572896 | tf_op jit(solution)/shard_map/all_to_all | solution.py:392
  36.9 2.4 %encode.1 = (bf16[16,80,128]{2,1,0:T(8,128)(2,1)S(1)}, f32[24,128]{1,0:T(8,128)S(1)}, s32[1,1]{1,0:T(1,128)}) custom-call(bf16[32,192,128]{2,1,0:T(8,128)(2,1)S(1)} %all-to-all-done.3.recv_ref, bf16[2048,288]{1,0:T(8,128)(2,1)S(1)} %bitcast.36, bf16[256,256]{1,0:T(8,128)(2,1)S(1)} %copy.66.rest_ref), custom_call_target="tpu_custom_call" | custom-call | flops 3019898880 | bytes 6000000 | tf_op jit(solution)/shard_map/encode/pallas_call | solution.py:470
  39.3 12.3 %all_to_all.38 = bf16[4,320,128]{2,1,0:T(8,128)(2,1)S(1)} all-to-all(bf16[4,320,128]{2,1,0:T(8,128)(2,1)S(1)} %bitcast.38), channel_id=1, replica_groups=mesh['dp_outer'=4,'dp_inner'=4,'latent'=8,'section'=4] {'dp_inner'}, dimensions={0} | all-to-all | bytes 655360 | tf_op jit(solution)/shard_map/all_to_all | solution.py:397
  51.6 28.1 %all-reduce.3 = bf16[320,128]{1,0:T(8,128)(2,1)S(1)} all-reduce(f32[320,128]{1,0:T(8,128)S(1)} %convert_reduce_fusion.1), channel_id=1, replica_groups=mesh['dp_outer'=4,'dp_inner'=4,'latent'=8,'section'=4] {'dp_outer'}, use_global_device_ids=true, to_apply=%region_1.0 | all-reduce | flops 40960 | bytes 245760 | tf_op jit(solution)/shard_map/psum | solution.py:398
  79.8 10.0 %all_to_all.39 = bf16[4,320,128]{2,1,0:T(8,128)(2,1)S(1)} all-to-all(bf16[4,320,128]{2,1,0:T(8,128)(2,1)S(1)} %broadcast_in_dim.2), channel_id=1, replica_groups=mesh['dp_outer'=4,'dp_inner'=4,'latent'=8,'section'=4] {'dp_inner'}, dimensions={0} | all-to-all | bytes 655360 | tf_op jit(solution)/shard_map/all_to_all | solution.py:401
  89.8 0.0 copy-start
  89.8 1.3 copy-done
  91.1 2.3 %decode.1 = bf16[32,192,128]{2,1,0:T(8,128)(2,1)S(1)} custom-call(bf16[16,80,128]{2,1,0:T(8,128)(2,1)S(1)} %bitcast.44, f32[24,128]{1,0:T(8,128)S(1)} %get-tuple-element.41.ids_ref, bf16[288,2048]{1,0:T(8,128)(2,1)S(1)} %bitcast.37), custom_call_target="tpu_custom_call" | custom-call | flops 3019898880 | bytes 6000000 | tf_op jit(solution)/shard_map/decode/pallas_call | solution.py:480
  93.4 0.0 copy-start.5
  93.4 0.0 copy-start.6
  93.4 36.8 %all_to_all.40.recv_ref = bf16[32,192,128]{2,1,0:T(8,128)(2,1)S(1)} all-to-all(bf16[32,192,128]{2,1,0:T(8,128)(2,1)S(1)} %decode.1), channel_id=1, replica_groups=mesh['dp_outer'=4,'dp_inner'=4,'latent'=8,'section'=4] {'latent','section'}, dimensions={0} | all-to-all | bytes 3145728 | tf_op jit(solution)/shard_map/all_to_all | solution.py:392
  130.2 0.0 copy-done.5
  130.2 0.0 copy-done.6
  130.2 0.0 copy-start.1
  130.2 3.5 %combine.1 = (bf16[32,192,128]{2,1,0:T(8,128)(2,1)}, f32[4,128]{1,0:T(4,128)S(1)}) custom-call(bf16[32,192,128]{2,1,0:T(8,128)(2,1)S(1)} %all_to_all.40.recv_ref, s32[8,512]{1,0:T(8,128)S(1)} %get-tuple-element.42.slots_ref, bf16[288,512]{1,0:T(8,128)(2,1)S(1)} %bitcast.48, bf16[288]{0:T(512)(128)(2,1)S(1)} %copy-done.5), custom_call_target="tpu_custom_call" | custom-call | flops 1509949440 | bytes 6000000 | tf_op jit(solution)/shard_map/combine/pallas_call | solution.py:492
  133.7 0.0 copy-start.7
  133.7 4.5 %all-to-all-start.7 = ((bf16[32,192,128]{2,1,0:T(8,128)(2,1)}), bf16[32,192,128]{2,1,0:T(8,128)(2,1)S(1)}, u32[]{:S(2)}, u32[]{:S(2)}) async-start(bf16[32,192,128]{2,1,0:T(8,128)(2,1)} %get-tuple-element.43), calls=%async_computation.7 | async-start | bytes 3145728 | tf_op jit(solution)/shard_map/all_to_all | solution.py:392
  138.9 8.4 %psum.36 = f32[4,128]{1,0:T(4,128)S(1)} all-reduce(f32[4,128]{1,0:T(4,128)S(1)} %get-tuple-element.44), channel_id=1, replica_groups=mesh['dp_outer'=4,'dp_inner'=4,'latent'=8,'section'=4] {'dp_inner'}, use_global_device_ids=true, to_apply=%region_2.0 | all-reduce | flops 512 | bytes 4096 | tf_op jit(solution)/shard_map/psum | solution.py:405
  147.3 10.7 %psum.37 = f32[4,128]{1,0:T(4,128)S(1)} all-reduce(f32[4,128]{1,0:T(4,128)S(1)} %psum.36), channel_id=1, replica_groups=mesh['dp_outer'=4,'dp_inner'=4,'latent'=8,'section'=4] {'dp_outer'}, use_global_device_ids=true, to_apply=%region_3.0 | all-reduce | flops 512 | bytes 4096 | tf_op jit(solution)/shard_map/psum | solution.py:405
  158.0 1.6 all-to-all-done.7
  159.6 0.0 copy-done.1
  159.6 0.0 copy-done.4
  159.6 0.0 copy-done.7
  159.6 3.7 %conditional.1 = (f32[512]{0:T(512)}, bf16[2048,288]{0,1:T(8,128)(2,1)}) conditional(s32[]{:T(128)} %bitcast.18, (bf16[32,192,128]{2,1,0:T(8,128)(2,1)S(1)}, bf16[16,80,128]{2,1,0:T(8,128)(2,1)S(1)}, f32[24,128]{1,0:T(8,128)S(1)}, f32[4,128]{1,0:T(4,128)S(1)}) %tuple.46, (s32[512,4]{0,1:T(4,128)S(1)}, bf16[512,288]{0,1:T(8,128)(2,1)S(1)}, ...), branch_computations={%region_4.0_spmd, %region_5.0_spmd} | conditional | flops 4205791488 | bytes 86911048 | solution.py:521
  159.8 3.3 %gradient.1 = (bf16[288,2048]{1,0:T(8,128)(2,1)}, f32[4,128]{1,0:T(4,128)}) custom-call(bf16[32,192,128]{2,1,0:T(8,128)(2,1)S(1)} %get-tuple-element.18.recv_ref, bf16[16,80,128]{2,1,0:T(8,128)(2,1)S(1)} %get-tuple-element.19.codes_ref, f32[24,128]{1,0:T(8,128)S(1)} %get-tuple-element.20.ids_ref, f32[4,128]{1,0:T(4,128)S(1)} %get-tuple-element.21.loss_ref), custom_call_target="tpu_custom_call" | custom-call | flops 3019898880 | bytes 6000000 | tf_op jit(solution)/shard_map/cond/branch_0_fun/gradient/pallas_call | solution.py:505
  (4 shorter events, 0.1 us)
Async XLA Ops:
  5.0 32.0 %all-to-all-start.3 = ((bf16[32,192,128]{2,1,0:T(8,128)(2,1)}), bf16[32,192,128]{2,1,0:T(8,128)(2,1)S(1)}, u32[]{:S(2)}, u32[]{:S(2)}) async-start(bf16[32,192,128]{2,1,0:T(8,128)(2,1)} %get-tuple-element.38), calls=%async_computation.3 | async-start | bytes 3145728 | tf_op jit(solution)/shard_map/all_to_all | solution.py:392
  89.8 1.3 copy-start
  93.4 36.8 %copy-start.5 = (bf16[288]{0:T(512)(128)(2,1)S(1)}, bf16[288]{0:T(512)(128)(2,1)}, u32[]{:S(2)}) copy-start(bf16[288]{0:T(512)(128)(2,1)} %bias_ref.3) | copy-start | bytes 1732
  93.4 36.8 %copy-start.6 = (bf16[512,288]{0,1:T(8,128)(2,1)S(1)}, bf16[512,288]{0,1:T(8,128)(2,1)}, u32[]{:S(2)}) copy-start(bf16[512,288]{0,1:T(8,128)(2,1)} %param.7) | copy-start | bytes 884740
  130.2 29.4 %copy-start.1 = (bf16[2048,288]{0,1:T(8,128)(2,1)S(1)}, bf16[2048,288]{0,1:T(8,128)(2,1)}, u32[]{:S(2)}) copy-start(bf16[2048,288]{0,1:T(8,128)(2,1)} %param.10) | copy-start | bytes 3538948
  130.2 29.4 %copy-start.4 = (s32[512,4]{0,1:T(4,128)S(1)}, s32[512,4]{0,1:T(4,128)}, u32[]{:S(2)}) copy-start(s32[512,4]{0,1:T(4,128)} %param.11) | copy-start | bytes 24580
  133.7 25.9 %copy-start.7 = (bf16[512,288]{0,1:T(8,128)(2,1)S(1)}, bf16[512,288]{0,1:T(8,128)(2,1)}, u32[]{:S(2)}) copy-start(bf16[512,288]{0,1:T(8,128)(2,1)} %param.7) | copy-start | bytes 884740
  133.7 25.9 %all-to-all-start.7 = ((bf16[32,192,128]{2,1,0:T(8,128)(2,1)}), bf16[32,192,128]{2,1,0:T(8,128)(2,1)S(1)}, u32[]{:S(2)}, u32[]{:S(2)}) async-start(bf16[32,192,128]{2,1,0:T(8,128)(2,1)} %get-tuple-element.43), calls=%async_computation.7 | async-start | bytes 3145728 | tf_op jit(solution)/shard_map/all_to_all | solution.py:392

commit v7 on v6

--- a/solution.py
+++ b/solution.py
@@ -284,7 +284,14 @@
             ]
 
 
-def decode_kernel(codes_ref, ids_ref, dec_ref, send_ref, full_ref, extra_ref):
+def decode_kernel(codes_ref, ids_ref, weights_ref, send_ref, full_ref, extra_ref, dec_ref, sems):
+    fetches = []
+    for quarter in range(QUARTERS):
+        lanes = pl.ds(quarter * 8 * BLOCK, 8 * BLOCK)
+        fetches.append(
+            pltpu.make_async_copy(weights_ref.at[:, lanes], dec_ref.at[:, lanes], sems.at[quarter])
+        )
+        fetches[-1].start()
     load_codes(codes_ref, full_ref)
 
     def contribution(tile):
@@ -297,13 +304,12 @@
         weights = dec_ref[:, first * BLOCK : (first + held) * BLOCK]
         return mm(weights, jnp.concatenate(spread, axis=0)).astype(BF16)
 
-    extra_ref[FEATURES:, :] = jnp.zeros((384 - FEATURES, EXTRA_SLOTS), BF16)
-    for tile in range(PAIRS // 2, LANE_TILES // 2):
-        start = tile * 256 - MAIN_SLOTS
-        extra_ref[0:FEATURES, start : start + 256] = contribution(tile)
-    store_extra(send_ref, mm_nt(identity(EXTRA_SLOTS), extra_ref[...]))
     for double in range(2):
-        values = [contribution(2 * quarter + double) for quarter in range(QUARTERS)]
+        values = []
+        for quarter in range(QUARTERS):
+            if double == 0:
+                fetches[quarter].wait()
+            values.append(contribution(2 * quarter + double))
         for side in range(2):
             lanes = slice(side * 128, (side + 1) * 128)
             tops = ungroup([value[:HALF, lanes] for value in values])
@@ -313,6 +319,11 @@
                 first, second = exchange(tops[j], bottoms[j], MAIN)
                 send_ref[pair, 0:HALF, :] = first
                 send_ref[pair + PAIRS, 0:HALF, :] = second
+    extra_ref[FEATURES:, :] = jnp.zeros((384 - FEATURES, EXTRA_SLOTS), BF16)
+    for tile in range(PAIRS // 2, LANE_TILES // 2):
+        start = tile * 256 - MAIN_SLOTS
+        extra_ref[0:FEATURES, start : start + 256] = contribution(tile)
+    store_extra(send_ref, mm_nt(identity(EXTRA_SLOTS), extra_ref[...]))
 
 
 def combine_kernel(
@@ -402,7 +413,7 @@
 
 
 def sum_loss(part):
-    return lax.psum(lax.psum(part, INNER), OUTER)
+    return lax.psum(lax.psum(part, OUTER), INNER)
 
 
 def padded_plan(activations, bias_dec, encoder, decoder, active_blocks):
@@ -483,11 +494,14 @@
         [
             pltpu.VMEM((BLOCK, SLOTS), BF16),
             pltpu.VMEM((384, EXTRA_SLOTS), BF16),
+            pltpu.VMEM((FEATURES, LOCAL * BLOCK), BF16),
+            pltpu.SemaphoreType.DMA((QUARTERS,)),
         ],
         spread_flops,
         "decode",
         20,
-    )(codes, ids, pltpu.with_memory_space_constraint(decoder.T, pltpu.VMEM))
+        in_specs=(vmem, vmem, hbm),
+    )(codes, ids, decoder.T)
     received = route(sent)
     sent, loss = call(
         combine_kernel,

time: 165 us -> 165 us (level)
  local copies, waits for them, and re-layouts: 7.14 us -> 4.3 us
  transfers between devices with their start and end apart: 2 -> 2, of which waited for: 2 -> 2; matrix products, arithmetic and copies ran while one was open for 4% -> 3% of each run, Pallas kernels for 0% -> 0%
where the time goes in v7:
time: 165 us; the launch traced here: 163 us
  blocking collectives  106 us (64%)
  waiting for transfers between devices  18.7 us (11%)
  Pallas kernels  16.9 us (10%)
  starting transfers between devices  14.9 us (9%)
  local copies, waits for them, and re-layouts  4.3 us (3%)
    all_to_all x1, blocking collectives, route(): lax.all_to_all(buffer, PLANE, split_axis=0, concat_axis=0, tiled=True)  36.8 us
    psum x1, blocking collectives, sum_codes(): total = lax.psum(jnp.sum(received.astype(F32), axis=0), OUTER)  28.1 us
    psum x2, blocking collectives, sum_loss(): return lax.psum(lax.psum(part, OUTER), INNER)  19.2 us
    all_to_all x2, waiting for transfers between devices, route(): lax.all_to_all(buffer, PLANE, split_axis=0, concat_axis=0, tiled=True)  18.7 us
    all_to_all x2, starting transfers between devices, route(): lax.all_to_all(buffer, PLANE, split_axis=0, concat_axis=0, tiled=True)  14.9 us
    all_to_all x1, blocking collectives, sum_codes(): lax.all_to_all(shares, INNER, split_axis=0, concat_axis=0, tiled=True)  12.3 us
    all_to_all x1, blocking collectives, sum_codes(): lax.all_to_all(copies, INNER, split_axis=0, concat_axis=0, tiled=True)  9.98 us
    pallas_call x1, Pallas kernels, on_device(): call(prepare_kernel, (packed, shape((8, ROWS), jnp.int32)), sending, 2 *...  4.32 us
  transfers between devices with their start and end apart: 2, of which 2 were waited for; matrix products, arithmetic and copies ran while one was open for 3% of the time, Pallas kernels for 0%

profile of v7, /device:TPU:1, one launch (start us, length us, event | category | flops | bytes accessed | tf_op | source)
XLA Modules:
  0.0 163.0 jit_solution(17681147184325357460)
XLA Ops:
  0.6 4.3 %prepare.1 = (bf16[32,192,128]{2,1,0:T(8,128)(2,1)}, s32[8,512]{1,0:T(8,128)S(1)}) custom-call(bf16[288,512]{1,0:T(8,128)(2,1)} %bitcast.47, bf16[288]{0:T(512)(128)(2,1)} %bias_ref.3, s32[4,512]{1,0:T(4,128)} %bitcast.46), custom_call_target="tpu_custom_call" | custom-call | flops 754974720 | bytes 6000000 | tf_op jit(solution)/shard_map/prepare/pallas_call | solution.py:469
  5.0 10.5 %all-to-all-start.3 = ((bf16[32,192,128]{2,1,0:T(8,128)(2,1)}), bf16[32,192,128]{2,1,0:T(8,128)(2,1)S(1)}, u32[]{:S(2)}, u32[]{:S(2)}) async-start(bf16[32,192,128]{2,1,0:T(8,128)(2,1)} %get-tuple-element.38), calls=%async_computation.3 | async-start | bytes 3145728 | tf_op jit(solution)/shard_map/all_to_all | solution.py:403
  15.5 1.8 %copy.64 = bf16[288,2048]{0,1:T(8,128)(2,1)S(1)} copy(bf16[288,2048]{1,0:T(8,128)(2,1)} %param.9) | data formatting | bytes 2359296 | tf_op args[2]
  17.3 0.8 slice.20
  18.1 1.3 copy.65
  19.4 0.2 reshape.54
  19.6 0.1 copy.66.rest_ref
  19.8 17.2 %all-to-all-done.3.recv_ref = bf16[32,192,128]{2,1,0:T(8,128)(2,1)S(1)} async-done(((bf16[32,192,128]{2,1,0:T(8,128)(2,1)}), bf16[32,192,128]{2,1,0:T(8,128)(2,1)S(1)}, u32[]{:S(2)}, u32[]{:S(2)}) %all-to-all-start.3) | async-done | bytes 1572896 | tf_op jit(solution)/shard_map/all_to_all | solution.py:403
  36.9 2.4 %encode.1 = (bf16[16,80,128]{2,1,0:T(8,128)(2,1)S(1)}, f32[24,128]{1,0:T(8,128)S(1)}, s32[1,1]{1,0:T(1,128)}) custom-call(bf16[32,192,128]{2,1,0:T(8,128)(2,1)S(1)} %all-to-all-done.3.recv_ref, bf16[2048,288]{1,0:T(8,128)(2,1)S(1)} %bitcast.36, bf16[256,256]{1,0:T(8,128)(2,1)S(1)} %copy.66.rest_ref), custom_call_target="tpu_custom_call" | custom-call | flops 3019898880 | bytes 6000000 | tf_op jit(solution)/shard_map/encode/pallas_call | solution.py:481
  39.3 12.3 %all_to_all.38 = bf16[4,320,128]{2,1,0:T(8,128)(2,1)S(1)} all-to-all(bf16[4,320,128]{2,1,0:T(8,128)(2,1)S(1)} %bitcast.37), channel_id=1, replica_groups=mesh['dp_outer'=4,'dp_inner'=4,'latent'=8,'section'=4] {'dp_inner'}, dimensions={0} | all-to-all | bytes 655360 | tf_op jit(solution)/shard_map/all_to_all | solution.py:408
  51.6 28.1 %all-reduce.3 = bf16[320,128]{1,0:T(8,128)(2,1)S(1)} all-reduce(f32[320,128]{1,0:T(8,128)S(1)} %convert_reduce_fusion.1), channel_id=1, replica_groups=mesh['dp_outer'=4,'dp_inner'=4,'latent'=8,'section'=4] {'dp_outer'}, use_global_device_ids=true, to_apply=%region_1.0 | all-reduce | flops 40960 | bytes 245760 | tf_op jit(solution)/shard_map/psum | solution.py:409
  79.8 10.0 %all_to_all.39 = bf16[4,320,128]{2,1,0:T(8,128)(2,1)S(1)} all-to-all(bf16[4,320,128]{2,1,0:T(8,128)(2,1)S(1)} %broadcast_in_dim.2), channel_id=1, replica_groups=mesh['dp_outer'=4,'dp_inner'=4,'latent'=8,'section'=4] {'dp_inner'}, dimensions={0} | all-to-all | bytes 655360 | tf_op jit(solution)/shard_map/all_to_all | solution.py:412
  89.8 3.5 %decode.1 = bf16[32,192,128]{2,1,0:T(8,128)(2,1)S(1)} custom-call(bf16[16,80,128]{2,1,0:T(8,128)(2,1)S(1)} %bitcast.44, f32[24,128]{1,0:T(8,128)S(1)} %get-tuple-element.41.ids_ref, bf16[288,2048]{1,0:T(8,128)(2,1)} %bitcast.42), custom_call_target="tpu_custom_call" | custom-call | flops 3019898880 | bytes 6000000 | tf_op jit(solution)/shard_map/decode/pallas_call | solution.py:491
  93.3 0.0 copy-start.3
  93.3 0.0 copy-start.4
  93.3 36.8 %all_to_all.40.recv_ref = bf16[32,192,128]{2,1,0:T(8,128)(2,1)S(1)} all-to-all(bf16[32,192,128]{2,1,0:T(8,128)(2,1)S(1)} %decode.1), channel_id=1, replica_groups=mesh['dp_outer'=4,'dp_inner'=4,'latent'=8,'section'=4] {'latent','section'}, dimensions={0} | all-to-all | bytes 3145728 | tf_op jit(solution)/shard_map/all_to_all | solution.py:403
  130.1 0.0 copy-done.3
  130.1 0.0 copy-done.4
  130.1 0.0 copy-start.2
  130.1 3.5 %combine.1 = (bf16[32,192,128]{2,1,0:T(8,128)(2,1)}, f32[4,128]{1,0:T(4,128)S(1)}) custom-call(bf16[32,192,128]{2,1,0:T(8,128)(2,1)S(1)} %all_to_all.40.recv_ref, s32[8,512]{1,0:T(8,128)S(1)} %get-tuple-element.42.slots_ref, bf16[288,512]{1,0:T(8,128)(2,1)S(1)} %bitcast.48, bf16[288]{0:T(512)(128)(2,1)S(1)} %copy-done.3), custom_call_target="tpu_custom_call" | custom-call | flops 1509949440 | bytes 6000000 | tf_op jit(solution)/shard_map/combine/pallas_call | solution.py:506
  133.6 4.4 %all-to-all-start.7 = ((bf16[32,192,128]{2,1,0:T(8,128)(2,1)}), bf16[32,192,128]{2,1,0:T(8,128)(2,1)S(1)}, u32[]{:S(2)}, u32[]{:S(2)}) async-start(bf16[32,192,128]{2,1,0:T(8,128)(2,1)} %get-tuple-element.43), calls=%async_computation.7 | async-start | bytes 3145728 | tf_op jit(solution)/shard_map/all_to_all | solution.py:403
  138.6 10.8 %psum.36 = f32[4,128]{1,0:T(4,128)S(1)} all-reduce(f32[4,128]{1,0:T(4,128)S(1)} %get-tuple-element.44), channel_id=1, replica_groups=mesh['dp_outer'=4,'dp_inner'=4,'latent'=8,'section'=4] {'dp_outer'}, use_global_device_ids=true, to_apply=%region_2.0 | all-reduce | flops 512 | bytes 4096 | tf_op jit(solution)/shard_map/psum | solution.py:416
  149.4 8.4 %psum.37 = f32[4,128]{1,0:T(4,128)S(1)} all-reduce(f32[4,128]{1,0:T(4,128)S(1)} %psum.36), channel_id=1, replica_groups=mesh['dp_outer'=4,'dp_inner'=4,'latent'=8,'section'=4] {'dp_inner'}, use_global_device_ids=true, to_apply=%region_3.0 | all-reduce | flops 512 | bytes 4096 | tf_op jit(solution)/shard_map/psum | solution.py:416
  157.8 1.6 all-to-all-done.7
  159.4 0.0 copy-done.2
  159.4 3.5 %conditional.1 = (f32[512]{0:T(512)}, bf16[2048,288]{0,1:T(8,128)(2,1)}) conditional(s32[]{:T(128)} %bitcast.18, (bf16[32,192,128]{2,1,0:T(8,128)(2,1)S(1)}, bf16[16,80,128]{2,1,0:T(8,128)(2,1)S(1)}, f32[24,128]{1,0:T(8,128)S(1)}, f32[4,128]{1,0:T(4,128)S(1)}) %tuple.45, (s32[512,4]{0,1:T(4,128)S(1)}, bf16[512,288]{0,1:T(8,128)(2,1)S(1)}, ...), branch_computations={%region_4.0_spmd, %region_5.0_spmd} | conditional | flops 4205791488 | bytes 89270392 | solution.py:535
  159.4 3.2 %gradient.1 = (bf16[288,2048]{1,0:T(8,128)(2,1)}, f32[4,128]{1,0:T(4,128)}) custom-call(bf16[32,192,128]{2,1,0:T(8,128)(2,1)S(1)} %get-tuple-element.18.recv_ref, bf16[16,80,128]{2,1,0:T(8,128)(2,1)S(1)} %get-tuple-element.19.codes_ref, f32[24,128]{1,0:T(8,128)S(1)} %get-tuple-element.20.ids_ref, f32[4,128]{1,0:T(4,128)S(1)} %get-tuple-element.21.loss_ref), custom_call_target="tpu_custom_call" | custom-call | flops 3019898880 | bytes 6000000 | tf_op jit(solution)/shard_map/cond/branch_0_fun/gradient/pallas_call | solution.py:519
  (3 shorter events, 0.1 us)
Async XLA Ops:
  5.0 32.0 %all-to-all-start.3 = ((bf16[32,192,128]{2,1,0:T(8,128)(2,1)}), bf16[32,192,128]{2,1,0:T(8,128)(2,1)S(1)}, u32[]{:S(2)}, u32[]{:S(2)}) async-start(bf16[32,192,128]{2,1,0:T(8,128)(2,1)} %get-tuple-element.38), calls=%async_computation.3 | async-start | bytes 3145728 | tf_op jit(solution)/shard_map/all_to_all | solution.py:403
  93.3 36.8 %copy-start.3 = (bf16[288]{0:T(512)(128)(2,1)S(1)}, bf16[288]{0:T(512)(128)(2,1)}, u32[]{:S(2)}) copy-start(bf16[288]{0:T(512)(128)(2,1)} %bias_ref.3) | copy-start | bytes 1732
  93.3 36.8 %copy-start.4 = (bf16[512,288]{0,1:T(8,128)(2,1)S(1)}, bf16[512,288]{0,1:T(8,128)(2,1)}, u32[]{:S(2)}) copy-start(bf16[512,288]{0,1:T(8,128)(2,1)} %param.7) | copy-start | bytes 884740
  130.1 29.3 %copy-start.2 = (s32[512,4]{0,1:T(4,128)S(1)}, s32[512,4]{0,1:T(4,128)}, u32[]{:S(2)}) copy-start(s32[512,4]{0,1:T(4,128)} %param.11) | copy-start | bytes 24580
  133.6 25.8 %all-to-all-start.7 = ((bf16[32,192,128]{2,1,0:T(8,128)(2,1)}), bf16[32,192,128]{2,1,0:T(8,128)(2,1)S(1)}, u32[]{:S(2)}, u32[]{:S(2)}) async-start(bf16[32,192,128]{2,1,0:T(8,128)(2,1)} %get-tuple-element.43), calls=%async_computation.7 | async-start | bytes 3145728 | tf_op jit(solution)/shard_map/all_to_all | solution.py:403

commit v8 on v6

--- a/solution.py
+++ b/solution.py
@@ -25,7 +25,7 @@
 SLOTS = MAIN_SLOTS + EXTRA_SLOTS
 PACKED = HALF + 3 * EXTRA
 PAIRS = GROUPS // 2
-EARLY = 12
+STAGE = 4
 LANE_TILES = SLOTS // 128
 CHUNK_TILES = 5
 CHUNK_ROWS = 16 * CHUNK_TILES
@@ -78,26 +78,25 @@
     out_ref[pair + PAIRS, 0:HALF, :] = second
 
 
-def stage_copies(buffer_ref, out_ref, sems, stage, early):
-    first, count = (0, early) if stage == 0 else (early, PAIRS - early)
+def stage_copies(buffer_ref, out_ref, sems, stage):
     copies = []
     for side in range(2):
-        devices = pl.ds(side * PAIRS + first, count)
+        devices = pl.ds(side * PAIRS + stage * STAGE, STAGE)
         copies.append(
             pltpu.make_async_copy(buffer_ref.at[devices], out_ref.at[devices], sems.at[2 * stage + side])
         )
     return copies
 
 
-def start_stage(buffer_ref, out_ref, sems, done, early=EARLY):
-    if done in (early, PAIRS):
-        for copy in stage_copies(buffer_ref, out_ref, sems, 0 if done == early else 1, early):
+def start_stage(buffer_ref, out_ref, sems, done):
+    if done % STAGE == 0:
+        for copy in stage_copies(buffer_ref, out_ref, sems, done // STAGE - 1):
             copy.start()
 
 
-def wait_stages(buffer_ref, out_ref, sems, early=EARLY):
-    for stage in range(2):
-        for copy in stage_copies(buffer_ref, out_ref, sems, stage, early):
+def wait_stages(buffer_ref, out_ref, sems):
+    for stage in range(PAIRS // STAGE):
+        for copy in stage_copies(buffer_ref, out_ref, sems, stage):
             copy.wait()
 
 
@@ -163,9 +162,13 @@
     count = GROUPS * QUARTERS
     groups = lax.broadcasted_iota(jnp.int32, (count, ROWS), 0)
     hits = [groups == group[k : k + 1, :] for k in range(NAMED)]
-    counts = sum(jnp.where(hit, 1.0, 0.0) for hit in hits).astype(BF16)
-    before = lax.broadcasted_iota(jnp.int32, (ROWS, ROWS), 0) < lax.broadcasted_iota(jnp.int32, (ROWS, ROWS), 1)
-    earlier = mm(counts, jnp.where(before, 1.0, 0.0).astype(BF16))
+    small = lax.broadcasted_iota(jnp.int16, (count, ROWS), 0)
+    counts = jnp.zeros((count, ROWS), BF16)
+    for k in range(NAMED):
+        hit = small == jnp.broadcast_to(group[k : k + 1, :].astype(jnp.int16), small.shape)
+        counts = counts + jnp.where(hit, BF16(1), BF16(0))
+    before = lax.broadcasted_iota(jnp.int16, (ROWS, ROWS), 0) < lax.broadcasted_iota(jnp.int16, (ROWS, ROWS), 1)
+    earlier = mm(counts, jnp.where(before, BF16(1), BF16(0)))
     beyond = jnp.maximum(mm(counts, jnp.ones((ROWS, 128), BF16)) - SHARE, 0.0).astype(BF16)
     one = lax.broadcasted_iota(jnp.int32, (count, count), 0)
     other = lax.broadcasted_iota(jnp.int32, (count, count), 1)
@@ -392,17 +395,35 @@
     return lax.all_to_all(buffer, PLANE, split_axis=0, concat_axis=0, tiled=True)
 
 
-def sum_codes(partial):
+def fetch_kernel(weights_ref, held_ref, sem):
+    copy = pltpu.make_async_copy(weights_ref, held_ref, sem)
+    copy.start()
+    copy.wait()
+
+
+def sum_codes(partial, weights):
     shares = partial.reshape(4, SHARDS // 4 * CHUNK_ROWS, 128)
     received = lax.all_to_all(shares, INNER, split_axis=0, concat_axis=0, tiled=True)
     total = lax.psum(jnp.sum(received.astype(F32), axis=0), OUTER)
     codes = jnp.maximum(total, 0.0).astype(BF16)
+    codes, weights = lax.optimization_barrier((codes, weights))
     copies = jnp.broadcast_to(codes[None], shares.shape)
-    return lax.all_to_all(copies, INNER, split_axis=0, concat_axis=0, tiled=True).reshape(partial.shape)
+    codes = lax.all_to_all(copies, INNER, split_axis=0, concat_axis=0, tiled=True)
+    held = call(
+        fetch_kernel,
+        pltpu.VMEM(weights.shape, BF16),
+        [pltpu.SemaphoreType.DMA],
+        0,
+        "fetch",
+        4,
+        in_specs=[pl.BlockSpec(memory_space=pltpu.HBM)],
+        out_specs=pl.BlockSpec(memory_space=pltpu.VMEM),
+    )(weights)
+    return codes.reshape(partial.shape), held
 
 
 def sum_loss(part):
-    return lax.psum(lax.psum(part, INNER), OUTER)
+    return lax.psum(lax.psum(part, OUTER), INNER)
 
 
 def padded_plan(activations, bias_dec, encoder, decoder, active_blocks):
@@ -452,7 +473,7 @@
     bias = bias_dec
     packed = in_hbm((GROUPS, PACKED, 128))
     full = pltpu.VMEM((FEATURES, SLOTS), BF16)
-    sending = [pltpu.VMEM((GROUPS, PACKED, 128), BF16), pltpu.SemaphoreType.DMA((4,))]
+    sending = [pltpu.VMEM((GROUPS, PACKED, 128), BF16), pltpu.SemaphoreType.DMA((2 * PAIRS // STAGE,))]
     vmem, hbm = pl.BlockSpec(memory_space=pltpu.VMEM), pl.BlockSpec(memory_space=pltpu.HBM)
     spread_flops = 2 * FEATURES * SLOTS * LOCAL * BLOCK
     sent, slots = call(
@@ -476,7 +497,7 @@
         20,
         out_specs=(vmem, vmem, pl.BlockSpec(memory_space=pltpu.SMEM)),
     )(received, turned, rest)
-    codes = sum_codes(partial)
+    codes, weights = sum_codes(partial, decoder.T)
     sent = call(
         decode_kernel,
         shape((GROUPS, PACKED, 128)),
@@ -487,7 +508,7 @@
         spread_flops,
         "decode",
         20,
-    )(codes, ids, pltpu.with_memory_space_constraint(decoder.T, pltpu.VMEM))
+    )(codes, ids, weights)
     received = route(sent)
     sent, loss = call(
         combine_kernel,

time: 165 us -> 165 us (level)
  blocking collectives: 106 us -> 98.1 us
  waiting for transfers between devices: 17.2 us -> 24.5 us
  starting transfers between devices: 15 us -> 18.4 us
  local copies, waits for them, and re-layouts: 7.14 us -> 5.03 us
    all_to_all x1 -> x0, blocking collectives: 9.98 us -> none  [sum_codes(): lax.all_to_all(copies, INNER, split_axis=0, concat_axis=0, tiled=True)]
    all_to_all x0 -> x1, waiting for transfers between devices: none -> 5.85 us  [sum_codes(): lax.all_to_all(copies, INNER, split_axis=0, concat_axis=0, tiled=True)]
    all_to_all x0 -> x1, starting transfers between devices: none -> 3.45 us  [sum_codes(): lax.all_to_all(copies, INNER, split_axis=0, concat_axis=0, tiled=True)]
  transfers between devices with their start and end apart: 2 -> 3, of which waited for: 2 -> 3; matrix products, arithmetic and copies ran while one was open for 4% -> 3% of each run, Pallas kernels for 0% -> 0%
where the time goes in v8:
time: 165 us; the launch traced here: 163 us
  blocking collectives  98.1 us (59%)
  waiting for transfers between devices  24.5 us (15%)
  starting transfers between devices  18.4 us (11%)
  Pallas kernels  15.7 us (10%)
  local copies, waits for them, and re-layouts  5.03 us (3%)
    all_to_all x1, blocking collectives, route(): lax.all_to_all(buffer, PLANE, split_axis=0, concat_axis=0, tiled=True)  38.2 us
    psum x1, blocking collectives, sum_codes(): total = lax.psum(jnp.sum(received.astype(F32), axis=0), OUTER)  28.1 us
    psum x2, blocking collectives, sum_loss(): return lax.psum(lax.psum(part, OUTER), INNER)  19.3 us
    all_to_all x2, waiting for transfers between devices, route(): lax.all_to_all(buffer, PLANE, split_axis=0, concat_axis=0, tiled=True)  18.6 us
    all_to_all x2, starting transfers between devices, route(): lax.all_to_all(buffer, PLANE, split_axis=0, concat_axis=0, tiled=True)  14.9 us
    all_to_all x1, blocking collectives, sum_codes(): lax.all_to_all(shares, INNER, split_axis=0, concat_axis=0, tiled=True)  12.4 us
    all_to_all x1, waiting for transfers between devices, sum_codes(): lax.all_to_all(copies, INNER, split_axis=0, concat_axis=0, tiled=True)  5.85 us
    pallas_call x1, Pallas kernels, on_device(): call(prepare_kernel, (packed, shape((8, ROWS), jnp.int32)), sending, 2 *...  4.23 us
  transfers between devices with their start and end apart: 3, of which 3 were waited for; matrix products, arithmetic and copies ran while one was open for 3% of the time, Pallas kernels for 0%

profile of v8, /device:TPU:1, one launch (start us, length us, event | category | flops | bytes accessed | tf_op | source)
XLA Modules:
  0.0 163.5 jit_solution(14910894682324309625)
XLA Ops:
  0.6 4.2 %prepare.1 = (bf16[32,192,128]{2,1,0:T(8,128)(2,1)}, s32[8,512]{1,0:T(8,128)S(1)}) custom-call(bf16[288,512]{1,0:T(8,128)(2,1)} %bitcast.47, bf16[288]{0:T(512)(128)(2,1)} %bias_ref.3, s32[4,512]{1,0:T(4,128)} %bitcast.46), custom_call_target="tpu_custom_call" | custom-call | flops 754974720 | bytes 6000000 | tf_op jit(solution)/shard_map/prepare/pallas_call | solution.py:479
  4.9 10.5 %all-to-all-start.3 = ((bf16[32,192,128]{2,1,0:T(8,128)(2,1)}), bf16[32,192,128]{2,1,0:T(8,128)(2,1)S(1)}, u32[]{:S(2)}, u32[]{:S(2)}) async-start(bf16[32,192,128]{2,1,0:T(8,128)(2,1)} %get-tuple-element.40), calls=%async_computation.3 | async-start | bytes 3145728 | tf_op jit(solution)/shard_map/all_to_all | solution.py:395
  15.4 1.8 %copy.64 = bf16[288,2048]{0,1:T(8,128)(2,1)S(1)} copy(bf16[288,2048]{1,0:T(8,128)(2,1)} %param.9) | data formatting | bytes 2359296 | tf_op args[2]
  17.2 0.8 slice.20
  18.0 1.3 copy.65
  19.3 0.2 reshape.54
  19.6 0.1 copy.66.rest_ref
  19.7 17.2 %all-to-all-done.3.recv_ref = bf16[32,192,128]{2,1,0:T(8,128)(2,1)S(1)} async-done(((bf16[32,192,128]{2,1,0:T(8,128)(2,1)}), bf16[32,192,128]{2,1,0:T(8,128)(2,1)S(1)}, u32[]{:S(2)}, u32[]{:S(2)}) %all-to-all-start.3) | async-done | bytes 1572896 | tf_op jit(solution)/shard_map/all_to_all | solution.py:395
  36.8 2.4 %encode.1 = (bf16[16,80,128]{2,1,0:T(8,128)(2,1)S(1)}, f32[24,128]{1,0:T(8,128)S(1)}, s32[1,1]{1,0:T(1,128)}) custom-call(bf16[32,192,128]{2,1,0:T(8,128)(2,1)S(1)} %all-to-all-done.3.recv_ref, bf16[2048,288]{1,0:T(8,128)(2,1)S(1)} %bitcast.36, bf16[256,256]{1,0:T(8,128)(2,1)S(1)} %copy.66.rest_ref), custom_call_target="tpu_custom_call" | custom-call | flops 3019898880 | bytes 6000000 | tf_op jit(solution)/shard_map/encode/pallas_call | solution.py:491
  39.2 0.0 copy-start.2
  39.2 12.4 %all_to_all.38 = bf16[4,320,128]{2,1,0:T(8,128)(2,1)S(1)} all-to-all(bf16[4,320,128]{2,1,0:T(8,128)(2,1)S(1)} %bitcast.37), channel_id=1, replica_groups=mesh['dp_outer'=4,'dp_inner'=4,'latent'=8,'section'=4] {'dp_inner'}, dimensions={0} | all-to-all | bytes 655360 | tf_op jit(solution)/shard_map/all_to_all | solution.py:406
  51.7 28.1 %all-reduce.3 = bf16[320,128]{1,0:T(8,128)(2,1)S(1)} all-reduce(f32[320,128]{1,0:T(8,128)S(1)} %convert_reduce_fusion.1), channel_id=1, replica_groups=mesh['dp_outer'=4,'dp_inner'=4,'latent'=8,'section'=4] {'dp_outer'}, use_global_device_ids=true, to_apply=%region_1.0 | all-reduce | flops 40960 | bytes 245760 | tf_op jit(solution)/shard_map/psum | solution.py:407
  79.8 0.8 broadcast_in_dim.2
  80.6 3.5 %all-to-all-start.5 = ((bf16[4,320,128]{2,1,0:T(8,128)(2,1)}), bf16[4,320,128]{2,1,0:T(8,128)(2,1)S(1)}, u32[]{:S(2)}, u32[]{:S(2)}) async-start(bf16[4,320,128]{2,1,0:T(8,128)(2,1)} %broadcast_in_dim.2), calls=%async_computation.5 | async-start | bytes 655360 | tf_op jit(solution)/shard_map/all_to_all | solution.py:411
  84.0 0.0 copy-done.2
  84.1 0.3 fetch.1.dec_ref
  84.3 5.8 %all-to-all-done.5 = bf16[4,320,128]{2,1,0:T(8,128)(2,1)S(1)} async-done(((bf16[4,320,128]{2,1,0:T(8,128)(2,1)}), bf16[4,320,128]{2,1,0:T(8,128)(2,1)S(1)}, u32[]{:S(2)}, u32[]{:S(2)}) %all-to-all-start.5) | async-done | bytes 327712 | tf_op jit(solution)/shard_map/all_to_all | solution.py:411
  90.2 2.3 %decode.1 = bf16[32,192,128]{2,1,0:T(8,128)(2,1)S(1)} custom-call(bf16[16,80,128]{2,1,0:T(8,128)(2,1)S(1)} %bitcast.44, f32[24,128]{1,0:T(8,128)S(1)} %get-tuple-element.44.ids_ref, bf16[288,2048]{1,0:T(8,128)(2,1)S(1)} %fetch.1.dec_ref), custom_call_target="tpu_custom_call" | custom-call | flops 3019898880 | bytes 6000000 | tf_op jit(solution)/shard_map/decode/pallas_call | solution.py:501
  92.5 0.0 copy-start.4
  92.5 0.0 copy-start.5
  92.5 38.2 %all_to_all.39.recv_ref = bf16[32,192,128]{2,1,0:T(8,128)(2,1)S(1)} all-to-all(bf16[32,192,128]{2,1,0:T(8,128)(2,1)S(1)} %decode.1), channel_id=1, replica_groups=mesh['dp_outer'=4,'dp_inner'=4,'latent'=8,'section'=4] {'latent','section'}, dimensions={0} | all-to-all | bytes 3145728 | tf_op jit(solution)/shard_map/all_to_all | solution.py:395
  130.7 0.0 copy-done.4
  130.8 0.0 copy-done.5
  130.8 0.0 copy-start.3
  130.8 3.3 %combine.1 = (bf16[32,192,128]{2,1,0:T(8,128)(2,1)}, f32[4,128]{1,0:T(4,128)S(1)}) custom-call(bf16[32,192,128]{2,1,0:T(8,128)(2,1)S(1)} %all_to_all.39.recv_ref, s32[8,512]{1,0:T(8,128)S(1)} %get-tuple-element.46.slots_ref, bf16[288,512]{1,0:T(8,128)(2,1)S(1)} %bitcast.48, bf16[288]{0:T(512)(128)(2,1)S(1)} %copy-done.4), custom_call_target="tpu_custom_call" | custom-call | flops 1509949440 | bytes 6000000 | tf_op jit(solution)/shard_map/combine/pallas_call | solution.py:513
  134.1 4.4 %all-to-all-start.7 = ((bf16[32,192,128]{2,1,0:T(8,128)(2,1)}), bf16[32,192,128]{2,1,0:T(8,128)(2,1)S(1)}, u32[]{:S(2)}, u32[]{:S(2)}) async-start(bf16[32,192,128]{2,1,0:T(8,128)(2,1)} %get-tuple-element.47), calls=%async_computation.7 | async-start | bytes 3145728 | tf_op jit(solution)/shard_map/all_to_all | solution.py:395
  139.1 10.7 %psum.36 = f32[4,128]{1,0:T(4,128)S(1)} all-reduce(f32[4,128]{1,0:T(4,128)S(1)} %get-tuple-element.48), channel_id=1, replica_groups=mesh['dp_outer'=4,'dp_inner'=4,'latent'=8,'section'=4] {'dp_outer'}, use_global_device_ids=true, to_apply=%region_2.0 | all-reduce | flops 512 | bytes 4096 | tf_op jit(solution)/shard_map/psum | solution.py:426
  149.8 8.6 %psum.37 = f32[4,128]{1,0:T(4,128)S(1)} all-reduce(f32[4,128]{1,0:T(4,128)S(1)} %psum.36), channel_id=1, replica_groups=mesh['dp_outer'=4,'dp_inner'=4,'latent'=8,'section'=4] {'dp_inner'}, use_global_device_ids=true, to_apply=%region_3.0 | all-reduce | flops 512 | bytes 4096 | tf_op jit(solution)/shard_map/psum | solution.py:426
  158.4 1.4 all-to-all-done.7
  159.8 0.0 copy-done.3
  159.8 3.5 %conditional.1 = (f32[512]{0:T(512)}, bf16[2048,288]{0,1:T(8,128)(2,1)}) conditional(s32[]{:T(128)} %bitcast.18, (bf16[32,192,128]{2,1,0:T(8,128)(2,1)S(1)}, bf16[16,80,128]{2,1,0:T(8,128)(2,1)S(1)}, f32[24,128]{1,0:T(8,128)S(1)}, f32[4,128]{1,0:T(4,128)S(1)}) %tuple.47, (s32[512,4]{0,1:T(4,128)S(1)}, bf16[512,288]{0,1:T(8,128)(2,1)S(1)}, ...), branch_computations={%region_4.0_spmd, %region_5.0_spmd} | conditional | flops 4205791488 | bytes 89270392 | solution.py:542
  159.8 3.2 %gradient.1 = (bf16[288,2048]{1,0:T(8,128)(2,1)}, f32[4,128]{1,0:T(4,128)}) custom-call(bf16[32,192,128]{2,1,0:T(8,128)(2,1)S(1)} %get-tuple-element.18.recv_ref, bf16[16,80,128]{2,1,0:T(8,128)(2,1)S(1)} %get-tuple-element.19.codes_ref, f32[24,128]{1,0:T(8,128)S(1)} %get-tuple-element.20.ids_ref, f32[4,128]{1,0:T(4,128)S(1)} %get-tuple-element.21.loss_ref), custom_call_target="tpu_custom_call" | custom-call | flops 3019898880 | bytes 6000000 | tf_op jit(solution)/shard_map/cond/branch_0_fun/gradient/pallas_call | solution.py:526
  (2 shorter events, 0.1 us)
Async XLA Ops:
  4.9 32.0 %all-to-all-start.3 = ((bf16[32,192,128]{2,1,0:T(8,128)(2,1)}), bf16[32,192,128]{2,1,0:T(8,128)(2,1)S(1)}, u32[]{:S(2)}, u32[]{:S(2)}) async-start(bf16[32,192,128]{2,1,0:T(8,128)(2,1)} %get-tuple-element.40), calls=%async_computation.3 | async-start | bytes 3145728 | tf_op jit(solution)/shard_map/all_to_all | solution.py:395
  39.2 44.8 %copy-start.2 = (bf16[2048,288]{0,1:T(8,128)(2,1)S(1)}, bf16[2048,288]{0,1:T(8,128)(2,1)}, u32[]{:S(2)}) copy-start(bf16[2048,288]{0,1:T(8,128)(2,1)} %param.10) | copy-start | bytes 3538948
  80.6 9.6 %all-to-all-start.5 = ((bf16[4,320,128]{2,1,0:T(8,128)(2,1)}), bf16[4,320,128]{2,1,0:T(8,128)(2,1)S(1)}, u32[]{:S(2)}, u32[]{:S(2)}) async-start(bf16[4,320,128]{2,1,0:T(8,128)(2,1)} %broadcast_in_dim.2), calls=%async_computation.5 | async-start | bytes 655360 | tf_op jit(solution)/shard_map/all_to_all | solution.py:411
  92.5 38.3 %copy-start.4 = (bf16[288]{0:T(512)(128)(2,1)S(1)}, bf16[288]{0:T(512)(128)(2,1)}, u32[]{:S(2)}) copy-start(bf16[288]{0:T(512)(128)(2,1)} %bias_ref.3) | copy-start | bytes 1732
  92.5 38.3 %copy-start.5 = (bf16[512,288]{0,1:T(8,128)(2,1)S(1)}, bf16[512,288]{0,1:T(8,128)(2,1)}, u32[]{:S(2)}) copy-start(bf16[512,288]{0,1:T(8,128)(2,1)} %param.7) | copy-start | bytes 884740
  130.8 29.1 %copy-start.3 = (s32[512,4]{0,1:T(4,128)S(1)}, s32[512,4]{0,1:T(4,128)}, u32[]{:S(2)}) copy-start(s32[512,4]{0,1:T(4,128)} %param.11) | copy-start | bytes 24580
  134.1 25.8 %all-to-all-start.7 = ((bf16[32,192,128]{2,1,0:T(8,128)(2,1)}), bf16[32,192,128]{2,1,0:T(8,128)(2,1)S(1)}, u32[]{:S(2)}, u32[]{:S(2)}) async-start(bf16[32,192,128]{2,1,0:T(8,128)(2,1)} %get-tuple-element.47), calls=%async_computation.7 | async-start | bytes 3145728 | tf_op jit(solution)/shard_map/all_to_all | solution.py:395

commit v9 on v7

--- a/solution.py
+++ b/solution.py
@@ -25,7 +25,7 @@
 SLOTS = MAIN_SLOTS + EXTRA_SLOTS
 PACKED = HALF + 3 * EXTRA
 PAIRS = GROUPS // 2
-EARLY = 12
+STAGE = 4
 LANE_TILES = SLOTS // 128
 CHUNK_TILES = 5
 CHUNK_ROWS = 16 * CHUNK_TILES
@@ -78,26 +78,25 @@
     out_ref[pair + PAIRS, 0:HALF, :] = second
 
 
-def stage_copies(buffer_ref, out_ref, sems, stage, early):
-    first, count = (0, early) if stage == 0 else (early, PAIRS - early)
+def stage_copies(buffer_ref, out_ref, sems, stage):
     copies = []
     for side in range(2):
-        devices = pl.ds(side * PAIRS + first, count)
+        devices = pl.ds(side * PAIRS + stage * STAGE, STAGE)
         copies.append(
             pltpu.make_async_copy(buffer_ref.at[devices], out_ref.at[devices], sems.at[2 * stage + side])
         )
     return copies
 
 
-def start_stage(buffer_ref, out_ref, sems, done, early=EARLY):
-    if done in (early, PAIRS):
-        for copy in stage_copies(buffer_ref, out_ref, sems, 0 if done == early else 1, early):
+def start_stage(buffer_ref, out_ref, sems, done):
+    if done % STAGE == 0:
+        for copy in stage_copies(buffer_ref, out_ref, sems, done // STAGE - 1):
             copy.start()
 
 
-def wait_stages(buffer_ref, out_ref, sems, early=EARLY):
-    for stage in range(2):
-        for copy in stage_copies(buffer_ref, out_ref, sems, stage, early):
+def wait_stages(buffer_ref, out_ref, sems):
+    for stage in range(PAIRS // STAGE):
+        for copy in stage_copies(buffer_ref, out_ref, sems, stage):
             copy.wait()
 
 
@@ -163,9 +162,13 @@
     count = GROUPS * QUARTERS
     groups = lax.broadcasted_iota(jnp.int32, (count, ROWS), 0)
     hits = [groups == group[k : k + 1, :] for k in range(NAMED)]
-    counts = sum(jnp.where(hit, 1.0, 0.0) for hit in hits).astype(BF16)
-    before = lax.broadcasted_iota(jnp.int32, (ROWS, ROWS), 0) < lax.broadcasted_iota(jnp.int32, (ROWS, ROWS), 1)
-    earlier = mm(counts, jnp.where(before, 1.0, 0.0).astype(BF16))
+    small = lax.broadcasted_iota(jnp.int16, (count, ROWS), 0)
+    counts = jnp.zeros((count, ROWS), BF16)
+    for k in range(NAMED):
+        hit = small == jnp.broadcast_to(group[k : k + 1, :].astype(jnp.int16), small.shape)
+        counts = counts + jnp.where(hit, BF16(1), BF16(0))
+    before = lax.broadcasted_iota(jnp.int16, (ROWS, ROWS), 0) < lax.broadcasted_iota(jnp.int16, (ROWS, ROWS), 1)
+    earlier = mm(counts, jnp.where(before, BF16(1), BF16(0)))
     beyond = jnp.maximum(mm(counts, jnp.ones((ROWS, 128), BF16)) - SHARE, 0.0).astype(BF16)
     one = lax.broadcasted_iota(jnp.int32, (count, count), 0)
     other = lax.broadcasted_iota(jnp.int32, (count, count), 1)
@@ -463,7 +466,7 @@
     bias = bias_dec
     packed = in_hbm((GROUPS, PACKED, 128))
     full = pltpu.VMEM((FEATURES, SLOTS), BF16)
-    sending = [pltpu.VMEM((GROUPS, PACKED, 128), BF16), pltpu.SemaphoreType.DMA((4,))]
+    sending = [pltpu.VMEM((GROUPS, PACKED, 128), BF16), pltpu.SemaphoreType.DMA((2 * PAIRS // STAGE,))]
     vmem, hbm = pl.BlockSpec(memory_space=pltpu.VMEM), pl.BlockSpec(memory_space=pltpu.HBM)
     spread_flops = 2 * FEATURES * SLOTS * LOCAL * BLOCK
     sent, slots = call(

time: 165 us -> 165 us (level)
  no operation moved by 1% of the time
where the time goes in v9:
time: 165 us; the launch traced here: 163 us
  blocking collectives  107 us (65%)
  waiting for transfers between devices  18 us (11%)
  Pallas kernels  16.6 us (10%)
  starting transfers between devices  14.9 us (9%)
  local copies, waits for them, and re-layouts  4.3 us (3%)
    all_to_all x1, blocking collectives, route(): lax.all_to_all(buffer, PLANE, split_axis=0, concat_axis=0, tiled=True)  36.8 us
    psum x1, blocking collectives, sum_codes(): total = lax.psum(jnp.sum(received.astype(F32), axis=0), OUTER)  28.1 us
    psum x2, blocking collectives, sum_loss(): return lax.psum(lax.psum(part, OUTER), INNER)  20 us
    all_to_all x2, waiting for transfers between devices, route(): lax.all_to_all(buffer, PLANE, split_axis=0, concat_axis=0, tiled=True)  18 us
    all_to_all x2, starting transfers between devices, route(): lax.all_to_all(buffer, PLANE, split_axis=0, concat_axis=0, tiled=True)  14.9 us
    all_to_all x1, blocking collectives, sum_codes(): lax.all_to_all(shares, INNER, split_axis=0, concat_axis=0, tiled=True)  12.3 us
    all_to_all x1, blocking collectives, sum_codes(): lax.all_to_all(copies, INNER, split_axis=0, concat_axis=0, tiled=True)  9.99 us
    pallas_call x1, Pallas kernels, on_device(): call(prepare_kernel, (packed, shape((8, ROWS), jnp.int32)), sending, 2 *...  4.23 us
  transfers between devices with their start and end apart: 2, of which 2 were waited for; matrix products, arithmetic and copies ran while one was open for 3% of the time, Pallas kernels for 0%

profile of v9, /device:TPU:1, one launch (start us, length us, event | category | flops | bytes accessed | tf_op | source)
XLA Modules:
  0.0 162.7 jit_solution(10140270807612518106)
XLA Ops:
  0.6 4.2 %prepare.1 = (bf16[32,192,128]{2,1,0:T(8,128)(2,1)}, s32[8,512]{1,0:T(8,128)S(1)}) custom-call(bf16[288,512]{1,0:T(8,128)(2,1)} %bitcast.47, bf16[288]{0:T(512)(128)(2,1)} %bias_ref.3, s32[4,512]{1,0:T(4,128)} %bitcast.46), custom_call_target="tpu_custom_call" | custom-call | flops 754974720 | bytes 6000000 | tf_op jit(solution)/shard_map/prepare/pallas_call | solution.py:472
  4.9 10.5 %all-to-all-start.3 = ((bf16[32,192,128]{2,1,0:T(8,128)(2,1)}), bf16[32,192,128]{2,1,0:T(8,128)(2,1)S(1)}, u32[]{:S(2)}, u32[]{:S(2)}) async-start(bf16[32,192,128]{2,1,0:T(8,128)(2,1)} %get-tuple-element.38), calls=%async_computation.3 | async-start | bytes 3145728 | tf_op jit(solution)/shard_map/all_to_all | solution.py:406
  15.4 1.8 %copy.64 = bf16[288,2048]{0,1:T(8,128)(2,1)S(1)} copy(bf16[288,2048]{1,0:T(8,128)(2,1)} %param.9) | data formatting | bytes 2359296 | tf_op args[2]
  17.2 0.8 slice.20
  18.0 1.3 copy.65
  19.3 0.2 reshape.54
  19.6 0.1 copy.66.rest_ref
  19.7 17.2 %all-to-all-done.3.recv_ref = bf16[32,192,128]{2,1,0:T(8,128)(2,1)S(1)} async-done(((bf16[32,192,128]{2,1,0:T(8,128)(2,1)}), bf16[32,192,128]{2,1,0:T(8,128)(2,1)S(1)}, u32[]{:S(2)}, u32[]{:S(2)}) %all-to-all-start.3) | async-done | bytes 1572896 | tf_op jit(solution)/shard_map/all_to_all | solution.py:406
  36.8 2.4 %encode.1 = (bf16[16,80,128]{2,1,0:T(8,128)(2,1)S(1)}, f32[24,128]{1,0:T(8,128)S(1)}, s32[1,1]{1,0:T(1,128)}) custom-call(bf16[32,192,128]{2,1,0:T(8,128)(2,1)S(1)} %all-to-all-done.3.recv_ref, bf16[2048,288]{1,0:T(8,128)(2,1)S(1)} %bitcast.36, bf16[256,256]{1,0:T(8,128)(2,1)S(1)} %copy.66.rest_ref), custom_call_target="tpu_custom_call" | custom-call | flops 3019898880 | bytes 6000000 | tf_op jit(solution)/shard_map/encode/pallas_call | solution.py:484
  39.2 12.3 %all_to_all.38 = bf16[4,320,128]{2,1,0:T(8,128)(2,1)S(1)} all-to-all(bf16[4,320,128]{2,1,0:T(8,128)(2,1)S(1)} %bitcast.37), channel_id=1, replica_groups=mesh['dp_outer'=4,'dp_inner'=4,'latent'=8,'section'=4] {'dp_inner'}, dimensions={0} | all-to-all | bytes 655360 | tf_op jit(solution)/shard_map/all_to_all | solution.py:411
  51.5 28.1 %all-reduce.3 = bf16[320,128]{1,0:T(8,128)(2,1)S(1)} all-reduce(f32[320,128]{1,0:T(8,128)S(1)} %convert_reduce_fusion.1), channel_id=1, replica_groups=mesh['dp_outer'=4,'dp_inner'=4,'latent'=8,'section'=4] {'dp_outer'}, use_global_device_ids=true, to_apply=%region_1.0 | all-reduce | flops 40960 | bytes 245760 | tf_op jit(solution)/shard_map/psum | solution.py:412
  79.7 10.0 %all_to_all.39 = bf16[4,320,128]{2,1,0:T(8,128)(2,1)S(1)} all-to-all(bf16[4,320,128]{2,1,0:T(8,128)(2,1)S(1)} %broadcast_in_dim.2), channel_id=1, replica_groups=mesh['dp_outer'=4,'dp_inner'=4,'latent'=8,'section'=4] {'dp_inner'}, dimensions={0} | all-to-all | bytes 655360 | tf_op jit(solution)/shard_map/all_to_all | solution.py:415
  89.7 3.5 %decode.1 = bf16[32,192,128]{2,1,0:T(8,128)(2,1)S(1)} custom-call(bf16[16,80,128]{2,1,0:T(8,128)(2,1)S(1)} %bitcast.44, f32[24,128]{1,0:T(8,128)S(1)} %get-tuple-element.41.ids_ref, bf16[288,2048]{1,0:T(8,128)(2,1)} %bitcast.42), custom_call_target="tpu_custom_call" | custom-call | flops 3019898880 | bytes 6000000 | tf_op jit(solution)/shard_map/decode/pallas_call | solution.py:494
  93.2 0.0 copy-start.3
  93.2 0.0 copy-start.4
  93.2 36.8 %all_to_all.40.recv_ref = bf16[32,192,128]{2,1,0:T(8,128)(2,1)S(1)} all-to-all(bf16[32,192,128]{2,1,0:T(8,128)(2,1)S(1)} %decode.1), channel_id=1, replica_groups=mesh['dp_outer'=4,'dp_inner'=4,'latent'=8,'section'=4] {'latent','section'}, dimensions={0} | all-to-all | bytes 3145728 | tf_op jit(solution)/shard_map/all_to_all | solution.py:406
  130.0 0.0 copy-done.3
  130.0 0.0 copy-done.4
  130.0 0.0 copy-start.2
  130.0 3.3 %combine.1 = (bf16[32,192,128]{2,1,0:T(8,128)(2,1)}, f32[4,128]{1,0:T(4,128)S(1)}) custom-call(bf16[32,192,128]{2,1,0:T(8,128)(2,1)S(1)} %all_to_all.40.recv_ref, s32[8,512]{1,0:T(8,128)S(1)} %get-tuple-element.42.slots_ref, bf16[288,512]{1,0:T(8,128)(2,1)S(1)} %bitcast.48, bf16[288]{0:T(512)(128)(2,1)S(1)} %copy-done.3), custom_call_target="tpu_custom_call" | custom-call | flops 1509949440 | bytes 6000000 | tf_op jit(solution)/shard_map/combine/pallas_call | solution.py:509
  133.3 4.4 %all-to-all-start.7 = ((bf16[32,192,128]{2,1,0:T(8,128)(2,1)}), bf16[32,192,128]{2,1,0:T(8,128)(2,1)S(1)}, u32[]{:S(2)}, u32[]{:S(2)}) async-start(bf16[32,192,128]{2,1,0:T(8,128)(2,1)} %get-tuple-element.43), calls=%async_computation.7 | async-start | bytes 3145728 | tf_op jit(solution)/shard_map/all_to_all | solution.py:406
  138.3 11.6 %psum.36 = f32[4,128]{1,0:T(4,128)S(1)} all-reduce(f32[4,128]{1,0:T(4,128)S(1)} %get-tuple-element.44), channel_id=1, replica_groups=mesh['dp_outer'=4,'dp_inner'=4,'latent'=8,'section'=4] {'dp_outer'}, use_global_device_ids=true, to_apply=%region_2.0 | all-reduce | flops 512 | bytes 4096 | tf_op jit(solution)/shard_map/psum | solution.py:419
  149.9 8.4 %psum.37 = f32[4,128]{1,0:T(4,128)S(1)} all-reduce(f32[4,128]{1,0:T(4,128)S(1)} %psum.36), channel_id=1, replica_groups=mesh['dp_outer'=4,'dp_inner'=4,'latent'=8,'section'=4] {'dp_inner'}, use_global_device_ids=true, to_apply=%region_3.0 | all-reduce | flops 512 | bytes 4096 | tf_op jit(solution)/shard_map/psum | solution.py:419
  158.3 0.8 all-to-all-done.7
  159.1 0.0 copy-done.2
  159.1 3.5 %conditional.1 = (f32[512]{0:T(512)}, bf16[2048,288]{0,1:T(8,128)(2,1)}) conditional(s32[]{:T(128)} %bitcast.18, (bf16[32,192,128]{2,1,0:T(8,128)(2,1)S(1)}, bf16[16,80,128]{2,1,0:T(8,128)(2,1)S(1)}, f32[24,128]{1,0:T(8,128)S(1)}, f32[4,128]{1,0:T(4,128)S(1)}) %tuple.45, (s32[512,4]{0,1:T(4,128)S(1)}, bf16[512,288]{0,1:T(8,128)(2,1)S(1)}, ...), branch_computations={%region_4.0_spmd, %region_5.0_spmd} | conditional | flops 4205791488 | bytes 89270392 | solution.py:538
  159.1 3.3 %gradient.1 = (bf16[288,2048]{1,0:T(8,128)(2,1)}, f32[4,128]{1,0:T(4,128)}) custom-call(bf16[32,192,128]{2,1,0:T(8,128)(2,1)S(1)} %get-tuple-element.18.recv_ref, bf16[16,80,128]{2,1,0:T(8,128)(2,1)S(1)} %get-tuple-element.19.codes_ref, f32[24,128]{1,0:T(8,128)S(1)} %get-tuple-element.20.ids_ref, f32[4,128]{1,0:T(4,128)S(1)} %get-tuple-element.21.loss_ref), custom_call_target="tpu_custom_call" | custom-call | flops 3019898880 | bytes 6000000 | tf_op jit(solution)/shard_map/cond/branch_0_fun/gradient/pallas_call | solution.py:522
  (3 shorter events, 0.1 us)
Async XLA Ops:
  4.9 32.0 %all-to-all-start.3 = ((bf16[32,192,128]{2,1,0:T(8,128)(2,1)}), bf16[32,192,128]{2,1,0:T(8,128)(2,1)S(1)}, u32[]{:S(2)}, u32[]{:S(2)}) async-start(bf16[32,192,128]{2,1,0:T(8,128)(2,1)} %get-tuple-element.38), calls=%async_computation.3 | async-start | bytes 3145728 | tf_op jit(solution)/shard_map/all_to_all | solution.py:406
  93.2 36.8 %copy-start.3 = (bf16[288]{0:T(512)(128)(2,1)S(1)}, bf16[288]{0:T(512)(128)(2,1)}, u32[]{:S(2)}) copy-start(bf16[288]{0:T(512)(128)(2,1)} %bias_ref.3) | copy-start | bytes 1732
  93.2 36.8 %copy-start.4 = (bf16[512,288]{0,1:T(8,128)(2,1)S(1)}, bf16[512,288]{0,1:T(8,128)(2,1)}, u32[]{:S(2)}) copy-start(bf16[512,288]{0,1:T(8,128)(2,1)} %param.7) | copy-start | bytes 884740
  130.0 29.1 %copy-start.2 = (s32[512,4]{0,1:T(4,128)S(1)}, s32[512,4]{0,1:T(4,128)}, u32[]{:S(2)}) copy-start(s32[512,4]{0,1:T(4,128)} %param.11) | copy-start | bytes 24580
  133.3 25.8 %all-to-all-start.7 = ((bf16[32,192,128]{2,1,0:T(8,128)(2,1)}), bf16[32,192,128]{2,1,0:T(8,128)(2,1)S(1)}, u32[]{:S(2)}, u32[]{:S(2)}) async-start(bf16[32,192,128]{2,1,0:T(8,128)(2,1)} %get-tuple-element.43), calls=%async_computation.7 | async-start | bytes 3145728 | tf_op jit(solution)/shard_map/all_to_all | solution.py:406

commit v10 on v9

--- a/solution.py
+++ b/solution.py
@@ -409,8 +409,10 @@
 def sum_codes(partial):
     shares = partial.reshape(4, SHARDS // 4 * CHUNK_ROWS, 128)
     received = lax.all_to_all(shares, INNER, split_axis=0, concat_axis=0, tiled=True)
-    total = lax.psum(jnp.sum(received.astype(F32), axis=0), OUTER)
-    codes = jnp.maximum(total, 0.0).astype(BF16)
+    run = jnp.sum(received.astype(F32), axis=0).astype(BF16)
+    runs = jnp.broadcast_to(run[None], shares.shape)
+    runs = lax.all_to_all(runs, OUTER, split_axis=0, concat_axis=0, tiled=True)
+    codes = jnp.maximum(jnp.sum(runs.astype(F32), axis=0), 0.0).astype(BF16)
     copies = jnp.broadcast_to(codes[None], shares.shape)
     return lax.all_to_all(copies, INNER, split_axis=0, concat_axis=0, tiled=True).reshape(partial.shape)
 

time: 165 us -> 166 us (level)
  blocking collectives: 107 us -> 109 us
    all_to_all x0 -> x1, blocking collectives: none -> 30.4 us  [sum_codes(): runs = lax.all_to_all(runs, OUTER, split_axis=0, concat_axis=0, tiled=True)]
    psum x1 -> x0, blocking collectives: 28.1 us -> none  [sum_codes(): total = lax.psum(jnp.sum(received.astype(F32), axis=0), OUTER)]
where the time goes in v10:
time: 166 us; the launch traced here: 165 us
  blocking collectives  109 us (66%)
  waiting for transfers between devices  18.9 us (11%)
  Pallas kernels  15.8 us (10%)
  starting transfers between devices  14.9 us (9%)
  local copies, waits for them, and re-layouts  4.35 us (3%)
    all_to_all x1, blocking collectives, route(): lax.all_to_all(buffer, PLANE, split_axis=0, concat_axis=0, tiled=True)  36.2 us
    all_to_all x1, blocking collectives, sum_codes(): runs = lax.all_to_all(runs, OUTER, split_axis=0, concat_axis=0, tiled=True)  30.4 us
    psum x2, blocking collectives, sum_loss(): return lax.psum(lax.psum(part, OUTER), INNER)  19.1 us
    all_to_all x2, waiting for transfers between devices, route(): lax.all_to_all(buffer, PLANE, split_axis=0, concat_axis=0, tiled=True)  18.9 us
    all_to_all x2, starting transfers between devices, route(): lax.all_to_all(buffer, PLANE, split_axis=0, concat_axis=0, tiled=True)  14.9 us
    all_to_all x1, blocking collectives, sum_codes(): lax.all_to_all(shares, INNER, split_axis=0, concat_axis=0, tiled=True)  12.4 us
    all_to_all x1, blocking collectives, sum_codes(): lax.all_to_all(copies, INNER, split_axis=0, concat_axis=0, tiled=True)  10.6 us
    pallas_call x1, Pallas kernels, on_device(): call(prepare_kernel, (packed, shape((8, ROWS), jnp.int32)), sending, 2 *...  4.23 us
  transfers between devices with their start and end apart: 2, of which 2 were waited for; matrix products, arithmetic and copies ran while one was open for 3% of the time, Pallas kernels for 0%

profile of v10, /device:TPU:1, one launch (start us, length us, event | category | flops | bytes accessed | tf_op | source)
XLA Modules:
  0.0 164.6 jit_solution(3045770657779850301)
XLA Ops:
  0.6 4.2 %prepare.1 = (bf16[32,192,128]{2,1,0:T(8,128)(2,1)}, s32[8,512]{1,0:T(8,128)S(1)}) custom-call(bf16[288,512]{1,0:T(8,128)(2,1)} %bitcast.47, bf16[288]{0:T(512)(128)(2,1)} %bias_ref.3, s32[4,512]{1,0:T(4,128)} %bitcast.46), custom_call_target="tpu_custom_call" | custom-call | flops 754974720 | bytes 6000000 | tf_op jit(solution)/shard_map/prepare/pallas_call | solution.py:474
  4.9 10.5 %all-to-all-start.3 = ((bf16[32,192,128]{2,1,0:T(8,128)(2,1)}), bf16[32,192,128]{2,1,0:T(8,128)(2,1)S(1)}, u32[]{:S(2)}, u32[]{:S(2)}) async-start(bf16[32,192,128]{2,1,0:T(8,128)(2,1)} %get-tuple-element.38), calls=%async_computation.3 | async-start | bytes 3145728 | tf_op jit(solution)/shard_map/all_to_all | solution.py:406
  15.4 1.8 %copy.64 = bf16[288,2048]{0,1:T(8,128)(2,1)S(1)} copy(bf16[288,2048]{1,0:T(8,128)(2,1)} %param.9) | data formatting | bytes 2359296 | tf_op args[2]
  17.2 0.8 slice.20
  18.0 1.3 copy.65
  19.3 0.2 reshape.58
  19.6 0.1 copy.66.rest_ref
  19.7 17.2 %all-to-all-done.3.recv_ref = bf16[32,192,128]{2,1,0:T(8,128)(2,1)S(1)} async-done(((bf16[32,192,128]{2,1,0:T(8,128)(2,1)}), bf16[32,192,128]{2,1,0:T(8,128)(2,1)S(1)}, u32[]{:S(2)}, u32[]{:S(2)}) %all-to-all-start.3) | async-done | bytes 1572896 | tf_op jit(solution)/shard_map/all_to_all | solution.py:406
  36.8 2.4 %encode.1 = (bf16[16,80,128]{2,1,0:T(8,128)(2,1)S(1)}, f32[24,128]{1,0:T(8,128)S(1)}, s32[1,1]{1,0:T(1,128)}) custom-call(bf16[32,192,128]{2,1,0:T(8,128)(2,1)S(1)} %all-to-all-done.3.recv_ref, bf16[2048,288]{1,0:T(8,128)(2,1)S(1)} %bitcast.36, bf16[256,256]{1,0:T(8,128)(2,1)S(1)} %copy.66.rest_ref), custom_call_target="tpu_custom_call" | custom-call | flops 3019898880 | bytes 6000000 | tf_op jit(solution)/shard_map/encode/pallas_call | solution.py:486
  39.2 0.0 copy-start.2
  39.2 12.4 %all_to_all.43 = bf16[4,320,128]{2,1,0:T(8,128)(2,1)S(1)} all-to-all(bf16[4,320,128]{2,1,0:T(8,128)(2,1)S(1)} %bitcast.37), channel_id=1, replica_groups=mesh['dp_outer'=4,'dp_inner'=4,'latent'=8,'section'=4] {'dp_inner'}, dimensions={0} | all-to-all | bytes 655360 | tf_op jit(solution)/shard_map/all_to_all | solution.py:411
  51.7 30.4 %all_to_all.44 = bf16[4,320,128]{2,1,0:T(8,128)(2,1)S(1)} all-to-all(bf16[4,320,128]{2,1,0:T(8,128)(2,1)S(1)} %broadcast_in_dim.4), channel_id=1, replica_groups=mesh['dp_outer'=4,'dp_inner'=4,'latent'=8,'section'=4] {'dp_outer'}, dimensions={0} | all-to-all | bytes 655360 | tf_op jit(solution)/shard_map/all_to_all | solution.py:414
  82.3 10.6 %all_to_all.45 = bf16[4,320,128]{2,1,0:T(8,128)(2,1)S(1)} all-to-all(bf16[4,320,128]{2,1,0:T(8,128)(2,1)S(1)} %broadcast_in_dim.5), channel_id=1, replica_groups=mesh['dp_outer'=4,'dp_inner'=4,'latent'=8,'section'=4] {'dp_inner'}, dimensions={0} | all-to-all | bytes 655360 | tf_op jit(solution)/shard_map/all_to_all | solution.py:417
  92.9 0.0 copy-done.2
  92.9 2.7 %decode.1 = bf16[32,192,128]{2,1,0:T(8,128)(2,1)S(1)} custom-call(bf16[16,80,128]{2,1,0:T(8,128)(2,1)S(1)} %bitcast.44, f32[24,128]{1,0:T(8,128)S(1)} %get-tuple-element.41.ids_ref, bf16[288,2048]{1,0:T(8,128)(2,1)S(1)} %bitcast.42), custom_call_target="tpu_custom_call" | custom-call | flops 3019898880 | bytes 6000000 | tf_op jit(solution)/shard_map/decode/pallas_call | solution.py:496
  95.6 0.0 copy-start.4
  95.6 0.0 copy-start.5
  95.6 36.2 %all_to_all.46.recv_ref = bf16[32,192,128]{2,1,0:T(8,128)(2,1)S(1)} all-to-all(bf16[32,192,128]{2,1,0:T(8,128)(2,1)S(1)} %decode.1), channel_id=1, replica_groups=mesh['dp_outer'=4,'dp_inner'=4,'latent'=8,'section'=4] {'latent','section'}, dimensions={0} | all-to-all | bytes 3145728 | tf_op jit(solution)/shard_map/all_to_all | solution.py:406
  131.8 0.0 copy-done.4
  131.8 0.0 copy-done.5
  131.8 0.0 copy-start.3
  131.8 3.3 %combine.1 = (bf16[32,192,128]{2,1,0:T(8,128)(2,1)}, f32[4,128]{1,0:T(4,128)S(1)}) custom-call(bf16[32,192,128]{2,1,0:T(8,128)(2,1)S(1)} %all_to_all.46.recv_ref, s32[8,512]{1,0:T(8,128)S(1)} %get-tuple-element.42.slots_ref, bf16[288,512]{1,0:T(8,128)(2,1)S(1)} %bitcast.48, bf16[288]{0:T(512)(128)(2,1)S(1)} %copy-done.4), custom_call_target="tpu_custom_call" | custom-call | flops 1509949440 | bytes 6000000 | tf_op jit(solution)/shard_map/combine/pallas_call | solution.py:511
  135.1 4.4 %all-to-all-start.8 = ((bf16[32,192,128]{2,1,0:T(8,128)(2,1)}), bf16[32,192,128]{2,1,0:T(8,128)(2,1)S(1)}, u32[]{:S(2)}, u32[]{:S(2)}) async-start(bf16[32,192,128]{2,1,0:T(8,128)(2,1)} %get-tuple-element.43), calls=%async_computation.8 | async-start | bytes 3145728 | tf_op jit(solution)/shard_map/all_to_all | solution.py:406
  140.2 10.7 %psum.28 = f32[4,128]{1,0:T(4,128)S(1)} all-reduce(f32[4,128]{1,0:T(4,128)S(1)} %get-tuple-element.44), channel_id=1, replica_groups=mesh['dp_outer'=4,'dp_inner'=4,'latent'=8,'section'=4] {'dp_outer'}, use_global_device_ids=true, to_apply=%region_2.0 | all-reduce | flops 512 | bytes 4096 | tf_op jit(solution)/shard_map/psum | solution.py:421
  150.8 8.4 %psum.29 = f32[4,128]{1,0:T(4,128)S(1)} all-reduce(f32[4,128]{1,0:T(4,128)S(1)} %psum.28), channel_id=1, replica_groups=mesh['dp_outer'=4,'dp_inner'=4,'latent'=8,'section'=4] {'dp_inner'}, use_global_device_ids=true, to_apply=%region_3.0 | all-reduce | flops 512 | bytes 4096 | tf_op jit(solution)/shard_map/psum | solution.py:421
  159.2 1.7 %all-to-all-done.8 = bf16[32,192,128]{2,1,0:T(8,128)(2,1)S(1)} async-done(((bf16[32,192,128]{2,1,0:T(8,128)(2,1)}), bf16[32,192,128]{2,1,0:T(8,128)(2,1)S(1)}, u32[]{:S(2)}, u32[]{:S(2)}) %all-to-all-start.8) | async-done | bytes 1572896 | tf_op jit(solution)/shard_map/all_to_all | solution.py:406
  160.9 0.0 copy-done.3
  160.9 3.5 %conditional.1 = (f32[512]{0:T(512)}, bf16[2048,288]{0,1:T(8,128)(2,1)}) conditional(s32[]{:T(128)} %bitcast.18, (bf16[32,192,128]{2,1,0:T(8,128)(2,1)S(1)}, bf16[16,80,128]{2,1,0:T(8,128)(2,1)S(1)}, f32[24,128]{1,0:T(8,128)S(1)}, f32[4,128]{1,0:T(4,128)S(1)}) %tuple.45, (s32[512,4]{0,1:T(4,128)S(1)}, bf16[512,288]{0,1:T(8,128)(2,1)S(1)}, ...), branch_computations={%region_4.0_spmd, %region_5.0_spmd} | conditional | flops 4205791488 | bytes 89270392 | solution.py:540
  160.9 3.3 %gradient.1 = (bf16[288,2048]{1,0:T(8,128)(2,1)}, f32[4,128]{1,0:T(4,128)}) custom-call(bf16[32,192,128]{2,1,0:T(8,128)(2,1)S(1)} %get-tuple-element.18.recv_ref, bf16[16,80,128]{2,1,0:T(8,128)(2,1)S(1)} %get-tuple-element.19.codes_ref, f32[24,128]{1,0:T(8,128)S(1)} %get-tuple-element.20.ids_ref, f32[4,128]{1,0:T(4,128)S(1)} %get-tuple-element.21.loss_ref), custom_call_target="tpu_custom_call" | custom-call | flops 3019898880 | bytes 6000000 | tf_op jit(solution)/shard_map/cond/branch_0_fun/gradient/pallas_call | solution.py:524
  (5 shorter events, 0.2 us)
Async XLA Ops:
  4.9 32.0 %all-to-all-start.3 = ((bf16[32,192,128]{2,1,0:T(8,128)(2,1)}), bf16[32,192,128]{2,1,0:T(8,128)(2,1)S(1)}, u32[]{:S(2)}, u32[]{:S(2)}) async-start(bf16[32,192,128]{2,1,0:T(8,128)(2,1)} %get-tuple-element.38), calls=%async_computation.3 | async-start | bytes 3145728 | tf_op jit(solution)/shard_map/all_to_all | solution.py:406
  39.2 53.7 %copy-start.2 = (bf16[2048,288]{0,1:T(8,128)(2,1)S(1)}, bf16[2048,288]{0,1:T(8,128)(2,1)}, u32[]{:S(2)}) copy-start(bf16[2048,288]{0,1:T(8,128)(2,1)} %param.10) | copy-start | bytes 3538948
  95.6 36.2 %copy-start.4 = (bf16[288]{0:T(512)(128)(2,1)S(1)}, bf16[288]{0:T(512)(128)(2,1)}, u32[]{:S(2)}) copy-start(bf16[288]{0:T(512)(128)(2,1)} %bias_ref.3) | copy-start | bytes 1732
  95.6 36.2 %copy-start.5 = (bf16[512,288]{0,1:T(8,128)(2,1)S(1)}, bf16[512,288]{0,1:T(8,128)(2,1)}, u32[]{:S(2)}) copy-start(bf16[512,288]{0,1:T(8,128)(2,1)} %param.7) | copy-start | bytes 884740
  131.8 29.1 %copy-start.3 = (s32[512,4]{0,1:T(4,128)S(1)}, s32[512,4]{0,1:T(4,128)}, u32[]{:S(2)}) copy-start(s32[512,4]{0,1:T(4,128)} %param.11) | copy-start | bytes 24580
  135.1 25.8 %all-to-all-start.8 = ((bf16[32,192,128]{2,1,0:T(8,128)(2,1)}), bf16[32,192,128]{2,1,0:T(8,128)(2,1)S(1)}, u32[]{:S(2)}, u32[]{:S(2)}) async-start(bf16[32,192,128]{2,1,0:T(8,128)(2,1)} %get-tuple-element.43), calls=%async_computation.8 | async-start | bytes 3145728 | tf_op jit(solution)/shard_map/all_to_all | solution.py:406

commit v11 on v9

--- a/solution.py
+++ b/solution.py
@@ -203,14 +203,16 @@
     store_extra(send_ref, values)
     lane = lax.broadcasted_iota(jnp.int32, (EXTRA_SLOTS, 128), 1)
     ids = mm(named, jnp.ones((ROWS, 128), BF16))
+    line = jnp.bitwise_and(lax.broadcasted_iota(jnp.int32, (EXTRA_SLOTS, 128), 0), EXTRA - 1)
     last = jnp.where(lane == 32, ids, values[:, 256:])
-    row = lax.broadcasted_iota(jnp.int32, (EXTRA, 128), 0)
-    high = lax.broadcasted_iota(jnp.int32, (EXTRA, 128), 1) >= MAIN
-    flag = jnp.broadcast_to(over, (EXTRA, 128))
+    last = jnp.where((lane >= MAIN) & (line == 1), jnp.broadcast_to(over, last.shape), last).astype(BF16)
+    row = lax.broadcasted_iota(jnp.int16, (EXTRA, 128), 0)
+    place_ids = row * jnp.int16(128) + lax.broadcasted_iota(jnp.int16, (EXTRA, 128), 1)
+    named_here = (place_ids >= jnp.int16(MAIN)) & (place_ids < jnp.int16(128))
     for double in range(PAIRS // 2):
         named, place = placed(slots, names, double * 256, 256)
         values = mm_nt(shifted, place)
-        ids = mm_nt(jnp.ones((EXTRA, ROWS), BF16), named)
+        ids = mm_nt(jnp.ones((EXTRA, ROWS), BF16), named).astype(BF16)
         for side in range(2):
             pair = 2 * double + side
             store_pair(send_ref, pair, values[:, side * 128 : (side + 1) * 128])
@@ -219,9 +221,7 @@
                 mine = ids[:, side * 128 : (side + 1) * 128]
                 mine = mine if half else pltpu.roll(mine, MAIN, 1)
                 tile = last[device * EXTRA : (device + 1) * EXTRA]
-                tile = jnp.where(high & (row == 0), mine, tile)
-                tile = jnp.where(high & (row == 1), flag, tile)
-                send_ref[device, HALF + 2 * EXTRA :, :] = tile.astype(BF16)
+                send_ref[device, HALF + 2 * EXTRA :, :] = jnp.where(named_here, mine, tile)
         start_stage(send_ref, out_ref, sems, 2 * double + 2)
     wait_stages(send_ref, out_ref, sems)
 

time: 165 us -> 164 us (level)
  no operation moved by 1% of the time
where the time goes in v11:
time: 164 us; the launch traced here: 161 us
  blocking collectives  106 us (65%)
  waiting for transfers between devices  17.3 us (11%)
  Pallas kernels  16.6 us (10%)
  starting transfers between devices  14.9 us (9%)
  local copies, waits for them, and re-layouts  4.3 us (3%)
    all_to_all x1, blocking collectives, route(): lax.all_to_all(buffer, PLANE, split_axis=0, concat_axis=0, tiled=True)  35.1 us
    psum x1, blocking collectives, sum_codes(): total = lax.psum(jnp.sum(received.astype(F32), axis=0), OUTER)  28.1 us
    psum x2, blocking collectives, sum_loss(): return lax.psum(lax.psum(part, OUTER), INNER)  20.6 us
    all_to_all x2, waiting for transfers between devices, route(): lax.all_to_all(buffer, PLANE, split_axis=0, concat_axis=0, tiled=True)  17.3 us
    all_to_all x2, starting transfers between devices, route(): lax.all_to_all(buffer, PLANE, split_axis=0, concat_axis=0, tiled=True)  14.9 us
    all_to_all x1, blocking collectives, sum_codes(): lax.all_to_all(shares, INNER, split_axis=0, concat_axis=0, tiled=True)  12.3 us
    all_to_all x1, blocking collectives, sum_codes(): lax.all_to_all(copies, INNER, split_axis=0, concat_axis=0, tiled=True)  9.99 us
    pallas_call x1, Pallas kernels, on_device(): call(prepare_kernel, (packed, shape((8, ROWS), jnp.int32)), sending, 2 *...  4.22 us
  transfers between devices with their start and end apart: 2, of which 2 were waited for; matrix products, arithmetic and copies ran while one was open for 3% of the time, Pallas kernels for 0%

profile of v11, /device:TPU:1, one launch (start us, length us, event | category | flops | bytes accessed | tf_op | source)
XLA Modules:
  0.0 161.3 jit_solution(5815291816560388948)
XLA Ops:
  0.6 4.2 %prepare.1 = (bf16[32,192,128]{2,1,0:T(8,128)(2,1)}, s32[8,512]{1,0:T(8,128)S(1)}) custom-call(bf16[288,512]{1,0:T(8,128)(2,1)} %bitcast.47, bf16[288]{0:T(512)(128)(2,1)} %bias_ref.3, s32[4,512]{1,0:T(4,128)} %bitcast.46), custom_call_target="tpu_custom_call" | custom-call | flops 754974720 | bytes 6000000 | tf_op jit(solution)/shard_map/prepare/pallas_call | solution.py:472
  4.9 10.5 %all-to-all-start.3 = ((bf16[32,192,128]{2,1,0:T(8,128)(2,1)}), bf16[32,192,128]{2,1,0:T(8,128)(2,1)S(1)}, u32[]{:S(2)}, u32[]{:S(2)}) async-start(bf16[32,192,128]{2,1,0:T(8,128)(2,1)} %get-tuple-element.38), calls=%async_computation.3 | async-start | bytes 3145728 | tf_op jit(solution)/shard_map/all_to_all | solution.py:406
  15.4 1.8 %copy.64 = bf16[288,2048]{0,1:T(8,128)(2,1)S(1)} copy(bf16[288,2048]{1,0:T(8,128)(2,1)} %param.9) | data formatting | bytes 2359296 | tf_op args[2]
  17.2 0.8 slice.20
  18.0 1.3 copy.65
  19.3 0.2 reshape.54
  19.6 0.1 copy.66.rest_ref
  19.7 17.2 %all-to-all-done.3.recv_ref = bf16[32,192,128]{2,1,0:T(8,128)(2,1)S(1)} async-done(((bf16[32,192,128]{2,1,0:T(8,128)(2,1)}), bf16[32,192,128]{2,1,0:T(8,128)(2,1)S(1)}, u32[]{:S(2)}, u32[]{:S(2)}) %all-to-all-start.3) | async-done | bytes 1572896 | tf_op jit(solution)/shard_map/all_to_all | solution.py:406
  36.8 2.4 %encode.1 = (bf16[16,80,128]{2,1,0:T(8,128)(2,1)S(1)}, f32[24,128]{1,0:T(8,128)S(1)}, s32[1,1]{1,0:T(1,128)}) custom-call(bf16[32,192,128]{2,1,0:T(8,128)(2,1)S(1)} %all-to-all-done.3.recv_ref, bf16[2048,288]{1,0:T(8,128)(2,1)S(1)} %bitcast.36, bf16[256,256]{1,0:T(8,128)(2,1)S(1)} %copy.66.rest_ref), custom_call_target="tpu_custom_call" | custom-call | flops 3019898880 | bytes 6000000 | tf_op jit(solution)/shard_map/encode/pallas_call | solution.py:484
  39.2 12.3 %all_to_all.38 = bf16[4,320,128]{2,1,0:T(8,128)(2,1)S(1)} all-to-all(bf16[4,320,128]{2,1,0:T(8,128)(2,1)S(1)} %bitcast.37), channel_id=1, replica_groups=mesh['dp_outer'=4,'dp_inner'=4,'latent'=8,'section'=4] {'dp_inner'}, dimensions={0} | all-to-all | bytes 655360 | tf_op jit(solution)/shard_map/all_to_all | solution.py:411
  51.5 28.1 %all-reduce.3 = bf16[320,128]{1,0:T(8,128)(2,1)S(1)} all-reduce(f32[320,128]{1,0:T(8,128)S(1)} %convert_reduce_fusion.1), channel_id=1, replica_groups=mesh['dp_outer'=4,'dp_inner'=4,'latent'=8,'section'=4] {'dp_outer'}, use_global_device_ids=true, to_apply=%region_1.0 | all-reduce | flops 40960 | bytes 245760 | tf_op jit(solution)/shard_map/psum | solution.py:412
  79.7 10.0 %all_to_all.39 = bf16[4,320,128]{2,1,0:T(8,128)(2,1)S(1)} all-to-all(bf16[4,320,128]{2,1,0:T(8,128)(2,1)S(1)} %broadcast_in_dim.2), channel_id=1, replica_groups=mesh['dp_outer'=4,'dp_inner'=4,'latent'=8,'section'=4] {'dp_inner'}, dimensions={0} | all-to-all | bytes 655360 | tf_op jit(solution)/shard_map/all_to_all | solution.py:415
  89.7 3.5 %decode.1 = bf16[32,192,128]{2,1,0:T(8,128)(2,1)S(1)} custom-call(bf16[16,80,128]{2,1,0:T(8,128)(2,1)S(1)} %bitcast.44, f32[24,128]{1,0:T(8,128)S(1)} %get-tuple-element.41.ids_ref, bf16[288,2048]{1,0:T(8,128)(2,1)} %bitcast.42), custom_call_target="tpu_custom_call" | custom-call | flops 3019898880 | bytes 6000000 | tf_op jit(solution)/shard_map/decode/pallas_call | solution.py:494
  93.2 0.0 copy-start.3
  93.2 0.0 copy-start.4
  93.2 35.1 %all_to_all.40.recv_ref = bf16[32,192,128]{2,1,0:T(8,128)(2,1)S(1)} all-to-all(bf16[32,192,128]{2,1,0:T(8,128)(2,1)S(1)} %decode.1), channel_id=1, replica_groups=mesh['dp_outer'=4,'dp_inner'=4,'latent'=8,'section'=4] {'latent','section'}, dimensions={0} | all-to-all | bytes 3145728 | tf_op jit(solution)/shard_map/all_to_all | solution.py:406
  128.4 0.0 copy-done.3
  128.4 0.0 copy-done.4
  128.4 0.0 copy-start.2
  128.4 3.3 %combine.1 = (bf16[32,192,128]{2,1,0:T(8,128)(2,1)}, f32[4,128]{1,0:T(4,128)S(1)}) custom-call(bf16[32,192,128]{2,1,0:T(8,128)(2,1)S(1)} %all_to_all.40.recv_ref, s32[8,512]{1,0:T(8,128)S(1)} %get-tuple-element.42.slots_ref, bf16[288,512]{1,0:T(8,128)(2,1)S(1)} %bitcast.48, bf16[288]{0:T(512)(128)(2,1)S(1)} %copy-done.3), custom_call_target="tpu_custom_call" | custom-call | flops 1509949440 | bytes 6000000 | tf_op jit(solution)/shard_map/combine/pallas_call | solution.py:509
  131.7 4.4 %all-to-all-start.7 = ((bf16[32,192,128]{2,1,0:T(8,128)(2,1)}), bf16[32,192,128]{2,1,0:T(8,128)(2,1)S(1)}, u32[]{:S(2)}, u32[]{:S(2)}) async-start(bf16[32,192,128]{2,1,0:T(8,128)(2,1)} %get-tuple-element.43), calls=%async_computation.7 | async-start | bytes 3145728 | tf_op jit(solution)/shard_map/all_to_all | solution.py:406
  136.7 12.3 %psum.36 = f32[4,128]{1,0:T(4,128)S(1)} all-reduce(f32[4,128]{1,0:T(4,128)S(1)} %get-tuple-element.44), channel_id=1, replica_groups=mesh['dp_outer'=4,'dp_inner'=4,'latent'=8,'section'=4] {'dp_outer'}, use_global_device_ids=true, to_apply=%region_2.0 | all-reduce | flops 512 | bytes 4096 | tf_op jit(solution)/shard_map/psum | solution.py:419
  148.9 8.4 %psum.37 = f32[4,128]{1,0:T(4,128)S(1)} all-reduce(f32[4,128]{1,0:T(4,128)S(1)} %psum.36), channel_id=1, replica_groups=mesh['dp_outer'=4,'dp_inner'=4,'latent'=8,'section'=4] {'dp_inner'}, use_global_device_ids=true, to_apply=%region_3.0 | all-reduce | flops 512 | bytes 4096 | tf_op jit(solution)/shard_map/psum | solution.py:419
  157.3 0.1 all-to-all-done.7
  157.4 0.0 copy-done.2
  157.4 3.7 %conditional.1 = (f32[512]{0:T(512)}, bf16[2048,288]{0,1:T(8,128)(2,1)}) conditional(s32[]{:T(128)} %bitcast.18, (bf16[32,192,128]{2,1,0:T(8,128)(2,1)S(1)}, bf16[16,80,128]{2,1,0:T(8,128)(2,1)S(1)}, f32[24,128]{1,0:T(8,128)S(1)}, f32[4,128]{1,0:T(4,128)S(1)}) %tuple.45, (s32[512,4]{0,1:T(4,128)S(1)}, bf16[512,288]{0,1:T(8,128)(2,1)S(1)}, ...), branch_computations={%region_4.0_spmd, %region_5.0_spmd} | conditional | flops 4205791488 | bytes 89270392 | solution.py:538
  157.6 3.3 %gradient.1 = (bf16[288,2048]{1,0:T(8,128)(2,1)}, f32[4,128]{1,0:T(4,128)}) custom-call(bf16[32,192,128]{2,1,0:T(8,128)(2,1)S(1)} %get-tuple-element.18.recv_ref, bf16[16,80,128]{2,1,0:T(8,128)(2,1)S(1)} %get-tuple-element.19.codes_ref, f32[24,128]{1,0:T(8,128)S(1)} %get-tuple-element.20.ids_ref, f32[4,128]{1,0:T(4,128)S(1)} %get-tuple-element.21.loss_ref), custom_call_target="tpu_custom_call" | custom-call | flops 3019898880 | bytes 6000000 | tf_op jit(solution)/shard_map/cond/branch_0_fun/gradient/pallas_call | solution.py:522
  (3 shorter events, 0.1 us)
Async XLA Ops:
  4.9 32.0 %all-to-all-start.3 = ((bf16[32,192,128]{2,1,0:T(8,128)(2,1)}), bf16[32,192,128]{2,1,0:T(8,128)(2,1)S(1)}, u32[]{:S(2)}, u32[]{:S(2)}) async-start(bf16[32,192,128]{2,1,0:T(8,128)(2,1)} %get-tuple-element.38), calls=%async_computation.3 | async-start | bytes 3145728 | tf_op jit(solution)/shard_map/all_to_all | solution.py:406
  93.2 35.2 %copy-start.3 = (bf16[288]{0:T(512)(128)(2,1)S(1)}, bf16[288]{0:T(512)(128)(2,1)}, u32[]{:S(2)}) copy-start(bf16[288]{0:T(512)(128)(2,1)} %bias_ref.3) | copy-start | bytes 1732
  93.2 35.2 %copy-start.4 = (bf16[512,288]{0,1:T(8,128)(2,1)S(1)}, bf16[512,288]{0,1:T(8,128)(2,1)}, u32[]{:S(2)}) copy-start(bf16[512,288]{0,1:T(8,128)(2,1)} %param.7) | copy-start | bytes 884740
  128.4 29.1 %copy-start.2 = (s32[512,4]{0,1:T(4,128)S(1)}, s32[512,4]{0,1:T(4,128)}, u32[]{:S(2)}) copy-start(s32[512,4]{0,1:T(4,128)} %param.11) | copy-start | bytes 24580
  131.7 25.8 %all-to-all-start.7 = ((bf16[32,192,128]{2,1,0:T(8,128)(2,1)}), bf16[32,192,128]{2,1,0:T(8,128)(2,1)S(1)}, u32[]{:S(2)}, u32[]{:S(2)}) async-start(bf16[32,192,128]{2,1,0:T(8,128)(2,1)} %get-tuple-element.43), calls=%async_computation.7 | async-start | bytes 3145728 | tf_op jit(solution)/shard_map/all_to_all | solution.py:406
